TPU v7x, 32 devices: a whole 2x2x4 slice. The times are simulated.
32 devices in a mesh: expert: 8 (over z, y), shard: 4 (over x, core).
Axes of the slice: x: 2, y: 2, z: 4, core: 2. Of those that a mesh axis runs over, the one named last changes fastest.
Arguments:
- tokens: bfloat16 [4096, 2048], P(('expert', 'shard')), may hold values from -6 to 6
- cotangent: bfloat16 [4096, 2048], P(('expert', 'shard')), may hold values from -6 to 6
- norm1_gain: bfloat16 [2048], P(('expert', 'shard')), may hold values from 0.5 to 1.5
- q_weight: bfloat16 [2048, 3072], P(('expert', 'shard')), may hold values from -0.125 to 0.125
- kva_weight: bfloat16 [2048, 576], P(('expert', 'shard')), may hold values from -0.125 to 0.125
- kv_gain: bfloat16 [512], P(('expert', 'shard')), may hold values from 0.5 to 1.5
- kvb_weight: bfloat16 [512, 4096], P(('expert', 'shard')), may hold values from -0.25 to 0.25
- o_weight: bfloat16 [2048, 2048], P(('expert', 'shard')), may hold values from -0.75 to 0.75
- norm2_gain: bfloat16 [2048], P(('expert', 'shard')), may hold values from 0.5 to 1.5
- router_weight: bfloat16 [2048, 16], P(('expert', 'shard')), may hold values from -0.0625 to 0.0625
- shared_gate: bfloat16 [2048, 2816], P(('expert', 'shard')), may hold values from -0.125 to 0.125
- shared_up: bfloat16 [2048, 2816], P(('expert', 'shard')), may hold values from -0.125 to 0.125
- shared_down: bfloat16 [2816, 2048], P(('expert', 'shard')), may hold values from -0.15625 to 0.15625
- expert_gate: bfloat16 [16, 2048, 1408], P('expert', None, 'shard'), may hold values from -0.125 to 0.125
- expert_up: bfloat16 [16, 2048, 1408], P('expert', None, 'shard'), may hold values from -0.125 to 0.125
- expert_down: bfloat16 [16, 1408, 2048], P('expert', 'shard'), may hold values from -0.4375 to 0.4375
- expert_ids: int32 [4096, 6], P(('expert', 'shard')), may hold values from 0 to 15, all different within a row
- token_rank: int32 [4096], P(('expert', 'shard')), may hold values from 0 to 127, as said below
- seq_ids: int32 [4096], P('expert'), may hold values from 0 to 2, as said below
Outputs:
- output: bfloat16 [4096, 2048], P(('expert', 'shard'))
- tokens_grad: float32 [4096, 2048], P(('expert', 'shard'))
- norm1_gain_grad: float32 [2048], P(('expert', 'shard'))
- q_weight_grad: float32 [2048, 3072], P(('expert', 'shard'))
- kva_weight_grad: float32 [2048, 576], P(('expert', 'shard'))
- kv_gain_grad: float32 [512], P(('expert', 'shard'))
- kvb_weight_grad: float32 [512, 4096], P(('expert', 'shard'))
- o_weight_grad: float32 [2048, 2048], P(('expert', 'shard'))
- norm2_gain_grad: float32 [2048], P(('expert', 'shard'))
- router_weight_grad: float32 [2048, 16], P(('expert', 'shard'))
- shared_gate_grad: float32 [2048, 2816], P(('expert', 'shard'))
- shared_up_grad: float32 [2048, 2816], P(('expert', 'shard'))
- shared_down_grad: float32 [2816, 2048], P(('expert', 'shard'))
- expert_gate_grad: float32 [16, 2048, 1408], P('expert', None, 'shard')
- expert_up_grad: float32 [16, 2048, 1408], P('expert', None, 'shard')
- expert_down_grad: float32 [16, 1408, 2048], P('expert', 'shard')
Inputs may be any that keep to these rules, and one draw needn't show every extreme that they name: `token_rank`: within each aligned block of 128 tokens (the rows of one device) every value of 0 to 127 appears once. `seq_ids`: in each group of 512 tokens the ids never fall; the first 256 are 0 and the others belong to continuations 1 to 2, each of one token or more.
All inputs are finite; a program needn't handle non-finite values.
Results may differ from a plain program's by a relative error of at most 0.02.
Values may be sent and summed in bfloat16 or wider, within the bound.
A program may use at most 448 MiB of HBM per device.

v0:
```python
import jax
import jax.numpy as jnp
from jax import lax
from jax.sharding import PartitionSpec as P

HEADS = 16
NOPE = 128
ROPE = 64
VDIM = 128
KV_RANK = 512
CONTS = 2


EPSILON = 1e-06
THETA = 10000.0
NEGATIVE = -1e30


def rms_forward(values, gain_row):
    inverse = lax.rsqrt(jnp.mean(values * values, axis=-1, keepdims=True) + EPSILON)
    return (values * inverse * gain_row, inverse)


def rms_backward(values, inverse, gain_row, upstream):
    normed = values * inverse
    scaled = upstream * gain_row
    value_grad = inverse * (scaled - normed * jnp.mean(scaled * normed, axis=-1, keepdims=True))
    return (value_grad, jnp.sum(upstream * normed, axis=0))


def rope_tables(positions, width):
    half_width = width // 2
    frequency = THETA ** (-2.0 * jnp.arange(half_width, dtype=jnp.float32) / width)
    angles = positions.astype(jnp.float32)[:, None] * frequency[None, :]
    return (jnp.cos(angles), jnp.sin(angles))


def rotate(values, cosine_table, sine_table):
    half_width = values.shape[-1] // 2
    first_half = values[..., :half_width]
    second = values[..., half_width:]
    return jnp.concatenate(
        [
            first_half * cosine_table - second * sine_table,
            second * cosine_table + first_half * sine_table,
        ],
        axis=-1,
    )


def positions_of(group_ids):
    length = group_ids.shape[0]
    token_index = jnp.arange(length, dtype=jnp.int32)
    labels = jnp.arange(CONTS + 1, dtype=jnp.int32)
    member = (group_ids[:, None] == labels[None, :]).astype(jnp.int32)
    counts = jnp.sum(member, axis=0)
    starts = jnp.cumsum(counts) - counts
    start_of = jnp.sum(member * starts[None, :], axis=1)
    return token_index - start_of + jnp.where(group_ids > 0, counts[0], 0)


def route_slots(choice_ids, rank_row, expert_total, capacity):
    row_count, top_count = choice_ids.shape
    pair_count = row_count * top_count
    order_key = (
        jnp.arange(top_count, dtype=jnp.int32)[None, :] * row_count + rank_row[:, None]
    ).reshape(pair_count)
    flat_ids = choice_ids.reshape(pair_count)
    pair_range = jnp.arange(pair_count, dtype=jnp.int32)
    in_order = jnp.zeros((pair_count,), jnp.int32).at[order_key].set(pair_range)
    sorted_ids = flat_ids[in_order]
    member = (sorted_ids[:, None] == jnp.arange(expert_total, dtype=jnp.int32)[None, :]).astype(
        jnp.int32
    )
    earlier = jnp.cumsum(member, axis=0) - member
    place_sorted = jnp.sum(earlier * member, axis=1)
    pair_place = place_sorted[order_key]
    pair_dest = jnp.where(
        pair_place < capacity, flat_ids * capacity + pair_place, expert_total * capacity
    )
    slot_pair = (
        jnp.full((expert_total * capacity + 1,), pair_count, jnp.int32)
        .at[pair_dest]
        .set(pair_range)
    )
    return (pair_dest.reshape(row_count, top_count), slot_pair[: expert_total * capacity])


def silu_parts(values):
    sigmoid_val = jax.nn.sigmoid(values)
    return (values * sigmoid_val, sigmoid_val * (1.0 + values * (1.0 - sigmoid_val)))


def on_device(
    tokens,
    cotangent,
    norm1_gain,
    q_weight,
    kva_weight,
    kv_gain,
    kvb_weight,
    o_weight,
    norm2_gain,
    router_weight,
    shared_gate,
    shared_up,
    shared_down,
    expert_gate,
    expert_up,
    expert_down,
    expert_ids,
    token_rank,
    seq_ids,
):
    expert_count = lax.axis_size("expert")
    tok_rows = tokens.shape[0]
    group_len = seq_ids.shape[0]
    width = tokens.shape[1]
    local_experts = expert_gate.shape[0]
    all_experts = local_experts * expert_count
    top_count = expert_ids.shape[1]
    capacity = max(2, tok_rows * top_count // all_experts)
    pair_total = tok_rows * top_count
    score_scale = (NOPE + ROPE) ** (-0.5)

    def to_owners(buffer):
        arrived = lax.all_to_all(buffer, "expert", split_axis=0, concat_axis=0, tiled=True)
        return lax.all_gather(arrived[:, None], "shard", axis=1, tiled=True)

    def from_owners(partial_value):
        summed = lax.psum_scatter(
            partial_value.astype(jnp.bfloat16), "shard", scatter_dimension=1, tiled=True
        ).astype(jnp.float32)[:, 0]
        homed = lax.all_to_all(
            summed.astype(jnp.bfloat16), "expert", split_axis=0, concat_axis=0, tiled=True
        )
        return homed.astype(jnp.float32)

    own_start = lax.axis_index("shard") * tok_rows
    all_positions = positions_of(seq_ids)
    own_positions = lax.dynamic_slice_in_dim(all_positions, own_start, tok_rows)
    own_ids = lax.dynamic_slice_in_dim(seq_ids, own_start, tok_rows)
    cosine_table, sine_table = rope_tables(own_positions, ROPE)
    query_index = own_start + jnp.arange(tok_rows, dtype=jnp.int32)
    key_index = jnp.arange(group_len, dtype=jnp.int32)
    allowed = (key_index[None, :] <= query_index[:, None]) & (
        (seq_ids[None, :] == 0) | (seq_ids[None, :] == own_ids[:, None])
    )
    (
        first_norm_scale,
        query_weight,
        compress_weight,
        latent_norm_scale,
        expand_weight,
        output_weight,
    ) = (
        lax.all_gather(norm1_gain, ("expert", "shard"), axis=0, tiled=True),
        lax.all_gather(q_weight, ("expert", "shard"), axis=0, tiled=True),
        lax.all_gather(kva_weight, ("expert", "shard"), axis=0, tiled=True),
        lax.all_gather(kv_gain, ("expert", "shard"), axis=0, tiled=True),
        lax.all_gather(kvb_weight, ("expert", "shard"), axis=0, tiled=True),
        lax.all_gather(o_weight, ("expert", "shard"), axis=0, tiled=True),
    )
    first_norm_scale = first_norm_scale.astype(jnp.float32)
    latent_norm_scale = latent_norm_scale.astype(jnp.float32)
    input_rows = tokens.astype(jnp.float32)
    normed_one, inverse_one = rms_forward(input_rows, first_norm_scale)
    hidden_one = normed_one.astype(jnp.bfloat16)
    query_raw = jnp.dot(hidden_one, query_weight, preferred_element_type=jnp.float32).reshape(
        tok_rows, HEADS, NOPE + ROPE
    )
    q_nope = query_raw[:, :, :NOPE].astype(jnp.bfloat16)
    q_rope = rotate(
        query_raw[:, :, NOPE:], cosine_table[:, None, :], sine_table[:, None, :]
    ).astype(jnp.bfloat16)
    compressed = jnp.dot(hidden_one, compress_weight, preferred_element_type=jnp.float32)
    latent_raw = compressed[:, :KV_RANK]
    latent_norm, inverse_latent = rms_forward(latent_raw, latent_norm_scale)
    latent = latent_norm.astype(jnp.bfloat16)
    k_rope = rotate(compressed[:, KV_RANK:], cosine_table, sine_table).astype(jnp.bfloat16)
    keyval = (
        jnp.dot(latent, expand_weight, preferred_element_type=jnp.float32)
        .astype(jnp.bfloat16)
        .reshape(tok_rows, HEADS, NOPE + VDIM)
    )
    k_nope = keyval[:, :, :NOPE].reshape(tok_rows, HEADS * NOPE)
    k_values = keyval[:, :, NOPE:].reshape(tok_rows, HEADS * VDIM)
    keys_all, rope_all, values_all = (
        lax.all_gather(k_nope, "shard", axis=0, tiled=True),
        lax.all_gather(k_rope, "shard", axis=0, tiled=True),
        lax.all_gather(k_values, "shard", axis=0, tiled=True),
    )
    keys_all = keys_all.reshape(group_len, HEADS, NOPE)
    values_all = values_all.reshape(group_len, HEADS, VDIM)

    def score_block():
        raw_scores = jnp.einsum(
            "qhd,khd->hqk", q_nope, keys_all, preferred_element_type=jnp.float32
        )
        raw_scores = raw_scores + jnp.einsum(
            "qhd,kd->hqk", q_rope, rope_all, preferred_element_type=jnp.float32
        )
        return jnp.where(allowed[None], raw_scores * score_scale, NEGATIVE)

    scores = score_block()
    top_score = jnp.max(scores, axis=-1, keepdims=True)
    log_total = top_score + jnp.log(jnp.sum(jnp.exp(scores - top_score), axis=-1, keepdims=True))
    prob_low = jnp.exp(scores - log_total).astype(jnp.bfloat16)
    attended = (
        jnp.einsum("hqk,khd->qhd", prob_low, values_all, preferred_element_type=jnp.float32)
        .astype(jnp.bfloat16)
        .reshape(tok_rows, HEADS * VDIM)
    )
    mixed = input_rows + jnp.dot(attended, output_weight, preferred_element_type=jnp.float32)
    second_norm_scale, router_matrix, shared_gate_weight, shared_up_weight, shared_down_weight = (
        lax.all_gather(norm2_gain, ("expert", "shard"), axis=0, tiled=True),
        lax.all_gather(router_weight, ("expert", "shard"), axis=0, tiled=True),
        lax.all_gather(shared_gate, ("expert", "shard"), axis=0, tiled=True),
        lax.all_gather(shared_up, ("expert", "shard"), axis=0, tiled=True),
        lax.all_gather(shared_down, ("expert", "shard"), axis=0, tiled=True),
    )
    second_norm_scale = second_norm_scale.astype(jnp.float32)
    normed_two, inverse_two = rms_forward(mixed, second_norm_scale)
    hidden_two = normed_two.astype(jnp.bfloat16)
    logits = jnp.dot(hidden_two, router_matrix, preferred_element_type=jnp.float32)
    choice_hot = (
        expert_ids[:, :, None] == jnp.arange(all_experts, dtype=jnp.int32)[None, None, :]
    ).astype(jnp.float32)
    chosen = jnp.sum(choice_hot * logits[:, None, :], axis=-1)
    gate_probs = jax.nn.softmax(chosen, axis=-1)
    shared_gate_val = jnp.dot(hidden_two, shared_gate_weight, preferred_element_type=jnp.float32)
    shared_up_val = jnp.dot(hidden_two, shared_up_weight, preferred_element_type=jnp.float32)
    shared_act, shared_slope = silu_parts(shared_gate_val)
    shared_hidden = (shared_act * shared_up_val).astype(jnp.bfloat16)
    shared_out = jnp.dot(shared_hidden, shared_down_weight, preferred_element_type=jnp.float32)
    pair_dest, slot_pair = route_slots(expert_ids, token_rank, all_experts, capacity)
    dest_flat = pair_dest.reshape(pair_total)
    slot_token = slot_pair // top_count
    padded_rows = jnp.concatenate([hidden_two, jnp.zeros((1, width), jnp.bfloat16)], axis=0)
    send_rows = jnp.take(padded_rows, slot_token, axis=0).reshape(
        expert_count, local_experts, capacity, width
    )
    received_rows = to_owners(send_rows)
    gate_val = jnp.einsum(
        "abecd,edf->abecf", received_rows, expert_gate, preferred_element_type=jnp.float32
    )
    up_val = jnp.einsum(
        "abecd,edf->abecf", received_rows, expert_up, preferred_element_type=jnp.float32
    )
    expert_act, expert_slope = silu_parts(gate_val)
    expert_hidden = (expert_act * up_val).astype(jnp.bfloat16)
    partial_value = jnp.einsum(
        "abecf,efd->abecd", expert_hidden, expert_down, preferred_element_type=jnp.float32
    )
    returned = (
        from_owners(partial_value).astype(jnp.bfloat16).reshape(all_experts * capacity, width)
    )
    padded_out = jnp.concatenate([returned, jnp.zeros((1, width), jnp.bfloat16)], axis=0)
    pair_out = (
        jnp.take(padded_out, dest_flat, axis=0)
        .reshape(tok_rows, top_count, width)
        .astype(jnp.float32)
    )
    routed = jnp.sum(gate_probs[:, :, None] * pair_out, axis=1)
    output = (mixed + routed + shared_out).astype(jnp.bfloat16)
    upstream = cotangent.astype(jnp.float32)
    shared_dh = jnp.dot(cotangent, shared_down_weight.T, preferred_element_type=jnp.float32)
    sdown_grad = jnp.dot(shared_hidden.T, cotangent, preferred_element_type=jnp.float32)
    sgate_d = (shared_dh * shared_up_val * shared_slope).astype(jnp.bfloat16)
    sup_d = (shared_dh * shared_act).astype(jnp.bfloat16)
    sgate_grad = jnp.dot(hidden_two.T, sgate_d, preferred_element_type=jnp.float32)
    sup_grad = jnp.dot(hidden_two.T, sup_d, preferred_element_type=jnp.float32)
    hidden_two_grad = jnp.dot(
        sgate_d, shared_gate_weight.T, preferred_element_type=jnp.float32
    ) + jnp.dot(sup_d, shared_up_weight.T, preferred_element_type=jnp.float32)
    gates_flat = jnp.concatenate([gate_probs.reshape(pair_total), jnp.zeros((1,), jnp.float32)])
    padded_up = jnp.concatenate([upstream, jnp.zeros((1, width), jnp.float32)], axis=0)
    slot_grad = (
        jnp.take(gates_flat, slot_pair)[:, None] * jnp.take(padded_up, slot_token, axis=0)
    ).astype(jnp.bfloat16)
    received_grad = to_owners(slot_grad.reshape(expert_count, local_experts, capacity, width))
    hidden_grad = jnp.einsum(
        "abecd,efd->abecf", received_grad, expert_down, preferred_element_type=jnp.float32
    )
    edown_grad = jnp.einsum(
        "abecf,abecd->efd", expert_hidden, received_grad, preferred_element_type=jnp.float32
    )
    gate_d = (hidden_grad * up_val * expert_slope).astype(jnp.bfloat16)
    up_projection_gradient = (hidden_grad * expert_act).astype(jnp.bfloat16)
    egate_grad = jnp.einsum(
        "uznpr,uznpw->nrw", received_rows, gate_d, preferred_element_type=jnp.float32
    )
    expert_up_weight_gradient = jnp.einsum(
        "uznpr,uznpw->nrw",
        received_rows,
        up_projection_gradient,
        preferred_element_type=jnp.float32,
    )
    rows_grad = jnp.einsum(
        "abecf,edf->abecd", gate_d, expert_gate, preferred_element_type=jnp.float32
    )
    rows_grad = rows_grad + jnp.einsum(
        "abecf,edf->abecd", up_projection_gradient, expert_up, preferred_element_type=jnp.float32
    )
    back_rows = from_owners(rows_grad).astype(jnp.bfloat16).reshape(all_experts * capacity, width)
    padded_back = jnp.concatenate([back_rows, jnp.zeros((1, width), jnp.bfloat16)], axis=0)
    pair_back = (
        jnp.take(padded_back, dest_flat, axis=0)
        .reshape(tok_rows, top_count, width)
        .astype(jnp.float32)
    )
    hidden_two_grad = hidden_two_grad + jnp.sum(pair_back, axis=1)
    gate_grad = jnp.sum(pair_out * upstream[:, None, :], axis=-1)
    chosen_grad = gate_probs * (gate_grad - jnp.sum(gate_probs * gate_grad, axis=-1, keepdims=True))
    logit_grad = jnp.sum(choice_hot * chosen_grad[:, :, None], axis=1).astype(jnp.bfloat16)
    router_grad = jnp.dot(hidden_two.T, logit_grad, preferred_element_type=jnp.float32)
    hidden_two_grad = hidden_two_grad + jnp.dot(
        logit_grad, router_matrix.T, preferred_element_type=jnp.float32
    )
    mixed_norm_grad, gain_two_grad = rms_backward(
        mixed, inverse_two, second_norm_scale, hidden_two_grad
    )
    mixed_grad = upstream + mixed_norm_grad
    mixed_grad_low = mixed_grad.astype(jnp.bfloat16)
    output_w_grad = jnp.dot(attended.T, mixed_grad_low, preferred_element_type=jnp.float32)
    attended_grad = (
        jnp.dot(mixed_grad_low, output_weight.T, preferred_element_type=jnp.float32)
        .astype(jnp.bfloat16)
        .reshape(tok_rows, HEADS, VDIM)
    )
    soft_probs = jnp.exp(score_block() - log_total)
    prob_grad = jnp.einsum(
        "qhd,khd->hqk", attended_grad, values_all, preferred_element_type=jnp.float32
    )
    values_grad = jnp.einsum(
        "hqk,qhd->khd", prob_low, attended_grad, preferred_element_type=jnp.float32
    )
    score_grad = (
        soft_probs * (prob_grad - jnp.sum(soft_probs * prob_grad, axis=-1, keepdims=True))
    ).astype(jnp.bfloat16)
    q_nope_grad = (
        jnp.einsum("hqk,khd->qhd", score_grad, keys_all, preferred_element_type=jnp.float32)
        * score_scale
    )
    q_rope_grad = (
        jnp.einsum("hqk,kd->qhd", score_grad, rope_all, preferred_element_type=jnp.float32)
        * score_scale
    )
    keys_grad = (
        jnp.einsum("hqk,qhd->khd", score_grad, q_nope, preferred_element_type=jnp.float32)
        * score_scale
    )
    rope_grad = (
        jnp.einsum("hqk,qhd->kd", score_grad, q_rope, preferred_element_type=jnp.float32)
        * score_scale
    )
    own_keys, own_rope, own_values = (
        lax.psum_scatter(
            keys_grad.reshape(group_len, HEADS * NOPE).astype(jnp.bfloat16),
            "shard",
            scatter_dimension=0,
            tiled=True,
        ).astype(jnp.float32),
        lax.psum_scatter(
            rope_grad.astype(jnp.bfloat16), "shard", scatter_dimension=0, tiled=True
        ).astype(jnp.float32),
        lax.psum_scatter(
            values_grad.reshape(group_len, HEADS * VDIM).astype(jnp.bfloat16),
            "shard",
            scatter_dimension=0,
            tiled=True,
        ).astype(jnp.float32),
    )
    keyval_grad = jnp.concatenate(
        [own_keys.reshape(tok_rows, HEADS, NOPE), own_values.reshape(tok_rows, HEADS, VDIM)],
        axis=-1,
    )
    keyval_grad = keyval_grad.reshape(tok_rows, HEADS * (NOPE + VDIM)).astype(jnp.bfloat16)
    expand_grad = jnp.dot(latent.T, keyval_grad, preferred_element_type=jnp.float32)
    latent_grad = jnp.dot(keyval_grad, expand_weight.T, preferred_element_type=jnp.float32)
    latent_raw_grad, gain_latent_grad = rms_backward(
        latent_raw, inverse_latent, latent_norm_scale, latent_grad
    )
    compressed_grad = jnp.concatenate(
        [latent_raw_grad, rotate(own_rope, cosine_table, -sine_table)], axis=1
    ).astype(jnp.bfloat16)
    compress_w_grad = jnp.dot(hidden_one.T, compressed_grad, preferred_element_type=jnp.float32)
    query_grad = jnp.concatenate(
        [q_nope_grad, rotate(q_rope_grad, cosine_table[:, None, :], -sine_table[:, None, :])],
        axis=-1,
    )
    query_grad = query_grad.reshape(tok_rows, HEADS * (NOPE + ROPE)).astype(jnp.bfloat16)
    query_w_grad = jnp.dot(hidden_one.T, query_grad, preferred_element_type=jnp.float32)
    hidden_one_grad = jnp.dot(
        query_grad, query_weight.T, preferred_element_type=jnp.float32
    ) + jnp.dot(compressed_grad, compress_weight.T, preferred_element_type=jnp.float32)
    input_norm_grad, gain_one_grad = rms_backward(
        input_rows, inverse_one, first_norm_scale, hidden_one_grad
    )
    tokens_grad = mixed_grad + input_norm_grad
    attn_sums = (
        lax.psum_scatter(gain_one_grad, ("expert", "shard"), scatter_dimension=0, tiled=True),
        lax.psum_scatter(query_w_grad, ("expert", "shard"), scatter_dimension=0, tiled=True),
        lax.psum_scatter(compress_w_grad, ("expert", "shard"), scatter_dimension=0, tiled=True),
        lax.psum_scatter(gain_latent_grad, ("expert", "shard"), scatter_dimension=0, tiled=True),
        lax.psum_scatter(expand_grad, ("expert", "shard"), scatter_dimension=0, tiled=True),
        lax.psum_scatter(output_w_grad, ("expert", "shard"), scatter_dimension=0, tiled=True),
    )
    ffn_sums = (
        lax.psum_scatter(gain_two_grad, ("expert", "shard"), scatter_dimension=0, tiled=True),
        lax.psum_scatter(router_grad, ("expert", "shard"), scatter_dimension=0, tiled=True),
        lax.psum_scatter(sgate_grad, ("expert", "shard"), scatter_dimension=0, tiled=True),
        lax.psum_scatter(sup_grad, ("expert", "shard"), scatter_dimension=0, tiled=True),
        lax.psum_scatter(sdown_grad, ("expert", "shard"), scatter_dimension=0, tiled=True),
    )
    return (
        output,
        tokens_grad,
        attn_sums[0],
        attn_sums[1],
        attn_sums[2],
        attn_sums[3],
        attn_sums[4],
        attn_sums[5],
        ffn_sums[0],
        ffn_sums[1],
        ffn_sums[2],
        ffn_sums[3],
        ffn_sums[4],
        egate_grad,
        expert_up_weight_gradient,
        edown_grad,
    )


def solution(mesh):
    return jax.shard_map(
        on_device,
        mesh=mesh,
        in_specs=(
            P(("expert", "shard"), None),
            P(("expert", "shard"), None),
            P(("expert", "shard")),
            P(("expert", "shard"), None),
            P(("expert", "shard"), None),
            P(("expert", "shard")),
            P(("expert", "shard"), None),
            P(("expert", "shard"), None),
            P(("expert", "shard")),
            P(("expert", "shard"), None),
            P(("expert", "shard"), None),
            P(("expert", "shard"), None),
            P(("expert", "shard"), None),
            P("expert", None, "shard"),
            P("expert", None, "shard"),
            P("expert", "shard", None),
            P(("expert", "shard"), None),
            P(("expert", "shard")),
            P("expert"),
        ),
        out_specs=(
            P(("expert", "shard"), None),
            P(("expert", "shard"), None),
            P(("expert", "shard")),
            P(("expert", "shard"), None),
            P(("expert", "shard"), None),
            P(("expert", "shard")),
            P(("expert", "shard"), None),
            P(("expert", "shard"), None),
            P(("expert", "shard")),
            P(("expert", "shard"), None),
            P(("expert", "shard"), None),
            P(("expert", "shard"), None),
            P(("expert", "shard"), None),
            P("expert", None, "shard"),
            P("expert", None, "shard"),
            P("expert", "shard", None),
        ),
        check_vma=False,
    )
```

profile of v0, /device:TPU:0, one launch (start us, length us, event | category | flops | bytes accessed | tf_op | source)
XLA Modules:
  0.0 3325.0 jit_solution(8879572524505811661)
XLA Ops:
  12.0 42.2 %all-reduce.13 = (bf16[2048]{0:T(1024)(128)(2,1)S(1)}, bf16[512]{0:T(512)(128)(2,1)S(1)}, bf16[2048]{0:T(1024)(128)(2,1)S(1)}) all-reduce(bf16[2048]{0:T(1024)(128)(2,1)S(1)} %dynamic-update-slice, bf16[512]{0:T(512)(128)(2,1)S(1)} %dynamic-update-slice.1, ...), channel_id=1, replica_groups=mesh['expert'=8,'shard'=4] {'expert','shard'}, use_global_device_ids=true, to_apply=%add.4 | all-reduce | flops 4608 | bytes 18432
  55.5 16.0 all-gather.15.cloned.1.call-done
  74.7 60.7 %all-gather.17.cloned.1.call-done = bf16[512,4096]{1,0:T(8,128)(2,1)} async-done(((bf16[16,4096]{1,0:T(8,128)(2,1)}), bf16[512,4096]{1,0:T(8,128)(2,1)}) %all-gather.17.cloned.1.call-update) | async-done | bytes 4194320 | tf_op jit(solution)/shard_map/all_gather | solution.py:161
  171.0 6.2 all_gather.55
  177.2 56.1 %all-gather.21.cloned.1.call-done = bf16[2048,3072]{1,0:T(8,128)(2,1)} async-done(((bf16[64,3072]{1,0:T(8,128)(2,1)}), bf16[2048,3072]{1,0:T(8,128)(2,1)}) %all-gather.21.cloned.1.call-update) | async-done | bytes 12582928 | tf_op jit(solution)/shard_map/all_gather | solution.py:158
  233.3 8.1 fusion.102
  243.4 13.0 all-gather.23.cloned.1.call-done
  263.6 17.7 all-gather.19.cloned.1.call-done
  285.8 75.7 %all-gather.25.cloned.1.call-done = bf16[2048,2048]{1,0:T(8,128)(2,1)} async-done(((bf16[64,2048]{1,0:T(8,128)(2,1)}), bf16[2048,2048]{1,0:T(8,128)(2,1)}) %all-gather.25.cloned.1.call-update) | async-done | bytes 8388624 | tf_op jit(solution)/shard_map/all_gather | solution.py:162
  361.5 4.9 multiply_reduce_fusion.5
  374.1 75.2 %all_to_all.20 = bf16[8,2,48,2048]{3,2,1,0:T(8,128)(2,1)} all-to-all(bf16[8,2,48,2048]{3,2,1,0:T(8,128)(2,1)S(1)} %broadcast_select_fusion), channel_id=1, replica_groups=mesh['expert'=8,'shard'=4] {'expert'}, dimensions={0} | all-to-all | bytes 6291456 | tf_op jit(solution)/shard_map/all_to_all | solution.py:127
  449.4 40.5 %all-gather.2 = bf16[32,64,16]{1,2,0:T(8,128)(2,1)S(1)} all-gather(bf16[1,64,16]{1,2,0:T(8,128)(2,1)S(1)} %bitcast.265), channel_id=1, replica_groups=mesh['expert'=8,'shard'=4] {'expert','shard'}, dimensions={0}, use_global_device_ids=true | all-gather | bytes 67584 | tf_op jit(solution)/shard_map/all_gather | solution.py:217
  492.8 8.6 gather_fusion.4
  508.8 74.7 %all_to_all.21 = bf16[8,2,48,2048]{3,2,1,0:T(8,128)(2,1)} all-to-all(bf16[8,2,48,2048]{3,2,1,0:T(8,128)(2,1)S(1)} %multiply_convert_fusion), channel_id=1, replica_groups=mesh['expert'=8,'shard'=4] {'expert'}, dimensions={0} | all-to-all | bytes 6291456 | tf_op jit(solution)/shard_map/all_to_all | solution.py:127
  583.6 12.0 fusion.5
  598.3 8.6 fusion.7
  606.9 56.9 %all-gather.35.cloned.1.call-done = bf16[8,8,48,2048]{3,2,1,0:T(8,128)(2,1)} async-done(((bf16[8,2,48,2048]{3,2,1,0:T(8,128)(2,1)}), bf16[8,8,48,2048]{3,2,1,0:T(8,128)(2,1)}) %all-gather.35.cloned.1.call-update) | async-done | bytes 12582928 | tf_op jit(solution)/shard_map/all_gather | solution.py:128
  663.9 14.4 fusion.11
  678.3 12.0 fusion.26
  690.3 9.6 convert_bitcast_fusion
  699.9 15.8 fusion
  718.3 421.3 %all-reduce.17.cloned.1.call-done = (bf16[8,4,2,48,2048]{4,3,1,0,2:T(8,128)(2,1)}, bf16[8,4,2,48,2048]{4,3,1,0,2:T(8,128)(2,1)}) async-done(((bf16[8,4,2,48,2048]{4,3,1,0,2:T(8,128)(2,1)}, bf16[8,4,2,48,2048]{4,3,1,0,2:T(8,128)(2,1)}), (bf16[8,4,2,48,2048]{4,3,1,0,2:T(8,128)(2,1)}, bf16[8,4,2,48,2048]{4,3,1,0,2:T(8,128)(2,1)})) %all-reduce.17.cloned.1.call-update) | async-done | bytes 25165840
  1144.6 5.5 all-to-all-start.1
  1155.3 91.6 %all-to-all-done.1 = bf16[8,2,48,2048]{3,2,1,0:T(8,128)(2,1)} async-done(((bf16[8,2,48,2048]{3,2,1,0:T(8,128)(2,1)}), bf16[8,2,48,2048]{3,2,1,0:T(8,128)(2,1)}, u32[]{:S(2)}, u32[]{:S(2)}) %all-to-all-start.1) | async-done | bytes 3145760 | tf_op jit(solution)/shard_map/all_to_all | solution.py:134
  1255.8 8.7 mul.481
  1264.6 38.4 %all-gather.27.cloned.1.call-done = bf16[2048,2816]{1,0:T(8,128)(2,1)} async-done(((bf16[64,2816]{1,0:T(8,128)(2,1)}), bf16[2048,2816]{1,0:T(8,128)(2,1)}) %all-gather.27.cloned.1.call-update) | async-done | bytes 11534352 | tf_op jit(solution)/shard_map/all_gather | solution.py:218
  1303.0 7.1 fusion.109
  1310.0 106.9 %all-gather.29.cloned.1.call-done = bf16[2048,2816]{1,0:T(8,128)(2,1)} async-done(((bf16[64,2816]{1,0:T(8,128)(2,1)}), bf16[2048,2816]{1,0:T(8,128)(2,1)}) %all-gather.29.cloned.1.call-update) | async-done | bytes 11534352 | tf_op jit(solution)/shard_map/all_gather | solution.py:219
  1417.0 7.1 fusion.110
  1424.1 85.6 %all-gather.31.cloned.1.call-done = bf16[2816,2048]{1,0:T(8,128)(2,1)} async-done(((bf16[88,2048]{1,0:T(8,128)(2,1)}), bf16[2816,2048]{1,0:T(8,128)(2,1)}) %all-gather.31.cloned.1.call-update) | async-done | bytes 11534352 | tf_op jit(solution)/shard_map/all_gather | solution.py:220
  1509.6 10.3 multiply_convert_fusion.3
  1519.9 8.3 fusion.111
  1532.2 9.4 gather_fusion.5
  1541.6 4.7 multiply_reduce_fusion.1
  1550.5 9.4 gather_fusion.6
  1559.9 8.2 select_convert_fusion
  1568.1 8.0 reshape.545
  1576.1 7.0 reduce_sum.201
  1583.1 8.6 fusion.31
  1596.5 4.5 multiply_reduce_fusion.2
  1620.6 11.1 fusion.113
  1631.8 10.9 fusion.114
  1642.8 10.6 fusion.115
  1657.9 32.5 reduce-scatter.40.cloned.1.call-done
  1702.4 5.8 fusion.98
  1709.3 9.4 fusion.55
  1722.7 10.4 fusion.100
  1733.2 10.1 convolution_bitcast_fusion
  1743.3 10.6 convolution_bitcast_fusion.1
  1753.9 8.3 fusion.20
  1762.2 8.0 reshape.544
  1770.2 6.8 multiply_reduce_fusion
  1777.1 7.0 fusion.32
  1784.2 5.2 fusion.112
  1789.4 37.9 %reduce-scatter.46.cloned.1.call-done = f32[64,16]{1,0:T(8,128)} async-done(((f32[2048,16]{1,0:T(8,128)}), f32[64,16]{1,0:T(8,128)}) %reduce-scatter.46.cloned.1.call-update) | async-done | bytes 4112
  1828.9 4.6 fusion.51
  1833.6 45.8 %all-reduce.12 = (f32[2048]{0:T(1024)S(1)}, f32[512]{0:T(512)S(1)}, f32[2048]{0:T(1024)S(1)}) all-reduce(f32[2048]{0:T(1024)} %get-tuple-element.19, f32[512]{0:T(512)} %get-tuple-element.21, f32[2048]{0:T(1024)} %get-tuple-element.17), channel_id=9, replica_groups=mesh['expert'=8,'shard'=4] {'expert','shard'}, use_global_device_ids=true, to_apply=%region_31.33.clone | all-reduce | flops 4608 | bytes 36864
  1884.6 188.9 %reduce-scatter.34.cloned.1.call-done = f32[64,2816]{1,0:T(8,128)} async-done(((f32[2048,2816]{1,0:T(8,128)}), f32[64,2816]{1,0:T(8,128)}) %reduce-scatter.34.cloned.1.call-update) | async-done | bytes 720912 | tf_op jit(solution)/shard_map/reduce_scatter | solution.py:412
  2073.4 254.7 %reduce-scatter.36.cloned.1.call-done = f32[64,2816]{1,0:T(8,128)} async-done(((f32[2048,2816]{1,0:T(8,128)}), f32[64,2816]{1,0:T(8,128)}) %reduce-scatter.36.cloned.1.call-update) | async-done | bytes 720912 | tf_op jit(solution)/shard_map/reduce_scatter | solution.py:413
  2328.1 254.4 %reduce-scatter.38.cloned.1.call-done = f32[88,2048]{1,0:T(8,128)} async-done(((f32[2816,2048]{1,0:T(8,128)}), f32[88,2048]{1,0:T(8,128)}) %reduce-scatter.38.cloned.1.call-update) | async-done | bytes 720912 | tf_op jit(solution)/shard_map/reduce_scatter | solution.py:414
  2582.5 151.0 %reduce-scatter.28.cloned.1.call-done = f32[64,576]{1,0:T(8,128)} async-done(((f32[2048,576]{1,0:T(8,128)}), f32[64,576]{1,0:T(8,128)}) %reduce-scatter.28.cloned.1.call-update) | async-done | bytes 147472 | tf_op jit(solution)/shard_map/reduce_scatter | solution.py:404
  2733.5 147.7 %reduce-scatter.30.cloned.1.call-done = f32[16,4096]{1,0:T(8,128)} async-done(((f32[512,4096]{1,0:T(8,128)}), f32[16,4096]{1,0:T(8,128)}) %reduce-scatter.30.cloned.1.call-update) | async-done | bytes 262160 | tf_op jit(solution)/shard_map/reduce_scatter | solution.py:406
  2881.2 181.8 %reduce-scatter.32.cloned.1.call-done = f32[64,2048]{1,0:T(8,128)} async-done(((f32[2048,2048]{1,0:T(8,128)}), f32[64,2048]{1,0:T(8,128)}) %reduce-scatter.32.cloned.1.call-update) | async-done | bytes 524304 | tf_op jit(solution)/shard_map/reduce_scatter | solution.py:407
  3063.1 255.2 %reduce-scatter.26.cloned.1.call-done = f32[64,3072]{1,0:T(8,128)} async-done(((f32[2048,3072]{1,0:T(8,128)}), f32[64,3072]{1,0:T(8,128)}) %reduce-scatter.26.cloned.1.call-update) | async-done | bytes 786448 | tf_op jit(solution)/shard_map/reduce_scatter | solution.py:403
  (362 shorter events, 161.1 us)
Async XLA Ops:
  7.2 656.7 %copy-start = (bf16[2,352,2048]{2,1,0:T(8,128)(2,1)S(1)}, bf16[2,352,2048]{2,1,0:T(8,128)(2,1)}, u32[]{:S(2)}) copy-start(bf16[2,352,2048]{2,1,0:T(8,128)(2,1)} %param.36) | copy-start | bytes 8650756
  7.2 64.3 %all-gather.15.cloned.1.call-start = ((), (), s32[]{:S(2)}) async-start(), calls=%async_computation.15 | async-start | bytes 2703360 | tf_op jit(solution)/shard_map/all_gather | solution.py:159
  7.9 127.4 %all-gather.17.cloned.1.call-start = ((), (), s32[]{:S(2)}) async-start(), calls=%async_computation.16 | async-start | bytes 4325376 | tf_op jit(solution)/shard_map/all_gather | solution.py:161
  8.7 224.6 %all-gather.21.cloned.1.call-start = ((), (), s32[]{:S(2)}) async-start(), calls=%async_computation.18 | async-start | bytes 12976128 | tf_op jit(solution)/shard_map/all_gather | solution.py:158
  9.4 247.0 %all-gather.23.cloned.1.call-start = ((), (), s32[]{:S(2)}) async-start(), calls=%async_computation.19 | async-start | bytes 2621440 | tf_op jit(solution)/shard_map/all_gather | solution.py:189
  54.3 179.0 %copy-start.32 = (f32[2048]{0:T(1024)}, f32[2048]{0:T(1024)S(1)}, u32[]{:S(2)}) copy-start(f32[2048]{0:T(1024)S(1)} %convert_element_type.167) | copy-start | bytes 24580
  54.3 84.1 %copy-start.47 = (f32[512]{0:T(512)}, f32[512]{0:T(512)S(1)}, u32[]{:S(2)}) copy-start(f32[512]{0:T(512)S(1)} %convert_element_type.169) | copy-start | bytes 6148
  55.5 82.9 %copy-start.60 = (f32[128]{0:T(128)}, f32[128]{0:T(128)S(1)}, u32[]{:S(2)}) copy-start(f32[128]{0:T(128)S(1)} %add_rsqrt_fusion.2) | copy-start | bytes 1540
  74.6 65.2 %copy-start.18 = (f32[128,576]{0,1:T(8,128)}, f32[128,576]{0,1:T(8,128)S(1)}, u32[]{:S(2)}) copy-start(f32[128,576]{0,1:T(8,128)S(1)} %fusion.104) | copy-start | bytes 884740
  74.7 65.1 %copy-start.65 = (f32[128]{0:T(128)}, f32[128]{0:T(128)S(1)}, u32[]{:S(2)}) copy-start(f32[128]{0:T(128)S(1)} %add_rsqrt_fusion.1) | copy-start | bytes 1540
  142.1 139.1 %all-gather.19.cloned.1.call-start = ((), (), s32[]{:S(2)}) async-start(), calls=%async_computation.17 | async-start | bytes 2621440 | tf_op jit(solution)/shard_map/all_gather | solution.py:191
  144.4 217.0 %all-gather.25.cloned.1.call-start = ((), (), s32[]{:S(2)}) async-start(), calls=%async_computation.20 | async-start | bytes 8650752 | tf_op jit(solution)/shard_map/all_gather | solution.py:162
  145.0 438.6 %all-gather.33.cloned.1.call-start = ((), (), s32[]{:S(2)}) async-start(), calls=%async_computation.31 | async-start | bytes 15728640 | tf_op jit(solution)/shard_map/all_gather | solution.py:128
  146.4 220.0 %copy-start.45 = (f32[2048]{0:T(1024)}, f32[2048]{0:T(1024)S(1)}, u32[]{:S(2)}) copy-start(f32[2048]{0:T(1024)S(1)} %convert_element_type.177) | copy-start | bytes 24580
  147.0 14.8 copy-start.2
  150.4 82.9 %copy-start.8 = (bf16[128,2048]{1,0:T(8,128)(2,1)S(1)}, bf16[128,2048]{1,0:T(8,128)(2,1)}, u32[]{:S(2)}) copy-start(bf16[128,2048]{1,0:T(8,128)(2,1)} %param.21) | copy-start | bytes 1572868
  161.8 79.7 %copy-start.57 = (s32[768]{0:T(1024)}, s32[768]{0:T(1024)S(1)}, u32[]{:S(2)}) copy-start(s32[768]{0:T(1024)S(1)} %gather_fusion.1) | copy-start | bytes 9220
  165.3 76.1 %copy-start.50 = (s32[8,2,48]{2,1,0:T(2,128)}, s32[8,2,48]{2,1,0:T(2,128)S(1)}, u32[]{:S(2)}) copy-start(s32[8,2,48]{2,1,0:T(2,128)S(1)} %slice.69) | copy-start | bytes 9220
  165.4 76.1 %copy-start.71 = (f32[32]{0:T(128)}, f32[32]{0:T(128)S(1)}, u32[]{:S(2)}) copy-start(f32[32]{0:T(128)S(1)} %multiply_power_fusion) | copy-start | bytes 388
  166.9 74.6 %copy-start.73 = (f32[128]{0:T(128)}, f32[128]{0:T(128)S(1)}, u32[]{:S(2)}) copy-start(f32[128]{0:T(128)S(1)} %dynamic-slice_convert_fusion) | copy-start | bytes 1540
  233.3 9.4 copy-start.43
  233.3 9.4 copy-start.54
  243.4 16.9 copy-start.28
  263.6 102.8 %copy-start.41 = (f32[16,128]{1,0:T(8,128)}, f32[16,128]{1,0:T(8,128)S(1)}, u32[]{:S(2)}) copy-start(f32[16,128]{1,0:T(8,128)S(1)} %log_add_fusion) | copy-start | bytes 24580
  374.1 75.3 %copy-start.69 = (bf16[64,16]{0,1:T(8,128)(2,1)S(1)}, bf16[64,16]{0,1:T(8,128)(2,1)}, u32[]{:S(2)}) copy-start(bf16[64,16]{0,1:T(8,128)(2,1)} %param.30) | copy-start | bytes 6148
  374.1 117.6 %copy-start.15 = (bf16[128,2048]{1,0:T(8,128)(2,1)S(1)}, bf16[128,2048]{1,0:T(8,128)(2,1)}, u32[]{:S(2)}) copy-start(bf16[128,2048]{1,0:T(8,128)(2,1)} %param.22) | copy-start | bytes 1572868
  449.4 214.5 %all-gather.35.cloned.1.call-start = ((), (), s32[]{:S(2)}) async-start(), calls=%async_computation.32 | async-start | bytes 15728640 | tf_op jit(solution)/shard_map/all_gather | solution.py:128
  491.7 9.7 copy-start.38
  492.8 9.2 copy-start.63
  583.5 556.1 %all-reduce.17.cloned.1.call-start = ((), (), s32[]{:S(2)}) async-start(), calls=%async_computation.37 | async-start | bytes 50331648
  583.6 12.0 copy-start.24
  583.6 14.8 copy-start.76
  663.9 14.4 copy-start.25
  678.3 12.0 copy-start.26
  678.3 12.0 copy-start.78
  715.8 587.2 %all-gather.27.cloned.1.call-start = ((), (), s32[]{:S(2)}) async-start(), calls=%async_computation.21 | async-start | bytes 11894784 | tf_op jit(solution)/shard_map/all_gather | solution.py:218
  716.4 700.6 %all-gather.29.cloned.1.call-start = ((), (), s32[]{:S(2)}) async-start(), calls=%async_computation.22 | async-start | bytes 11894784 | tf_op jit(solution)/shard_map/all_gather | solution.py:219
  717.1 792.5 %all-gather.31.cloned.1.call-start = ((), (), s32[]{:S(2)}) async-start(), calls=%async_computation.23 | async-start | bytes 11894784 | tf_op jit(solution)/shard_map/all_gather | solution.py:220
  1144.6 102.3 %all-to-all-start.1 = ((bf16[8,2,48,2048]{3,2,1,0:T(8,128)(2,1)}), bf16[8,2,48,2048]{3,2,1,0:T(8,128)(2,1)}, u32[]{:S(2)}, u32[]{:S(2)}) async-start(bf16[8,2,48,2048]{3,2,1,0:T(8,128)(2,1)} %copy.144), calls=%async_computation.1 | async-start | bytes 6291456 | tf_op jit(solution)/shard_map/all_to_all | solution.py:134
  1155.3 96.1 %copy-start.16 = (bf16[128,2048]{1,0:T(8,128)(2,1)S(1)}, bf16[128,2048]{1,0:T(8,128)(2,1)}, u32[]{:S(2)}) copy-start(bf16[128,2048]{1,0:T(8,128)(2,1)} %param.22) | copy-start | bytes 1572868
  1246.9 299.7 %all-to-all-start.3 = ((bf16[8,2,48,2048]{3,2,1,0:T(8,128)(2,1)}), bf16[8,2,48,2048]{3,2,1,0:T(8,128)(2,1)}, u32[]{:S(2)}, u32[]{:S(2)}) async-start(bf16[8,2,48,2048]{3,2,1,0:T(8,128)(2,1)} %copy.147), calls=%async_computation.3 | async-start | bytes 6291456 | tf_op jit(solution)/shard_map/all_to_all | solution.py:134
  1251.4 402.2 %reduce-scatter.44.cloned.1.call-start = ((), (), s32[]{:S(2)}) async-start(), calls=%async_computation.35 | async-start | bytes 163840
  1583.1 10.1 slice-start
  1583.1 10.1 slice-start.1
  1603.4 52.5 %reduce-scatter.42.cloned.1.call-start = ((), (), s32[]{:S(2)}) async-start(), calls=%async_computation.34 | async-start | bytes 2621440
  1611.9 78.5 %reduce-scatter.40.cloned.1.call-start = ((), (), s32[]{:S(2)}) async-start(), calls=%async_computation.33 | async-start | bytes 2621440
  1619.1 208.2 %reduce-scatter.46.cloned.1.call-start = ((), (), s32[]{:S(2)}) async-start(), calls=%async_computation.36 | async-start | bytes 1081344
  1620.6 452.9 %reduce-scatter.34.cloned.1.call-start = ((), (), s32[]{:S(2)}) async-start(), calls=%async_computation.28 | async-start | bytes 23789568 | tf_op jit(solution)/shard_map/reduce_scatter | solution.py:412
  1631.8 696.3 %reduce-scatter.36.cloned.1.call-start = ((), (), s32[]{:S(2)}) async-start(), calls=%async_computation.29 | async-start | bytes 23789568 | tf_op jit(solution)/shard_map/reduce_scatter | solution.py:413
  1642.8 939.7 %reduce-scatter.38.cloned.1.call-start = ((), (), s32[]{:S(2)}) async-start(), calls=%async_computation.30 | async-start | bytes 23789568 | tf_op jit(solution)/shard_map/reduce_scatter | solution.py:414
  1653.4 41.3 %copy-start.19 = (f32[128,576]{0,1:T(8,128)S(1)}, f32[128,576]{0,1:T(8,128)}, u32[]{:S(2)}) copy-start(f32[128,576]{0,1:T(8,128)} %copy-done.18) | copy-start | bytes 884740
  1653.5 41.3 %copy-start.48 = (f32[512]{0:T(512)S(1)}, f32[512]{0:T(512)}, u32[]{:S(2)}) copy-start(f32[512]{0:T(512)} %copy-done.47) | copy-start | bytes 6148
  1653.5 41.3 %copy-start.66 = (f32[128]{0:T(128)S(1)}, f32[128]{0:T(128)}, u32[]{:S(2)}) copy-start(f32[128]{0:T(128)} %copy-done.65) | copy-start | bytes 1540
  1653.5 1080.1 %reduce-scatter.28.cloned.1.call-start = ((), (), s32[]{:S(2)}) async-start(), calls=%async_computation.25 | async-start | bytes 5406720 | tf_op jit(solution)/shard_map/reduce_scatter | solution.py:404
  1654.6 44.5 %copy-start.49 = (bf16[128,32]{0,1:T(8,128)(2,1)}, bf16[128,32]{0,1:T(8,128)(2,1)S(1)}, u32[]{:S(2)}) copy-start(bf16[128,32]{0,1:T(8,128)(2,1)S(1)} %get-tuple-element.48) | copy-start | bytes 24580
  1702.4 1178.8 %reduce-scatter.30.cloned.1.call-start = ((), (), s32[]{:S(2)}) async-start(), calls=%async_computation.26 | async-start | bytes 8650752 | tf_op jit(solution)/shard_map/reduce_scatter | solution.py:406
  1708.2 1354.8 %reduce-scatter.32.cloned.1.call-start = ((), (), s32[]{:S(2)}) async-start(), calls=%async_computation.27 | async-start | bytes 17301504 | tf_op jit(solution)/shard_map/reduce_scatter | solution.py:407
  1718.7 1599.5 %reduce-scatter.26.cloned.1.call-start = ((), (), s32[]{:S(2)}) async-start(), calls=%async_computation.24 | async-start | bytes 25952256 | tf_op jit(solution)/shard_map/reduce_scatter | solution.py:403
  1733.2 10.1 copy-start.27
  1733.2 20.7 slice-start.5
  1733.2 20.7 slice-start.6
  1743.3 10.6 slice-start.7
  1770.2 13.9 slice-start.2
  1827.3 1490.9 %copy-start.1 = (bf16[2,352,2048]{2,1,0:T(8,128)(2,1)S(1)}, bf16[2,352,2048]{2,1,0:T(8,128)(2,1)}, u32[]{:S(2)}) copy-start(bf16[2,352,2048]{2,1,0:T(8,128)(2,1)} %param.36) | copy-start | bytes 8650756
  (48 other events, 234.1 us)
Sparse Core Ops, SparseCore 0:
  10.9 60.6 all-gather.14
  74.4 60.9 all-gather.16
  138.2 95.0 all-gather.20
  235.3 21.0 all-gather.22
  258.4 22.8 all-gather.18
  284.0 77.4 all-gather.24
  449.5 81.4 all-gather.32
  583.6 80.2 all-gather.34
  715.9 423.6 all-reduce.16
  1142.7 160.2 all-gather.26
  1306.2 110.6 all-gather.28
  1420.1 89.5 all-gather.30
  1603.5 17.9 reduce-scatter.43
  1624.4 31.4 reduce-scatter.41
  1659.0 31.3 reduce-scatter.39
  1692.5 134.7 reduce-scatter.45
  1830.2 243.2 reduce-scatter.33
  2076.3 251.7 reduce-scatter.35
  2331.1 251.3 reduce-scatter.37
  2585.3 148.1 reduce-scatter.27
  2736.5 144.6 reduce-scatter.29
  2884.2 178.8 reduce-scatter.31
  3071.2 246.9 reduce-scatter.25
where the time goes:
time: 3330 us; the launch traced here: 3320 us
  waiting for transfers between devices  2550 us (77%)
  blocking collectives  285 us (9%)
  matrix products  274 us (8%)
  local copies, waits for them, and re-layouts  136 us (4%)
  other arithmetic  53 us (2%)
    unnamed x28, waiting for transfers between devices  498 us
    reduce_scatter x1, waiting for transfers between devices, on_device(): lax.psum_scatter(query_w_grad, ('expert', 'shard'), scatter_dimension=0,...  255 us
    reduce_scatter x1, waiting for transfers between devices, on_device(): lax.psum_scatter(sup_grad, ('expert', 'shard'), scatter_dimension=0, tile...  255 us
    reduce_scatter x1, waiting for transfers between devices, on_device(): lax.psum_scatter(sdown_grad, ('expert', 'shard'), scatter_dimension=0, ti...  254 us
    reduce_scatter x1, waiting for transfers between devices, on_device(): lax.psum_scatter(sgate_grad, ('expert', 'shard'), scatter_dimension=0, ti...  189 us
    reduce_scatter x1, waiting for transfers between devices, on_device(): lax.psum_scatter(output_w_grad, ('expert', 'shard'), scatter_dimension=0,...  182 us
    reduce_scatter x1, waiting for transfers between devices, on_device(): lax.psum_scatter(compress_w_grad, ('expert', 'shard'), scatter_dimension=...  151 us
    all_to_all x2, blocking collectives, to_owners(): lax.all_to_all(buffer, 'expert', split_axis=0, concat_axis=0, tiled=True)  150 us
  transfers between devices with their start and end apart: 25, of which 22 were waited for; matrix products, arithmetic and copies ran while one was open for 10% of the time, Pallas kernels for 0%

commit v1 on v0

v1 whole, which is shorter than its diff:
```python
import jax
import jax.numpy as jnp
from jax import lax
from jax.sharding import PartitionSpec as P

HEADS = 16
NOPE = 128
ROPE = 64
VDIM = 128
KV_RANK = 512
CONTS = 2


EPSILON = 1e-06
THETA = 10000.0
NEGATIVE = -1e30
BOTH = ("expert", "shard")
BF = jnp.bfloat16
F32 = jnp.float32


def rms_forward(values, gain_row):
    inverse = lax.rsqrt(jnp.mean(values * values, axis=-1, keepdims=True) + EPSILON)
    return (values * inverse * gain_row, inverse)


def rms_backward(values, inverse, gain_row, upstream):
    normed = values * inverse
    scaled = upstream * gain_row
    value_grad = inverse * (scaled - normed * jnp.mean(scaled * normed, axis=-1, keepdims=True))
    return (value_grad, jnp.sum(upstream * normed, axis=0))


def rope_tables(positions, width):
    half_width = width // 2
    frequency = THETA ** (-2.0 * jnp.arange(half_width, dtype=jnp.float32) / width)
    angles = positions.astype(jnp.float32)[:, None] * frequency[None, :]
    return (jnp.cos(angles), jnp.sin(angles))


def rotate(values, cosine_table, sine_table):
    half_width = values.shape[-1] // 2
    first_half = values[..., :half_width]
    second = values[..., half_width:]
    return jnp.concatenate(
        [
            first_half * cosine_table - second * sine_table,
            second * cosine_table + first_half * sine_table,
        ],
        axis=-1,
    )


def positions_of(group_ids):
    length = group_ids.shape[0]
    token_index = jnp.arange(length, dtype=jnp.int32)
    labels = jnp.arange(CONTS + 1, dtype=jnp.int32)
    member = (group_ids[:, None] == labels[None, :]).astype(jnp.int32)
    counts = jnp.sum(member, axis=0)
    starts = jnp.cumsum(counts) - counts
    start_of = jnp.sum(member * starts[None, :], axis=1)
    return token_index - start_of + jnp.where(group_ids > 0, counts[0], 0)


def kept_pairs(choice_ids, rank_row, choice_hot, capacity):
    row_count, top_count, expert_total = choice_hot.shape
    per_k = jnp.sum(choice_hot, axis=0)
    before_k = jnp.cumsum(per_k, axis=0) - per_k
    lower = (rank_row[None, :] < rank_row[:, None]).astype(F32)
    same_k = jnp.dot(
        lower.astype(BF),
        choice_hot.reshape(row_count, top_count * expert_total).astype(BF),
        preferred_element_type=F32,
    ).reshape(row_count, top_count, expert_total)
    place = jnp.sum((same_k + before_k[None]) * choice_hot, axis=-1)
    return (place < capacity).astype(F32)


def mm(a, b):
    return jnp.dot(a, b, preferred_element_type=F32)


def mm_nt(a, b):
    return lax.dot_general(a, b, (((1,), (1,)), ((), ())), preferred_element_type=F32)


def mm_tn(a, b):
    return lax.dot_general(a, b, (((0,), (0,)), ((), ())), preferred_element_type=F32)


def gather(value, axes):
    return lax.all_gather(value, axes, axis=0, tiled=True)


def scatter_sum(value, axes):
    return lax.psum_scatter(value, axes, scatter_dimension=0, tiled=True)


def columns_out(value):
    count = lax.axis_size("shard")
    rows, width = value.shape
    parts = value.reshape(rows, count, width // count).transpose(1, 0, 2)
    return lax.all_to_all(parts, "shard", split_axis=0, concat_axis=0).reshape(
        count * rows, width // count
    )


def columns_back(value):
    count = lax.axis_size("shard")
    rows, width = value.shape
    parts = lax.all_to_all(
        value.reshape(count, rows // count, width), "shard", split_axis=0, concat_axis=0
    )
    return parts.transpose(1, 0, 2).reshape(rows // count, count * width)


def ffn_chunk(rows, cots, gates, w_gate, w_up, w_down, widths):
    tokens = rows.shape[0]
    spread = jnp.concatenate(
        [
            jnp.broadcast_to(gates[:, i : i + 1], (tokens, width))
            for i, width in enumerate(widths[:-1])
        ]
        + [jnp.ones((tokens, widths[-1]), F32)],
        axis=1,
    )
    gate_val = mm(rows, w_gate)
    up_val = mm(rows, w_up)
    down_grad = mm_nt(cots, w_down)
    sigmoid = jax.nn.sigmoid(gate_val)
    act = gate_val * sigmoid
    slope = sigmoid * (1.0 + gate_val * (1.0 - sigmoid))
    hidden = (act * up_val).astype(BF).astype(F32)
    scaled_hidden = (hidden * spread).astype(BF)
    part = mm(scaled_hidden, w_down).astype(BF)
    weighted = hidden * down_grad
    starts = [sum(widths[:i]) for i in range(len(widths) - 1)]
    gate_grads = jnp.stack(
        [jnp.sum(weighted[:, b : b + w], axis=1) for b, w in zip(starts, widths)], axis=1
    )
    down_grad = down_grad * spread
    gate_d = (down_grad * up_val * slope).astype(BF)
    up_d = (down_grad * act).astype(BF)
    back = (mm_nt(gate_d, w_gate) + mm_nt(up_d, w_up)).astype(BF)
    return (
        part,
        back,
        gate_grads,
        mm_tn(rows, gate_d),
        mm_tn(rows, up_d),
        mm_tn(scaled_hidden, cots),
    )


def on_device(
    tokens,
    cotangent,
    norm1_gain,
    q_weight,
    kva_weight,
    kv_gain,
    kvb_weight,
    o_weight,
    norm2_gain,
    router_weight,
    shared_gate,
    shared_up,
    shared_down,
    expert_gate,
    expert_up,
    expert_down,
    expert_ids,
    token_rank,
    seq_ids,
):
    expert_count = lax.axis_size("expert")
    shard_count = lax.axis_size("shard")
    device_count = expert_count * shard_count
    expert_at = lax.axis_index("expert")
    shard_at = lax.axis_index("shard")
    tok_rows, width = tokens.shape
    group_len = seq_ids.shape[0]
    local_experts = expert_gate.shape[0]
    all_experts = local_experts * expert_count
    top_count = expert_ids.shape[1]
    capacity = max(2, tok_rows * top_count // all_experts)
    score_scale = (NOPE + ROPE) ** (-0.5)
    own_heads = HEADS // shard_count
    latent_width = kva_weight.shape[1]

    q_mine = gather(columns_out(q_weight), "expert")
    kvb_mine = gather(columns_out(kvb_weight), "expert")
    kva_all = gather(kva_weight, BOTH)
    o_all = gather(o_weight, BOTH)
    o_mine = lax.dynamic_slice_in_dim(o_all, shard_at * own_heads * VDIM, own_heads * VDIM)
    norm1_scale = gather(norm1_gain, BOTH).astype(F32)
    latent_scale = gather(kv_gain, BOTH).astype(F32)
    norm2_scale = gather(norm2_gain, BOTH).astype(F32)
    router = gather(router_weight, BOTH)

    positions = positions_of(seq_ids)
    cosine_table, sine_table = rope_tables(positions, ROPE)
    token_index = jnp.arange(group_len, dtype=jnp.int32)
    allowed = (token_index[None, :] <= token_index[:, None]) & (
        (seq_ids[None, :] == 0) | (seq_ids[None, :] == seq_ids[:, None])
    )
    input_rows = tokens.astype(F32)
    group_rows = gather(tokens, "shard").astype(F32)
    normed_group, _ = rms_forward(group_rows, norm1_scale)
    hidden_one = normed_group.astype(BF)
    query_raw = mm(hidden_one, q_mine).reshape(group_len, own_heads, NOPE + ROPE)
    q_nope = query_raw[:, :, :NOPE].astype(BF)
    q_rope = rotate(
        query_raw[:, :, NOPE:], cosine_table[:, None, :], sine_table[:, None, :]
    ).astype(BF)
    compressed = mm(hidden_one, kva_all)
    latent_norm, inverse_latent = rms_forward(compressed[:, :KV_RANK], latent_scale)
    latent = latent_norm.astype(BF)
    k_rope = rotate(compressed[:, KV_RANK:], cosine_table, sine_table).astype(BF)
    keyval = mm(latent, kvb_mine).astype(BF).reshape(group_len, own_heads, NOPE + VDIM)
    keys = keyval[:, :, :NOPE]
    values = keyval[:, :, NOPE:]
    scores = jnp.einsum("qhd,khd->hqk", q_nope, keys, preferred_element_type=F32)
    scores = scores + jnp.einsum("qhd,kd->hqk", q_rope, k_rope, preferred_element_type=F32)
    scores = jnp.where(allowed[None], scores * score_scale, NEGATIVE)
    top_score = jnp.max(scores, axis=-1, keepdims=True)
    log_total = top_score + jnp.log(jnp.sum(jnp.exp(scores - top_score), axis=-1, keepdims=True))
    soft_probs = jnp.exp(scores - log_total)
    prob_low = soft_probs.astype(BF)
    attended = (
        jnp.einsum("hqk,khd->qhd", prob_low, values, preferred_element_type=F32)
        .astype(BF)
        .reshape(group_len, own_heads * VDIM)
    )
    projected = scatter_sum(mm(attended, o_mine).astype(BF), "shard").astype(F32)
    mixed = input_rows + projected

    normed_two, inverse_two = rms_forward(mixed, norm2_scale)
    hidden_two = normed_two.astype(BF)
    logits = mm(hidden_two, router)
    choice_hot = (
        expert_ids[:, :, None] == jnp.arange(all_experts, dtype=jnp.int32)[None, None, :]
    ).astype(F32)
    chosen = jnp.sum(choice_hot * logits[:, None, :], axis=-1)
    gate_probs = jax.nn.softmax(chosen, axis=-1)
    kept = kept_pairs(expert_ids, token_rank, choice_hot, capacity)
    gate_table = jnp.sum(choice_hot * (gate_probs * kept)[:, :, None], axis=1)

    shared_width = shared_down.shape[0]
    both_shared = jnp.stack([shared_gate, shared_up]).reshape(
        2, shared_gate.shape[0], device_count, shared_width
    )
    both_shared = lax.all_to_all(
        both_shared.transpose(2, 0, 1, 3), BOTH, split_axis=0, concat_axis=0
    )
    both_shared = both_shared.transpose(1, 0, 2, 3).reshape(2, width, shared_width)
    own_width = expert_gate.shape[2]
    widths = [own_width] * local_experts + [shared_width]
    w_gate = jnp.concatenate([expert_gate[i] for i in range(local_experts)] + [both_shared[0]], 1)
    w_up = jnp.concatenate([expert_up[i] for i in range(local_experts)] + [both_shared[1]], 1)
    w_down = jnp.concatenate([expert_down[i] for i in range(local_experts)] + [shared_down], 0)
    def ffn(rows, cots, table):
        rows_all = gather(rows, BOTH)
        cots_all = gather(cots, BOTH)
        gates_all = gather(table, BOTH)
        gates_mine = lax.dynamic_slice_in_dim(
            gates_all, expert_at * local_experts, local_experts, 1
        )
        out_part, back_part, gate_grads, *weight_grads = ffn_chunk(
            rows_all, cots_all, gates_mine, w_gate, w_up, w_down, widths
        )
        gate_grad_table = jnp.where(
            (jnp.arange(128) // local_experts == expert_at)[None, :],
            jnp.tile(gate_grads, (1, 128 // local_experts)),
            0.0,
        ).astype(BF)
        back_sum = scatter_sum(jnp.concatenate([back_part, gate_grad_table], axis=1), BOTH)
        return scatter_sum(out_part, BOTH), back_sum, weight_grads

    rounds = max(1, tok_rows * device_count // 4096)
    if rounds == 1:
        out_sum, back_sum, weight_grads = ffn(hidden_two, cotangent, gate_table)
    else:

        def one_round(total, part):
            out_rows, back_rows, grads = ffn(*part)
            return [t + g for t, g in zip(total, grads)], (out_rows, back_rows)

        in_rounds = lambda value: value.reshape((rounds, -1) + value.shape[1:])
        zeros = [jnp.zeros(w.shape, F32) for w in (w_gate, w_up, w_down)]
        weight_grads, (out_sum, back_sum) = lax.scan(
            one_round, zeros, (in_rounds(hidden_two), in_rounds(cotangent), in_rounds(gate_table))
        )
        out_sum = out_sum.reshape((tok_rows,) + out_sum.shape[2:])
        back_sum = back_sum.reshape((tok_rows,) + back_sum.shape[2:])
    out_sum, back_sum = out_sum.astype(F32), back_sum.astype(F32)
    w_gate_grad, w_up_grad, w_down_grad = weight_grads
    output = (mixed + out_sum).astype(BF)

    def split_experts(grad, axis):
        pieces = [
            lax.slice_in_dim(grad, i * own_width, (i + 1) * own_width, axis=axis)
            for i in range(local_experts)
        ]
        shared = lax.slice_in_dim(grad, local_experts * own_width, None, axis=axis)
        return jnp.stack(pieces), shared

    egate_grad, sgate_mine = split_experts(w_gate_grad, 1)
    eup_grad, sup_mine = split_experts(w_up_grad, 1)
    edown_grad, sdown_grad = split_experts(w_down_grad, 0)
    shared_grads = (
        jnp.stack([sgate_mine, sup_mine])
        .reshape(2, device_count, width // device_count, shared_width)
        .transpose(1, 0, 2, 3)
    )
    shared_grads = lax.all_to_all(shared_grads, BOTH, split_axis=0, concat_axis=0)
    shared_grads = shared_grads.transpose(1, 2, 0, 3).reshape(
        2, width // device_count, device_count * shared_width
    )

    upstream = cotangent.astype(F32)
    gate_grad = jnp.sum(
        choice_hot * back_sum[:, None, width : width + all_experts], axis=-1
    ) * kept
    chosen_grad = gate_probs * (gate_grad - jnp.sum(gate_probs * gate_grad, axis=-1, keepdims=True))
    logit_grad = jnp.sum(choice_hot * chosen_grad[:, :, None], axis=1).astype(BF)
    router_part = mm_tn(hidden_two, logit_grad)
    hidden_two_grad = back_sum[:, :width] + mm_nt(logit_grad, router)
    mixed_norm_grad, norm2_part = rms_backward(mixed, inverse_two, norm2_scale, hidden_two_grad)
    mixed_grad = upstream + mixed_norm_grad

    mixed_grad_group = gather(mixed_grad.astype(BF), "shard")
    o_part = mm_tn(attended, mixed_grad_group)
    attended_grad = (
        mm_nt(mixed_grad_group, o_mine).astype(BF).reshape(group_len, own_heads, VDIM)
    )
    prob_grad = jnp.einsum("qhd,khd->hqk", attended_grad, values, preferred_element_type=F32)
    values_grad = jnp.einsum("hqk,qhd->khd", prob_low, attended_grad, preferred_element_type=F32)
    score_grad = (
        soft_probs * (prob_grad - jnp.sum(soft_probs * prob_grad, axis=-1, keepdims=True))
    ).astype(BF)
    q_nope_grad = (
        jnp.einsum("hqk,khd->qhd", score_grad, keys, preferred_element_type=F32) * score_scale
    )
    q_rope_grad = (
        jnp.einsum("hqk,kd->qhd", score_grad, k_rope, preferred_element_type=F32) * score_scale
    )
    keys_grad = (
        jnp.einsum("hqk,qhd->khd", score_grad, q_nope, preferred_element_type=F32) * score_scale
    )
    rope_grad = (
        jnp.einsum("hqk,qhd->kd", score_grad, q_rope, preferred_element_type=F32) * score_scale
    )
    keyval_grad = (
        jnp.concatenate([keys_grad, values_grad], axis=-1)
        .reshape(group_len, own_heads * (NOPE + VDIM))
        .astype(BF)
    )
    kvb_part = mm_tn(latent, keyval_grad)
    latent_part = jnp.concatenate([mm_nt(keyval_grad, kvb_mine), rope_grad], axis=1).astype(BF)
    latent_sum = scatter_sum(latent_part, "shard").astype(F32)
    own_start = shard_at * tok_rows
    own_rows = lambda value: lax.dynamic_slice_in_dim(value, own_start, tok_rows)
    latent_raw_grad, kv_gain_part = rms_backward(
        own_rows(compressed[:, :KV_RANK]),
        own_rows(inverse_latent),
        latent_scale,
        latent_sum[:, :KV_RANK],
    )
    compressed_grad = jnp.concatenate(
        [
            latent_raw_grad,
            rotate(latent_sum[:, KV_RANK:], own_rows(cosine_table), -own_rows(sine_table)),
        ],
        axis=1,
    ).astype(BF)
    compressed_grad_group = gather(compressed_grad, "shard")
    kva_columns = latent_width // shard_count
    compressed_mine = lax.dynamic_slice_in_dim(
        compressed_grad_group, shard_at * kva_columns, kva_columns, 1
    )
    kva_mine = lax.dynamic_slice_in_dim(kva_all, shard_at * kva_columns, kva_columns, 1)
    query_grad = jnp.concatenate(
        [q_nope_grad, rotate(q_rope_grad, cosine_table[:, None, :], -sine_table[:, None, :])],
        axis=-1,
    )
    query_grad = query_grad.reshape(group_len, own_heads * (NOPE + ROPE)).astype(BF)
    q_part = mm_tn(hidden_one, query_grad)
    kva_part = mm_tn(hidden_one, compressed_mine)
    hidden_one_part = mm_nt(query_grad, q_mine) + mm_nt(compressed_mine, kva_mine)
    hidden_one_grad = scatter_sum(hidden_one_part.astype(BF), "shard").astype(F32)
    _, inverse_one = rms_forward(input_rows, norm1_scale)
    input_norm_grad, norm1_part = rms_backward(
        input_rows, inverse_one, norm1_scale, hidden_one_grad
    )
    tokens_grad = mixed_grad + input_norm_grad

    q_grad = columns_back(scatter_sum(q_part.astype(BF), "expert")).astype(F32)
    kva_grad = columns_back(scatter_sum(kva_part.astype(BF), "expert")).astype(F32)
    kvb_grad = columns_back(scatter_sum(kvb_part.astype(BF), "expert")).astype(F32)
    o_wide = lax.dynamic_update_slice_in_dim(
        jnp.zeros(o_all.shape, BF), o_part.astype(BF), shard_at * own_heads * VDIM, 0
    )
    o_grad = scatter_sum(o_wide, BOTH).astype(F32)
    router_grad = scatter_sum(router_part, BOTH)
    norm1_grad = scatter_sum(norm1_part, BOTH)
    norm2_grad = scatter_sum(norm2_part, BOTH)
    kv_gain_grad = scatter_sum(kv_gain_part, BOTH)
    return (
        output,
        tokens_grad,
        norm1_grad,
        q_grad,
        kva_grad,
        kv_gain_grad,
        kvb_grad,
        o_grad,
        norm2_grad,
        router_grad,
        shared_grads[0],
        shared_grads[1],
        sdown_grad,
        egate_grad,
        eup_grad,
        edown_grad,
    )


def solution(mesh):
    rows = P(BOTH, None)
    flat = P(BOTH)
    columns = P("expert", None, "shard")
    depth = P("expert", "shard", None)
    return jax.shard_map(
        on_device,
        mesh=mesh,
        in_specs=(
            rows,
            rows,
            flat,
            rows,
            rows,
            flat,
            rows,
            rows,
            flat,
            rows,
            rows,
            rows,
            rows,
            columns,
            columns,
            depth,
            rows,
            flat,
            P("expert"),
        ),
        out_specs=(
            rows,
            rows,
            flat,
            rows,
            rows,
            flat,
            rows,
            rows,
            flat,
            rows,
            rows,
            rows,
            rows,
            columns,
            columns,
            depth,
        ),
        check_vma=False,
    )
```

time: 3330 us -> 1680 us (0.50)
  waiting for transfers between devices: 2550 us -> 1020 us
  blocking collectives: 285 us -> 213 us
  local copies, waits for them, and re-layouts: 136 us -> 76 us
    reduce_scatter x7 -> x8, waiting for transfers between devices: 1430 us -> 667 us  [scatter_sum(): return lax.psum_scatter(value, axes, scatter_dimension=0, tiled=True)]
    unnamed x28 -> x20, waiting for transfers between devices: 498 us -> 24.3 us
    all_gather x11 -> x8, waiting for transfers between devices: 527 us -> 289 us  [gather(): return lax.all_gather(value, axes, axis=0, tiled=True)]
    all_to_all x2, blocking collectives: 150 us -> 23.8 us  [columns_out(): lax.all_to_all(parts, 'shard', split_axis=0, concat_axis=0)]
    all_gather x2 -> x3, blocking collectives: 46.6 us -> 107 us  [gather(): return lax.all_gather(value, axes, axis=0, tiled=True)]
    all_to_all x2 -> x5, waiting for transfers between devices: 91.6 us -> 40 us  [the longest x1 36.1 us: on_device(): lax.all_to_all(shared_grads, BOTH, split_axis=0, concat_axis=0)]
    gather x8 -> x0, local copies, waits for them, and re-layouts: 41.2 us -> none  [the longest x1 9.4 us: on_device(): jnp.take(padded_out, dest_flat, axis=0).reshape(tok_rows, top_count, width)]
    dot_general x40 -> x32, matrix products: 268 us -> 268 us  [the longest x8 105 us: mm_nt(): lax.dot_general(a, b, (((1,), (1,)), ((), ())), preferred_element_type=F32)]
  transfers between devices with their start and end apart: 25 -> 23, of which waited for: 22 -> 18; matrix products, arithmetic and copies ran while one was open for 10% -> 15% of each run, Pallas kernels for 0% -> 0%
where the time goes in v1:
time: 1680 us; the launch traced here: 1670 us
  waiting for transfers between devices  1020 us (61%)
  matrix products  270 us (16%)
  blocking collectives  213 us (13%)
  local copies, waits for them, and re-layouts  76 us (5%)
  other arithmetic  55.7 us (3%)
  starting transfers between devices  21.5 us (1%)
    reduce_scatter x8, waiting for transfers between devices, scatter_sum(): return lax.psum_scatter(value, axes, scatter_dimension=0, tiled=True)  667 us
    all_gather x8, waiting for transfers between devices, gather(): return lax.all_gather(value, axes, axis=0, tiled=True)  289 us
    all_gather x3, blocking collectives, gather(): return lax.all_gather(value, axes, axis=0, tiled=True)  107 us
    dot_general x8, matrix products, mm_nt(): lax.dot_general(a, b, (((1,), (1,)), ((), ())), preferred_element_type=F32)  105 us
    unnamed x2, blocking collectives  82 us
    dot_general x8, matrix products, mm(): return jnp.dot(a, b, preferred_element_type=F32)  81.2 us
    dot_general x7, matrix products, mm_tn(): lax.dot_general(a, b, (((0,), (0,)), ((), ())), preferred_element_type=F32)  75.1 us
    all_to_all x1, waiting for transfers between devices, on_device(): lax.all_to_all(shared_grads, BOTH, split_axis=0, concat_axis=0)  36.1 us
  transfers between devices with their start and end apart: 23, of which 18 were waited for; matrix products, arithmetic and copies ran while one was open for 15% of the time, Pallas kernels for 0%

profile of v1, /device:TPU:0, one launch (start us, length us, event | category | flops | bytes accessed | tf_op | source)
XLA Modules:
  0.0 1672.7 jit_solution(9290703769984129238)
XLA Ops:
  9.8 8.7 all_to_all.35
  20.0 15.1 all_to_all.36
  36.7 40.3 %all-reduce.7 = (bf16[512]{0:T(512)(128)(2,1)S(1)}, bf16[2048]{0:T(1024)(128)(2,1)S(1)}, bf16[2048]{0:T(1024)(128)(2,1)S(1)}) all-reduce(bf16[512]{0:T(512)(128)(2,1)S(1)} %dynamic-update-slice.1, bf16[2048]{0:T(1024)(128)(2,1)S(1)} %dynamic-update-slice, ...), channel_id=1, replica_groups=mesh['expert'=8,'shard'=4] {'expert','shard'}, use_global_device_ids=true, to_apply=%add.1 | all-reduce | flops 4608 | bytes 18432
  80.1 20.0 %all-gather.12.cloned.1.call-done = bf16[2048,576]{1,0:T(8,128)(2,1)} async-done(((bf16[64,576]{1,0:T(8,128)(2,1)}), bf16[2048,576]{1,0:T(8,128)(2,1)}) %all-gather.12.cloned.1.call-update) | async-done | bytes 2359312 | tf_op jit(solution)/shard_map/all_gather | solution.py:92
  100.1 3.9 fusion.89
  105.3 36.1 %all-gather.14.cloned.1.call-done = bf16[512,1024]{1,0:T(8,128)(2,1)} async-done(((bf16[64,1024]{1,0:T(8,128)(2,1)}), bf16[512,1024]{1,0:T(8,128)(2,1)}) %all-gather.14.cloned.1.call-update) | async-done | bytes 1048592 | tf_op jit(solution)/shard_map/all_gather | solution.py:92
  148.6 54.1 %all-gather.16.cloned.1.call-done = bf16[2048,768]{1,0:T(8,128)(2,1)} async-done(((bf16[256,768]{1,0:T(8,128)(2,1)}), bf16[2048,768]{1,0:T(8,128)(2,1)}) %all-gather.16.cloned.1.call-update) | async-done | bytes 3145744 | tf_op jit(solution)/shard_map/all_gather | solution.py:92
  202.6 4.4 fusion.87
  212.7 68.7 %all-gather.18.cloned.1.call-done = bf16[2048,2048]{1,0:T(8,128)(2,1)} async-done(((bf16[64,2048]{1,0:T(8,128)(2,1)}), bf16[2048,2048]{1,0:T(8,128)(2,1)}) %all-gather.18.cloned.1.call-update) | async-done | bytes 8388624 | tf_op jit(solution)/shard_map/all_gather | solution.py:92
  281.5 4.2 convolution_convert_fusion.3
  286.1 29.7 %reduce-scatter.15.cloned.1.call-done = bf16[128,2048]{1,0:T(8,128)(2,1)} async-done(((bf16[512,2048]{1,0:T(8,128)(2,1)}), bf16[128,2048]{1,0:T(8,128)(2,1)}) %reduce-scatter.15.cloned.1.call-update) | async-done | bytes 524304 | tf_op jit(solution)/shard_map/reduce_scatter | solution.py:96
  324.7 4.6 all-to-all-start.2
  329.4 3.8 slice_bitcast_fusion.11
  333.2 60.2 %all-gather = bf16[32,64,16]{1,2,0:T(8,128)(2,1)S(1)} all-gather(bf16[1,64,16]{1,2,0:T(8,128)(2,1)S(1)} %bitcast.193), channel_id=1, replica_groups=mesh['expert'=8,'shard'=4] {'expert','shard'}, dimensions={0}, use_global_device_ids=true | all-gather | bytes 67584 | tf_op jit(solution)/shard_map/all_gather | solution.py:92
  394.4 4.1 slice_bitcast_fusion.9
  402.6 39.8 %all_gather.52 = f32[4096,16]{0,1:T(8,128)S(1)} all-gather(f32[128,16]{0,1:T(8,128)S(1)} %select_reduce_fusion.2), channel_id=1, replica_groups=mesh['expert'=8,'shard'=4] {'expert','shard'}, dimensions={0}, use_global_device_ids=true | all-gather | bytes 270336 | tf_op jit(solution)/shard_map/all_gather | solution.py:92
  442.3 11.4 all-gather.20.cloned.1.call-done
  453.7 20.9 %fusion.17 = f32[4096,792]{0,1:T(8,128)} fusion(bf16[4096,2048]{1,0:T(8,128)(2,1)} %all-gather.20.cloned.1.call-done, bf16[2048,88]{0,1:T(8,128)(2,1)S(1)} %copy.226, bf16[2048,352]{0,1:T(8,128)(2,1)} %get-tuple-element.48, bf16[2048,352]{0,1:T(8,128)(2,1)} %get-tuple-element.47), kind=kOutput, calls=%fused_computation.69 | convolution fusion | flops 13297287168 | bytes 32997376 | tf_op jit(solution)/shard_map/dot_general | solution.py:80
  474.6 19.9 %fusion.19 = f32[4096,792]{0,1:T(8,128)} fusion(bf16[4096,2048]{1,0:T(8,128)(2,1)} %all-gather.20.cloned.1.call-done, bf16[2048,88]{0,1:T(8,128)(2,1)S(1)} %copy.225, bf16[2048,352]{0,1:T(8,128)(2,1)S(1)} %copy-done.31, bf16[2048,352]{0,1:T(8,128)(2,1)S(1)} %copy-done.30), kind=kOutput, calls=%fused_computation.71 | convolution fusion | flops 13297287168 | bytes 32997376 | tf_op jit(solution)/shard_map/dot_general | solution.py:80
  494.6 75.7 %all-gather.22.cloned.1.call-done = bf16[4096,2048]{1,0:T(8,128)(2,1)} async-done(((bf16[128,2048]{1,0:T(8,128)(2,1)}), bf16[4096,2048]{1,0:T(8,128)(2,1)}) %all-gather.22.cloned.1.call-update) | async-done | bytes 16777232 | tf_op jit(solution)/shard_map/all_gather | solution.py:92
  570.3 3.2 broadcast_in_dim.44
  573.5 3.2 broadcast_in_dim.42
  576.7 39.0 %convert_multiply_fusion = (f32[4096,792]{0,1:T(8,128)}, bf16[4096,792]{0,1:T(8,128)(2,1)}, bf16[4096,792]{0,1:T(8,128)(2,1)}, bf16[4096,792]{0,1:T(8,128)(2,1)}) fusion(f32[4096,792]{0,1:T(8,128)} %fusion.17, f32[4096,792]{0,1:T(8,128)} %fusion.19, f32[792]{0:T(1024)S(1)} %pad.27.clone, f32[4096,352]{0,1:T(8,128)} %broadcast_in_dim.44, ...), kind=kOutput, calls=%fused_computation.2 | convolution fusion | flops 13362167808 | bytes 89951328 | tf_op jit(solution)/shard_map/dot_general | solution.py:84
  615.7 4.9 slice_reduce_fusion.1
  622.8 25.0 %fusion.18 = f32[4096,2048]{1,0:T(8,128)} fusion(bf16[4096,792]{0,1:T(8,128)(2,1)} %get-tuple-element.37, bf16[2048,88]{0,1:T(8,128)(2,1)} %copy-done.46, bf16[2048,352]{0,1:T(8,128)(2,1)} %get-tuple-element.46, bf16[2048,352]{0,1:T(8,128)(2,1)} %get-tuple-element.45), kind=kOutput, calls=%fused_computation.70 | convolution fusion | flops 13297287168 | bytes 43286528 | tf_op jit(solution)/shard_map/dot_general | solution.py:84
  647.9 27.2 %add_convert_fusion = bf16[4096,2048]{1,0:T(8,128)(2,1)} fusion(f32[4096,2048]{1,0:T(8,128)} %fusion.18, bf16[4096,792]{0,1:T(8,128)(2,1)} %get-tuple-element.38, bf16[2048,88]{0,1:T(8,128)(2,1)} %copy-done.45, bf16[2048,352]{0,1:T(8,128)(2,1)} %get-tuple-element.48, bf16[2048,352]{0,1:T(8,128)(2,1)S(1)} %copy-done.32), kind=kOutput, calls=%fused_computation | convolution fusion | flops 13314064384 | bytes 60063744 | tf_op jit(solution)/shard_map/dot_general | solution.py:84
  675.1 15.7 pad_maximum_fusion
  690.9 192.3 %reduce-scatter.19.cloned.1.call-done = bf16[128,2176]{1,0:T(8,128)(2,1)} async-done(((bf16[4096,2176]{1,0:T(8,128)(2,1)}), bf16[128,2176]{1,0:T(8,128)(2,1)}) %reduce-scatter.19.cloned.1.call-update) | async-done | bytes 557072 | tf_op jit(solution)/shard_map/reduce_scatter | solution.py:96
  889.3 23.5 %all-gather.24.cloned.1.call-done = bf16[512,2048]{1,0:T(8,128)(2,1)} async-done(((bf16[128,2048]{1,0:T(8,128)(2,1)}), bf16[512,2048]{1,0:T(8,128)(2,1)}) %all-gather.24.cloned.1.call-update) | async-done | bytes 2097168 | tf_op jit(solution)/shard_map/all_gather | solution.py:92
  912.8 3.6 fusion.20
  925.7 3.3 convolution_convert_fusion.5
  931.6 16.6 reduce-scatter.31.cloned.1.call-done
  952.9 7.2 all_gather.55
  960.9 3.3 convolution_convert_fusion.4
  964.5 4.0 fusion.97
  968.5 4.1 add_convert_fusion.1
  972.9 5.0 convolution_convert_fusion.1
  978.0 25.5 %convolution_convert_fusion = bf16[4096,2048]{1,0:T(8,128)(2,1)} fusion(bf16[88,2048]{1,0:T(8,128)(2,1)} %param.31, bf16[352,2048]{1,0:T(8,128)(2,1)} %get-tuple-element.50, bf16[352,2048]{1,0:T(8,128)(2,1)S(1)} %copy-done.28, bf16[4096,792]{0,1:T(8,128)(2,1)} %get-tuple-element.34, f32[4096,352]{0,1:T(8,128)} %broadcast_in_dim.44, ...), kind=kOutput, calls=%fused_computation.4 | convolution fusion | flops 13321895936 | bytes 38046816 | tf_op jit(solution)/shard_map/dot_general | solution.py:80
  1003.9 4.4 broadcast_in_dim.48
  1008.3 2.6 fusion.9
  1010.9 24.5 %fusion.82 = f32[792,2048]{1,0:T(8,128)} fusion(bf16[4096,2048]{1,0:T(8,128)(2,1)} %all-gather.22.cloned.1.call-done, bf16[4096,792]{0,1:T(8,128)(2,1)} %get-tuple-element.34, f32[4096,352]{0,1:T(8,128)} %broadcast_in_dim.44, f32[4096,352]{0,1:T(8,128)} %broadcast_in_dim.42, f32[792]{0:T(1024)S(1)} %pad.27.clone), kind=kOutput, calls=%fused_computation.207 | convolution fusion | flops 13303775232 | bytes 41290848 | tf_op jit(solution)/shard_map/dot_general | solution.py:88
  1037.4 18.2 %fusion.99 = f32[2048,792]{0,1:T(8,128)S(1)} fusion(bf16[4096,2048]{1,0:T(8,128)(2,1)} %all-gather.20.cloned.1.call-done, bf16[4096,792]{0,1:T(8,128)(2,1)} %get-tuple-element.38), kind=kOutput, calls=%fused_computation.218 | convolution fusion | flops 13287555072 | bytes 29753344 | tf_op jit(solution)/shard_map/dot_general | solution.py:88
  1055.6 2.7 copy-done.11
  1058.7 18.2 %fusion.98 = f32[2048,792]{0,1:T(8,128)S(1)} fusion(bf16[4096,2048]{1,0:T(8,128)(2,1)} %all-gather.20.cloned.1.call-done, bf16[4096,792]{0,1:T(8,128)(2,1)} %get-tuple-element.37), kind=kOutput, calls=%fused_computation.217 | convolution fusion | flops 13287555072 | bytes 29753344 | tf_op jit(solution)/shard_map/dot_general | solution.py:88
  1076.9 2.7 copy-done.12
  1081.7 4.9 all-to-all-start.6
  1086.7 3.3 slice_bitcast_fusion.1
  1089.9 3.3 pad_maximum_fusion.3
  1096.3 4.8 pad_maximum_fusion.1
  1101.1 36.1 %all-to-all-done.6 = f32[32,2,64,88]{3,2,1,0:T(8,128)S(1)} async-done(((f32[32,2,64,88]{3,2,1,0:T(8,128)}), f32[32,2,64,88]{3,2,1,0:T(8,128)S(1)}, u32[]{:S(2)}, u32[]{:S(2)}) %all-to-all-start.6) | async-done | bytes 1441824 | tf_op jit(solution)/shard_map/all_to_all | solution.py:316
  1140.5 3.0 copy.247
  1143.5 2.7 squeeze.42
  1146.1 3.3 all-to-all-start.5
  1149.5 4.8 reduce-scatter.33.cloned.1.call-done
  1155.7 58.0 %reduce-scatter.25.cloned.1.call-done = bf16[256,144]{0,1:T(8,128)(2,1)} async-done(((bf16[2048,144]{0,1:T(8,128)(2,1)}), bf16[256,144]{0,1:T(8,128)(2,1)}) %reduce-scatter.25.cloned.1.call-update) | async-done | bytes 73744 | tf_op jit(solution)/shard_map/reduce_scatter | solution.py:96
  1215.4 3.3 all-to-all-start.4
  1219.5 3.8 all-to-all-done.4
  1224.4 22.3 %reduce-scatter.21.cloned.1.call-done = bf16[128,2048]{1,0:T(8,128)(2,1)} async-done(((bf16[512,2048]{1,0:T(8,128)(2,1)}), bf16[128,2048]{1,0:T(8,128)(2,1)}) %reduce-scatter.21.cloned.1.call-update) | async-done | bytes 524304 | tf_op jit(solution)/shard_map/reduce_scatter | solution.py:96
  1248.2 41.6 %all-reduce.6 = (f32[2048]{0:T(1024)S(1)}, f32[512]{0:T(512)S(1)}, f32[2048]{0:T(1024)S(1)}) all-reduce(f32[2048]{0:T(1024)S(1)} %get-tuple-element.22, f32[512]{0:T(512)S(1)} %copy-done.75, f32[2048]{0:T(1024)S(1)} %copy-done.68), channel_id=7, replica_groups=mesh['expert'=8,'shard'=4] {'expert','shard'}, use_global_device_ids=true, to_apply=%region_31.32.clone | all-reduce | flops 4608 | bytes 36864
  1291.6 34.5 %reduce-scatter.23.cloned.1.call-done = bf16[256,768]{1,0:T(8,128)(2,1)} async-done(((bf16[2048,768]{1,0:T(8,128)(2,1)}), bf16[256,768]{1,0:T(8,128)(2,1)}) %reduce-scatter.23.cloned.1.call-update) | async-done | bytes 393232 | tf_op jit(solution)/shard_map/reduce_scatter | solution.py:96
  1326.1 3.5 all-to-all-start.3
  1329.5 180.2 %reduce-scatter.17.cloned.1.call-done = bf16[128,2048]{1,0:T(8,128)(2,1)} async-done(((bf16[4096,2048]{1,0:T(8,128)(2,1)}), bf16[128,2048]{1,0:T(8,128)(2,1)}) %reduce-scatter.17.cloned.1.call-update) | async-done | bytes 524304 | tf_op jit(solution)/shard_map/reduce_scatter | solution.py:96
  1509.8 3.1 fusion.35
  1514.0 149.7 %reduce-scatter.29.cloned.1.call-done = bf16[64,2048]{1,0:T(8,128)(2,1)} async-done(((bf16[2048,2048]{1,0:T(8,128)(2,1)}), bf16[64,2048]{1,0:T(8,128)(2,1)}) %reduce-scatter.29.cloned.1.call-update) | async-done | bytes 262160 | tf_op jit(solution)/shard_map/reduce_scatter | solution.py:96
  (367 shorter events, 84.7 us)
Async XLA Ops:
  7.2 70.8 %all-gather.10.cloned.1.call-start = ((), (), s32[]{:S(2)}) async-start(), calls=%async_computation.17 | async-start | bytes 2621440 | tf_op jit(solution)/shard_map/all_gather | solution.py:92
  8.0 92.2 %all-gather.12.cloned.1.call-start = ((), (), s32[]{:S(2)}) async-start(), calls=%async_computation.18 | async-start | bytes 2703360 | tf_op jit(solution)/shard_map/all_gather | solution.py:92
  8.7 132.6 %all-gather.14.cloned.1.call-start = ((), (), s32[]{:S(2)}) async-start(), calls=%async_computation.19 | async-start | bytes 1179648 | tf_op jit(solution)/shard_map/all_gather | solution.py:92
  18.6 184.1 %all-gather.16.cloned.1.call-start = ((), (), s32[]{:S(2)}) async-start(), calls=%async_computation.20 | async-start | bytes 3538944 | tf_op jit(solution)/shard_map/all_gather | solution.py:92
  35.1 246.4 %all-gather.18.cloned.1.call-start = ((), (), s32[]{:S(2)}) async-start(), calls=%async_computation.21 | async-start | bytes 8650752 | tf_op jit(solution)/shard_map/all_gather | solution.py:92
  35.6 280.2 %reduce-scatter.15.cloned.1.call-start = ((), (), s32[]{:S(2)}) async-start(), calls=%async_computation.22 | async-start | bytes 2621440 | tf_op jit(solution)/shard_map/reduce_scatter | solution.py:96
  77.1 64.3 %copy-start.66 = (f32[512]{0:T(512)}, f32[512]{0:T(512)S(1)}, u32[]{:S(2)}) copy-start(f32[512]{0:T(512)S(1)} %convert_element_type.180) | copy-start | bytes 6148
  77.1 125.5 %copy-start.62 = (f32[2048]{0:T(1024)}, f32[2048]{0:T(1024)S(1)}, u32[]{:S(2)}) copy-start(f32[2048]{0:T(1024)S(1)} %convert_element_type.178) | copy-start | bytes 24580
  104.0 42.8 %copy-start.21 = (f32[512,576]{0,1:T(8,128)}, f32[512,576]{0,1:T(8,128)S(1)}, u32[]{:S(2)}) copy-start(f32[512,576]{0,1:T(8,128)S(1)} %fusion.89) | copy-start | bytes 3538948
  105.3 36.1 %copy-start.76 = (f32[512]{0:T(512)}, f32[512]{0:T(512)S(1)}, u32[]{:S(2)}) copy-start(f32[512]{0:T(512)S(1)} %add_rsqrt_fusion) | copy-start | bytes 6148
  145.4 61.9 %copy-start.17 = (bf16[512,4,128]{2,1,0:T(4,128)(2,1)}, bf16[512,4,128]{2,1,0:T(4,128)(2,1)S(1)}, u32[]{:S(2)}) copy-start(bf16[512,4,128]{2,1,0:T(4,128)(2,1)S(1)} %get-tuple-element.63) | copy-start | bytes 1572868
  146.9 63.0 %copy-start.13 = (bf16[512,4,128]{0,2,1:T(8,128)(2,1)}, bf16[512,4,128]{0,2,1:T(8,128)(2,1)S(1)}, u32[]{:S(2)}) copy-start(bf16[512,4,128]{0,2,1:T(8,128)(2,1)S(1)} %copy.267) | copy-start | bytes 1572868
  148.5 58.6 %copy-start.39 = (f32[512,32]{0,1:T(8,128)}, f32[512,32]{0,1:T(8,128)S(1)}, u32[]{:S(2)}) copy-start(f32[512,32]{0,1:T(8,128)S(1)} %get-tuple-element.75) | copy-start | bytes 196612
  148.5 58.6 %copy-start.47 = (f32[512,32]{0,1:T(8,128)}, f32[512,32]{0,1:T(8,128)S(1)}, u32[]{:S(2)}) copy-start(f32[512,32]{0,1:T(8,128)S(1)} %get-tuple-element.72) | copy-start | bytes 196612
  148.5 59.4 %copy-start.48 = (bf16[512,32]{0,1:T(8,128)(2,1)}, bf16[512,32]{0,1:T(8,128)(2,1)S(1)}, u32[]{:S(2)}) copy-start(bf16[512,32]{0,1:T(8,128)(2,1)S(1)} %get-tuple-element.73) | copy-start | bytes 98308
  148.6 59.4 %copy-start.50 = (bf16[512,32]{0,1:T(8,128)(2,1)}, bf16[512,32]{0,1:T(8,128)(2,1)S(1)}, u32[]{:S(2)}) copy-start(bf16[512,32]{0,1:T(8,128)(2,1)S(1)} %get-tuple-element.74) | copy-start | bytes 98308
  212.7 107.0 %copy-start.24 = (bf16[4,128,512]{2,1,0:T(8,128)(2,1)}, bf16[4,128,512]{2,1,0:T(8,128)(2,1)S(1)}, u32[]{:S(2)}) copy-start(bf16[4,128,512]{2,1,0:T(8,128)(2,1)S(1)} %convolution_convert_fusion.8) | copy-start | bytes 1572868
  212.7 103.2 %copy-start.2 = (bf16[128,2048]{1,0:T(8,128)(2,1)S(1)}, bf16[128,2048]{1,0:T(8,128)(2,1)}, u32[]{:S(2)}) copy-start(bf16[128,2048]{1,0:T(8,128)(2,1)} %param.19) | copy-start | bytes 1572868
  281.5 39.1 %copy-start.43 = (bf16[64,2816]{1,0:T(8,128)(2,1)S(1)}, bf16[64,2816]{1,0:T(8,128)(2,1)}, u32[]{:S(2)}) copy-start(bf16[64,2816]{1,0:T(8,128)(2,1)} %param.29) | copy-start | bytes 1081348
  285.7 36.1 %copy-start.44 = (bf16[64,2816]{1,0:T(8,128)(2,1)S(1)}, bf16[64,2816]{1,0:T(8,128)(2,1)}, u32[]{:S(2)}) copy-start(bf16[64,2816]{1,0:T(8,128)(2,1)} %param.30) | copy-start | bytes 1081348
  285.7 168.0 %all-gather.20.cloned.1.call-start = ((), (), s32[]{:S(2)}) async-start(), calls=%async_computation.23 | async-start | bytes 17301504 | tf_op jit(solution)/shard_map/all_gather | solution.py:92
  286.1 38.6 %copy-start.53 = (f32[2048]{0:T(1024)}, f32[2048]{0:T(1024)S(1)}, u32[]{:S(2)}) copy-start(f32[2048]{0:T(1024)S(1)} %convert_element_type.190) | copy-start | bytes 24580
  319.8 250.5 %all-gather.22.cloned.1.call-start = ((), (), s32[]{:S(2)}) async-start(), calls=%async_computation.25 | async-start | bytes 17301504 | tf_op jit(solution)/shard_map/all_gather | solution.py:92
  324.7 69.1 %copy-start.60 = (s32[128,6]{0,1:T(8,128)S(1)}, s32[128,6]{0,1:T(8,128)}, u32[]{:S(2)}) copy-start(s32[128,6]{0,1:T(8,128)} %param.35) | copy-start | bytes 9220
  324.7 76.0 %all-to-all-start.2 = ((bf16[32,2,64,88]{3,2,1,0:T(8,128)(2,1)}), bf16[32,2,64,88]{3,2,1,0:T(8,128)(2,1)S(1)}, u32[]{:S(2)}, u32[]{:S(2)}) async-start(bf16[32,2,64,88]{3,2,1,0:T(8,128)(2,1)} %copy.224), calls=%async_computation.3 | async-start | bytes 2097152 | tf_op jit(solution)/shard_map/all_to_all | solution.py:253
  329.3 553.9 %reduce-scatter.19.cloned.1.call-start = ((), (), s32[]{:S(2)}) async-start(), calls=%async_computation.26 | async-start | bytes 18382848 | tf_op jit(solution)/shard_map/reduce_scatter | solution.py:96
  401.0 73.6 %copy-start.46 = (bf16[2048,88]{0,1:T(8,128)(2,1)}, bf16[2048,88]{0,1:T(8,128)(2,1)S(1)}, u32[]{:S(2)}) copy-start(bf16[2048,88]{0,1:T(8,128)(2,1)S(1)} %copy.225) | copy-start | bytes 1081348
  401.3 73.3 %copy-start.45 = (bf16[2048,88]{0,1:T(8,128)(2,1)}, bf16[2048,88]{0,1:T(8,128)(2,1)S(1)}, u32[]{:S(2)}) copy-start(bf16[2048,88]{0,1:T(8,128)(2,1)S(1)} %copy.226) | copy-start | bytes 1081348
  401.6 73.0 %copy-start.58 = (f32[128,6]{0,1:T(8,128)}, f32[128,6]{0,1:T(8,128)S(1)}, u32[]{:S(2)}) copy-start(f32[128,6]{0,1:T(8,128)S(1)} %get-tuple-element.25) | copy-start | bytes 9220
  690.7 193.3 %copy-start.61 = (s32[128,6]{0,1:T(8,128)S(1)}, s32[128,6]{0,1:T(8,128)}, u32[]{:S(2)}) copy-start(s32[128,6]{0,1:T(8,128)} %param.35) | copy-start | bytes 9220
  690.7 193.4 %copy-start.59 = (f32[128,6]{0,1:T(8,128)S(1)}, f32[128,6]{0,1:T(8,128)}, u32[]{:S(2)}) copy-start(f32[128,6]{0,1:T(8,128)} %copy-done.58) | copy-start | bytes 9220
  690.8 193.4 %copy-start.70 = (f32[128]{0:T(128)S(1)}, f32[128]{0:T(128)}, u32[]{:S(2)}) copy-start(f32[128]{0:T(128)} %copy-done.69) | copy-start | bytes 1540
  690.8 193.4 %copy-start.71 = (pred[128,6]{0,1:T(8,128)(4,1)S(1)}, pred[128,6]{0,1:T(8,128)(4,1)}, u32[]{:S(2)}) copy-start(pred[128,6]{0,1:T(8,128)(4,1)} %get-tuple-element.36) | copy-start | bytes 2308
  690.8 193.4 %copy-start.79 = (f32[128]{0:T(128)S(1)}, f32[128]{0:T(128)}, u32[]{:S(2)}) copy-start(f32[128]{0:T(128)} %copy-done.78) | copy-start | bytes 1540
  690.8 194.6 %copy-start.3 = (bf16[128,2048]{1,0:T(8,128)(2,1)S(1)}, bf16[128,2048]{1,0:T(8,128)(2,1)}, u32[]{:S(2)}) copy-start(bf16[128,2048]{1,0:T(8,128)(2,1)} %param.19) | copy-start | bytes 1572868
  690.8 194.6 %copy-start.5 = (bf16[128,2048]{1,0:T(8,128)(2,1)S(1)}, bf16[128,2048]{1,0:T(8,128)(2,1)}, u32[]{:S(2)}) copy-start(bf16[128,2048]{1,0:T(8,128)(2,1)} %reduce-scatter.15.cloned.1.call-done) | copy-start | bytes 1572868
  690.8 194.6 %copy-start.42 = (bf16[2048,16]{0,1:T(8,128)(2,1)S(1)}, bf16[2048,16]{0,1:T(8,128)(2,1)}, u32[]{:S(2)}) copy-start(bf16[2048,16]{0,1:T(8,128)(2,1)} %copy-done.41) | copy-start | bytes 196612
  690.8 194.6 %copy-start.54 = (f32[2048]{0:T(1024)S(1)}, f32[2048]{0:T(1024)}, u32[]{:S(2)}) copy-start(f32[2048]{0:T(1024)} %copy-done.53) | copy-start | bytes 24580
  690.8 194.6 %copy-start.73 = (f32[128]{0:T(128)S(1)}, f32[128]{0:T(128)}, u32[]{:S(2)}) copy-start(f32[128]{0:T(128)} %copy-done.72) | copy-start | bytes 1540
  690.8 196.7 %copy-start.15 = (bf16[128,2048]{1,0:T(8,128)(2,1)S(1)}, bf16[128,2048]{1,0:T(8,128)(2,1)}, u32[]{:S(2)}) copy-start(bf16[128,2048]{1,0:T(8,128)(2,1)} %param.20) | copy-start | bytes 1572868
  690.9 221.9 %all-gather.24.cloned.1.call-start = ((), (), s32[]{:S(2)}) async-start(), calls=%async_computation.27 | async-start | bytes 2621440 | tf_op jit(solution)/shard_map/all_gather | solution.py:92
  888.8 59.4 %reduce-scatter.31.cloned.1.call-start = ((), (), s32[]{:S(2)}) async-start(), calls=%async_computation.33 | async-start | bytes 819200
  925.6 220.5 %reduce-scatter.27.cloned.1.call-start = ((), (), s32[]{:S(2)}) async-start(), calls=%async_computation.31 | async-start | bytes 1179648 | tf_op jit(solution)/shard_map/reduce_scatter | solution.py:96
  929.0 225.3 %reduce-scatter.33.cloned.1.call-start = ((), (), s32[]{:S(2)}) async-start(), calls=%async_computation.34 | async-start | bytes 1081344
  930.5 283.3 %reduce-scatter.25.cloned.1.call-start = ((), (), s32[]{:S(2)}) async-start(), calls=%async_computation.30 | async-start | bytes 663552 | tf_op jit(solution)/shard_map/reduce_scatter | solution.py:96
  931.6 32.7 %copy-start.52 = (f32[512,32]{0,1:T(8,128)S(1)}, f32[512,32]{0,1:T(8,128)}, u32[]{:S(2)}) copy-start(f32[512,32]{0,1:T(8,128)} %get-tuple-element.71) | copy-start | bytes 196612
  964.2 282.5 %reduce-scatter.21.cloned.1.call-start = ((), (), s32[]{:S(2)}) async-start(), calls=%async_computation.28 | async-start | bytes 2621440 | tf_op jit(solution)/shard_map/reduce_scatter | solution.py:96
  972.7 353.4 %reduce-scatter.23.cloned.1.call-start = ((), (), s32[]{:S(2)}) async-start(), calls=%async_computation.29 | async-start | bytes 3538944 | tf_op jit(solution)/shard_map/reduce_scatter | solution.py:96
  978.0 531.8 %reduce-scatter.17.cloned.1.call-start = ((), (), s32[]{:S(2)}) async-start(), calls=%async_computation.24 | async-start | bytes 17301504 | tf_op jit(solution)/shard_map/reduce_scatter | solution.py:96
  1003.6 660.0 %reduce-scatter.29.cloned.1.call-start = ((), (), s32[]{:S(2)}) async-start(), calls=%async_computation.32 | async-start | bytes 8650752 | tf_op jit(solution)/shard_map/reduce_scatter | solution.py:96
  1081.7 55.5 %all-to-all-start.6 = ((f32[32,2,64,88]{3,2,1,0:T(8,128)}), f32[32,2,64,88]{3,2,1,0:T(8,128)S(1)}, u32[]{:S(2)}, u32[]{:S(2)}) async-start(f32[32,2,64,88]{3,2,1,0:T(8,128)} %copy.246), calls=%async_computation.14 | async-start | bytes 4194304 | tf_op jit(solution)/shard_map/all_to_all | solution.py:316
  1139.0 107.7 %copy-start.4 = (bf16[128,2048]{1,0:T(8,128)(2,1)S(1)}, bf16[128,2048]{1,0:T(8,128)(2,1)}, u32[]{:S(2)}) copy-start(bf16[128,2048]{1,0:T(8,128)(2,1)} %param.19) | copy-start | bytes 1572868
  1139.0 107.7 %copy-start.64 = (f32[2048]{0:T(1024)S(1)}, f32[2048]{0:T(1024)}, u32[]{:S(2)}) copy-start(f32[2048]{0:T(1024)} %copy-done.62) | copy-start | bytes 24580
  1140.4 107.8 %copy-start.68 = (f32[2048]{0:T(1024)S(1)}, f32[2048]{0:T(1024)}, u32[]{:S(2)}) copy-start(f32[2048]{0:T(1024)} %get-tuple-element.18) | copy-start | bytes 24580
  1140.4 107.8 %copy-start.75 = (f32[512]{0:T(512)S(1)}, f32[512]{0:T(512)}, u32[]{:S(2)}) copy-start(f32[512]{0:T(512)} %get-tuple-element.20) | copy-start | bytes 6148
  1140.4 369.3 %copy-start.6 = (bf16[128,2048]{1,0:T(8,128)(2,1)S(1)}, bf16[128,2048]{1,0:T(8,128)(2,1)}, u32[]{:S(2)}) copy-start(bf16[128,2048]{1,0:T(8,128)(2,1)} %reduce-scatter.15.cloned.1.call-done) | copy-start | bytes 1572868
  1140.4 369.3 %copy-start.8 = (f32[128,2048]{1,0:T(8,128)S(1)}, f32[128,2048]{1,0:T(8,128)}, u32[]{:S(2)}) copy-start(f32[128,2048]{1,0:T(8,128)} %copy-done.7) | copy-start | bytes 3145732
  1140.5 369.3 %copy-start.16 = (bf16[128,2048]{1,0:T(8,128)(2,1)S(1)}, bf16[128,2048]{1,0:T(8,128)(2,1)}, u32[]{:S(2)}) copy-start(bf16[128,2048]{1,0:T(8,128)(2,1)} %param.20) | copy-start | bytes 1572868
  1140.5 369.3 %copy-start.55 = (f32[2048]{0:T(1024)S(1)}, f32[2048]{0:T(1024)}, u32[]{:S(2)}) copy-start(f32[2048]{0:T(1024)} %copy-done.53) | copy-start | bytes 24580
  1140.5 369.3 %copy-start.74 = (f32[128]{0:T(128)S(1)}, f32[128]{0:T(128)}, u32[]{:S(2)}) copy-start(f32[128]{0:T(128)} %copy-done.72) | copy-start | bytes 1540
  1140.5 369.3 %copy-start.82 = (f32[128]{0:T(128)S(1)}, f32[128]{0:T(128)}, u32[]{:S(2)}) copy-start(f32[128]{0:T(128)} %copy-done.81) | copy-start | bytes 1540
  1146.1 69.3 %all-to-all-start.5 = ((bf16[4,16,1024]{2,1,0:T(8,128)(2,1)}), bf16[4,16,1024]{2,1,0:T(8,128)(2,1)S(1)}, u32[]{:S(2)}, u32[]{:S(2)}) async-start(bf16[4,16,1024]{2,1,0:T(8,128)(2,1)} %bitcast.187), calls=%async_computation.12 | async-start | bytes 262144 | tf_op jit(solution)/shard_map/all_to_all | solution.py:111
  1215.4 7.9 all-to-all-start.4
  1326.1 186.9 %all-to-all-start.3 = ((bf16[4,64,768]{2,1,0:T(8,128)(2,1)}), bf16[4,64,768]{2,1,0:T(8,128)(2,1)S(1)}, u32[]{:S(2)}, u32[]{:S(2)}) async-start(bf16[4,64,768]{2,1,0:T(8,128)(2,1)} %bitcast.185), calls=%async_computation.8 | async-start | bytes 786432 | tf_op jit(solution)/shard_map/all_to_all | solution.py:111
  (57 other events, 510.9 us)
Sparse Core Ops, SparseCore 0:
  9.6 29.4 all-gather.9
  42.0 58.1 all-gather.11
  102.3 39.0 all-gather.13
  143.4 59.1 all-gather.15
  205.3 76.0 all-gather.17
  285.8 29.9 reduce-scatter.14
  319.9 133.8 all-gather.19
  457.0 113.2 all-gather.21
  691.0 192.2 reduce-scatter.18
  888.9 23.7 all-gather.23
  925.7 22.4 reduce-scatter.30
  951.8 63.3 reduce-scatter.26
  1017.5 136.7 reduce-scatter.32
  1157.8 55.8 reduce-scatter.24
  1216.3 30.3 reduce-scatter.20
  1250.2 75.8 reduce-scatter.22
  1328.2 181.5 reduce-scatter.16
  1511.9 151.6 reduce-scatter.28

commit v2 on v1

--- a/solution.py
+++ b/solution.py
@@ -1,6 +1,10 @@
+import functools
+
 import jax
 import jax.numpy as jnp
 from jax import lax
+from jax.experimental import pallas as pl
+from jax.experimental.pallas import tpu as pltpu
 from jax.sharding import PartitionSpec as P
 
 HEADS = 16
@@ -96,22 +100,778 @@
     return lax.psum_scatter(value, axes, scatter_dimension=0, tiled=True)
 
 
-def columns_out(value):
-    count = lax.axis_size("shard")
+HBM = pl.BlockSpec(memory_space=pl.ANY)
+VMEM = pl.BlockSpec(memory_space=pltpu.VMEM)
+
+
+class Place:
+    def __init__(self):
+        e, s = lax.axis_index("expert"), lax.axis_index("shard")
+        self.z, self.y, self.x, self.c = e // 2, e % 2, s // 2, s % 2
+
+    def at(self, z=None, y=None, x=None, c=None):
+        z = self.z if z is None else z
+        y = self.y if y is None else y
+        x = self.x if x is None else x
+        c = self.c if c is None else c
+        return {"expert": 2 * z + y, "shard": 2 * x + c}
+
+
+def greet(partners):
+    barrier = pltpu.get_barrier_semaphore()
+    for partner in partners:
+        pl.semaphore_signal(
+            barrier, inc=1, device_id=partner, device_id_type=pl.DeviceIdType.MESH
+        )
+    pl.semaphore_wait(barrier, len(partners))
+
+
+def remote(src, dst, send, recv, where):
+    return pltpu.make_async_remote_copy(
+        src_ref=src,
+        dst_ref=dst,
+        send_sem=send,
+        recv_sem=recv,
+        device_id=where,
+        device_id_type=pl.DeviceIdType.MESH,
+    )
+
+
+def gather_all_kernel(lines, chunks, src, dst, own_sem, zs, zr, xs, xr, ys, yr, ds_, dr, cs, cr):
+    me = Place()
+    z, y, x, c = me.z, me.y, me.x, me.c
+    rows, width = src.shape
+    step_rows = rows // chunks
+    half = width // 256 * 128
+    others = [lax.rem(z + 1 + j, lines) for j in range(lines - 1)]
+    to_x, to_y, to_c = me.at(x=1 - x), me.at(y=1 - y), me.at(c=1 - c)
+    greet([me.at(z=o) for o in others] + [to_x, to_y, to_c])
+    cuts = (pl.ds(0, half), pl.ds(half, width - half))
+
+    def block(zz, yy, xx, k, cols=None, cc=None):
+        return dst.at[
+            zz, yy, xx, c if cc is None else cc,
+            pl.ds(k * step_rows, step_rows),
+            pl.ds(0, width) if cols is None else cuts[cols],
+        ]
+
+    own = pltpu.make_async_copy(src, dst.at[z, y, x, c], own_sem)
+    own.start()
+    pending = []
+
+    def go(copy):
+        copy.start()
+        pending.append(copy)
+        return copy
+
+    order = [None] + list(range(lines - 1))
+
+    def piece(k):
+        return src.at[pl.ds(k * step_rows, step_rows)]
+
+    def z_start(k):
+        for j, o in enumerate(others):
+            go(remote(piece(k), block(z, y, x, k), zs.at[k, j], zr.at[k, z], me.at(z=o)))
+        go(remote(piece(k), block(z, y, x, k), xs.at[k, lines - 1], xr.at[k, z], to_x))
+        go(remote(piece(k), block(z, y, x, k), ys.at[k, lines - 1], yr.at[k, z], to_y))
+
+    def z_land(k):
+        for j, o in reversed(list(enumerate(others))):
+            b = block(o, y, x, k)
+            remote(b, b, zs.at[k, j], zr.at[k, o], me.at(z=o)).wait_recv()
+            go(remote(b, b, xs.at[k, j], xr.at[k, o], to_x))
+            go(remote(b, b, ys.at[k, j], yr.at[k, o], to_y))
+
+    def core_send(k, slot, yy, xx):
+        b = dst.at[:, yy, xx, c, pl.ds(k * step_rows, step_rows)]
+        go(remote(b, b, cs.at[k, slot], cr.at[k, slot], to_c))
+
+    def xy_land(k):
+        for j, o in [(lines - 1, z)] + list(reversed(list(enumerate(others)))):
+            b = block(o, y, 1 - x, k)
+            remote(b, b, xs.at[k, j], xr.at[k, o], to_x).wait_recv()
+            b = block(o, y, 1 - x, k, 0)
+            go(remote(b, b, ds_.at[k, j, 0], dr.at[k, o, 0], to_y))
+            b = block(o, 1 - y, x, k)
+            remote(b, b, ys.at[k, j], yr.at[k, o], to_y).wait_recv()
+            b = block(o, 1 - y, x, k, 1)
+            go(remote(b, b, ds_.at[k, j, 1], dr.at[k, o, 1], to_x))
+        core_send(k, 1, y, 1 - x)
+        core_send(k, 2, 1 - y, x)
+
+    def diag_land(k):
+        for j, o in [(lines - 1, z)] + list(reversed(list(enumerate(others)))):
+            for h, w in ((0, to_y), (1, to_x)):
+                b = block(o, 1 - y, 1 - x, k, h)
+                remote(b, b, ds_.at[k, j, h], dr.at[k, o, h], w).wait_recv()
+        core_send(k, 3, 1 - y, 1 - x)
+
+    for step in range(chunks + 2):
+        if step < chunks:
+            z_start(step)
+        if step < chunks:
+            z_land(step)
+            if step == 0:
+                own.wait()
+            core_send(step, 0, y, x)
+        if 1 <= step <= chunks:
+            xy_land(step - 1)
+        if step >= 2:
+            diag_land(step - 2)
+    for k in range(chunks):
+        for slot, (yy, xx) in enumerate(((y, x), (y, 1 - x), (1 - y, x), (1 - y, 1 - x))):
+            b = dst.at[:, yy, xx, 1 - c, pl.ds(k * step_rows, step_rows)]
+            remote(b, b, cs.at[k, slot], cr.at[k, slot], to_c).wait_recv()
+    for copy in pending:
+        copy.wait_send()
+
+
+def gather_all(value, lines, ident, chunks=4):
     rows, width = value.shape
-    parts = value.reshape(rows, count, width // count).transpose(1, 0, 2)
-    return lax.all_to_all(parts, "shard", split_axis=0, concat_axis=0).reshape(
-        count * rows, width // count
-    )
-
-
-def columns_back(value):
-    count = lax.axis_size("shard")
+    dma = pltpu.SemaphoreType.DMA
+    out = pl.pallas_call(
+        functools.partial(gather_all_kernel, lines, chunks),
+        out_shape=jax.ShapeDtypeStruct((lines, 2, 2, 2, rows, width), value.dtype),
+        in_specs=[HBM],
+        out_specs=HBM,
+        scratch_shapes=[
+            dma,
+            dma((chunks, lines)), dma((chunks, lines)),
+            dma((chunks, lines)), dma((chunks, lines)),
+            dma((chunks, lines)), dma((chunks, lines)),
+            dma((chunks, lines, 2)), dma((chunks, lines, 2)),
+            dma((chunks, 4)), dma((chunks, 4)),
+        ],
+        compiler_params=pltpu.CompilerParams(collective_id=ident, has_side_effects=True),
+    )(value)
+    return out.reshape(lines * 8 * rows, width)
+
+
+def add_into(target, other, rows):
+    @pl.loop(0, rows // 16)
+    def _(i):
+        at = pl.ds(pl.multiple_of(i * 16, 16), 16)
+        target[at] = (target[at].astype(F32) + other[at].astype(F32)).astype(target.dtype)
+
+
+def sum_all_kernel(
+    lines, cuts, part, out, acc, cbuf, xbuf, ybuf, zbuf, xdiag, ydiag,
+    ls, cs, cr, xs, xr, ys, yr, zs, zr, xds, xdr, yds, ydr,
+):
+    me = Place()
+    z, y, x, c = me.z, me.y, me.x, me.c
+    rows, width = out.shape
+    cut = rows // cuts
+    half = width // 256 * 128
+    others = [lax.rem(z + 1 + j, lines) for j in range(lines - 1)]
+    to_x, to_y, to_c = me.at(x=1 - x), me.at(y=1 - y), me.at(c=1 - c)
+    greet([me.at(z=o) for o in others] + [to_x, to_y, to_c])
+    steps = [(o, k) for o in others + [z] for k in range(cuts)]
+    cols = (pl.ds(0, half), pl.ds(half, width - half))
+    sides = ((1 - y, 1 - x), (1 - y, x), (y, 1 - x), (y, x))
+    pending = []
+
+    def go(copy):
+        copy.start()
+        pending.append(copy)
+
+    def span(k):
+        return pl.ds(k * cut, cut)
+
+    def load(n, side):
+        o, k = steps[n]
+        yy, xx = sides[side]
+        return pltpu.make_async_copy(
+            part.at[o, yy, xx, c, span(k)], acc.at[o, yy, xx, span(k)], ls.at[n, side]
+        )
+
+    def to_core(n, side):
+        o, k = steps[n]
+        yy, xx = sides[side]
+        return remote(
+            part.at[o, yy, xx, 1 - c, span(k)],
+            cbuf.at[o, yy, xx, span(k)],
+            cs.at[n, side],
+            cr.at[n, side],
+            to_c,
+        )
+
+    def both_cores(n, side):
+        o, k = steps[n]
+        yy, xx = sides[side]
+        load(n, side).wait()
+        to_core(n, side).wait_recv()
+        add_into(acc.at[o, yy, xx, span(k)], cbuf.at[o, yy, xx, span(k)], cut)
+
+    def diag_sends(n):
+        o, k = steps[n]
+        block = acc.at[o, 1 - y, 1 - x, span(k)]
+        return (
+            remote(block.at[:, cols[0]], xdiag.at[o, span(k)], xds.at[n], xdr.at[n], to_x),
+            remote(block.at[:, cols[1]], ydiag.at[o, span(k)], yds.at[n], ydr.at[n], to_y),
+        )
+
+    def side_sends(n):
+        o, k = steps[n]
+        return (
+            remote(acc.at[o, y, 1 - x, span(k)], xbuf.at[o, span(k)], xs.at[n], xr.at[n], to_x),
+            remote(acc.at[o, 1 - y, x, span(k)], ybuf.at[o, span(k)], ys.at[n], yr.at[n], to_y),
+        )
+
+    def z_copy(n):
+        o, k = steps[n]
+        return remote(
+            acc.at[o, y, x, span(k)], zbuf.at[z, span(k)], zs.at[n], zr.at[z, k], me.at(z=o)
+        )
+
+    def first(n):
+        both_cores(n, 0)
+        for copy in diag_sends(n):
+            go(copy)
+
+    def second(n):
+        o, k = steps[n]
+        both_cores(n, 1)
+        both_cores(n, 2)
+        from_x, from_y = diag_sends(n)
+        from_x.wait_recv()
+        add_into(acc.at[o, 1 - y, x, span(k), cols[0]], xdiag.at[o, span(k)], cut)
+        from_y.wait_recv()
+        add_into(acc.at[o, y, 1 - x, span(k), cols[1]], ydiag.at[o, span(k)], cut)
+        for copy in side_sends(n):
+            go(copy)
+
+    def third(n):
+        o, k = steps[n]
+        both_cores(n, 3)
+        from_x, from_y = side_sends(n)
+        from_x.wait_recv()
+        from_y.wait_recv()
+        add_into(acc.at[o, y, x, span(k)], xbuf.at[o, span(k)], cut)
+        add_into(acc.at[o, y, x, span(k)], ybuf.at[o, span(k)], cut)
+        if n < (lines - 1) * cuts:
+            go(z_copy(n))
+
+    total = len(steps)
+    for n in range(total + 2):
+        for back, side_list in ((0, (0,)), (1, (1, 2)), (2, (3,))):
+            if 0 <= n - back < total:
+                for side in side_list:
+                    go(to_core(n - back, side))
+                    load(n - back, side).start()
+    for n in range(total + 2):
+        if n < total:
+            first(n)
+        if 0 <= n - 1 < total:
+            second(n - 1)
+        if 0 <= n - 2 < total:
+            third(n - 2)
+    for k in range(cuts):
+        for o in others:
+            block = zbuf.at[o, span(k)]
+            remote(block, block, zs.at[0], zr.at[o, k], me.at(z=o)).wait_recv()
+
+    @pl.loop(0, rows // 16)
+    def _(i):
+        at = pl.ds(pl.multiple_of(i * 16, 16), 16)
+        value = acc[z, y, x, at].astype(F32)
+        for o in others:
+            value = value + zbuf[o, at].astype(F32)
+        out[at] = value.astype(out.dtype)
+
+    for copy in pending:
+        copy.wait_send()
+
+
+def sum_all(part, lines, rows, ident, cuts=2):
+    width = part.shape[-1]
+    part = part.reshape(lines, 2, 2, 2, rows, width)
+    dma = pltpu.SemaphoreType.DMA
+    n = lines * cuts
+    buf = lambda *lead: pltpu.VMEM(lead + (rows, width), part.dtype)
+    half = width // 256 * 128
+    diag = lambda size: pltpu.VMEM((lines, rows, size), part.dtype)
+    return pl.pallas_call(
+        functools.partial(sum_all_kernel, lines, cuts),
+        out_shape=jax.ShapeDtypeStruct((rows, width), F32),
+        in_specs=[HBM],
+        out_specs=VMEM,
+        scratch_shapes=[
+            buf(lines, 2, 2), buf(lines, 2, 2), buf(lines), buf(lines), buf(lines),
+            diag(half), diag(width - half),
+            dma((n, 4)), dma((n, 4)), dma((n, 4)),
+            dma((n,)), dma((n,)), dma((n,)), dma((n,)), dma((n,)), dma((lines, cuts)),
+            dma((n,)), dma((n,)), dma((n,)), dma((n,)),
+        ],
+        compiler_params=pltpu.CompilerParams(
+            collective_id=ident, has_side_effects=True, vmem_limit_bytes=56 << 20
+        ),
+    )(part)
+
+
+def gather_group_kernel(cuts, src, dst, own_sem, send, recv):
+    me = Place()
+    x, c = me.x, me.c
+    to_x, to_c = me.at(x=1 - x), me.at(c=1 - c)
+    greet([to_x, to_c])
+    cut = src.shape[0] // cuts
+    span = lambda k: pl.ds(k * cut, cut)
+    own = pltpu.make_async_copy(src, dst.at[x, c], own_sem)
+    own.start()
+    over_x = [
+        remote(src.at[span(k)], dst.at[x, c, span(k)], send.at[0, k], recv.at[0, k], to_x)
+        for k in range(cuts)
+    ]
+    for copy in over_x:
+        copy.start()
+    over_c = remote(src, dst.at[x, c], send.at[1, 0], recv.at[1, 0], to_c)
+    over_c.start()
+    relays = []
+    for k in range(cuts):
+        far = dst.at[1 - x, c, span(k)]
+        remote(far, far, send.at[0, k], recv.at[0, k], to_x).wait_recv()
+        relays.append(remote(far, far, send.at[2, k], recv.at[2, k], to_c))
+        relays[-1].start()
+    far = dst.at[x, 1 - c]
+    remote(far, far, send.at[1, 0], recv.at[1, 0], to_c).wait_recv()
+    for k in range(cuts):
+        far = dst.at[1 - x, 1 - c, span(k)]
+        remote(far, far, send.at[2, k], recv.at[2, k], to_c).wait_recv()
+    own.wait()
+    for copy in over_x + [over_c] + relays:
+        copy.wait_send()
+
+
+def gather_group(value, ident, cuts=4):
     rows, width = value.shape
-    parts = lax.all_to_all(
-        value.reshape(count, rows // count, width), "shard", split_axis=0, concat_axis=0
-    )
-    return parts.transpose(1, 0, 2).reshape(rows // count, count * width)
+    dma = pltpu.SemaphoreType.DMA
+    out = pl.pallas_call(
+        functools.partial(gather_group_kernel, cuts),
+        out_shape=jax.ShapeDtypeStruct((2, 2, rows, width), value.dtype),
+        in_specs=[HBM],
+        out_specs=HBM,
+        scratch_shapes=[dma, dma((3, cuts)), dma((3, cuts))],
+        compiler_params=pltpu.CompilerParams(collective_id=ident, has_side_effects=True),
+    )(value)
+    return out.reshape(4 * rows, width)
+
+
+def sum_group_kernel(cuts, part, out, cbuf, xbuf, xsum, cs, cr, xs, xr):
+    me = Place()
+    x, c = me.x, me.c
+    rows, width = out.shape
+    cut = rows // cuts
+    to_x, to_c = me.at(x=1 - x), me.at(c=1 - c)
+    greet([to_x, to_c])
+    span = lambda k: pl.ds(k * cut, cut)
+    core = lambda k, far: remote(
+        part.at[1 - x if far else x, 1 - c, span(k)],
+        cbuf.at[far, span(k)],
+        cs.at[k, far],
+        cr.at[k, far],
+        to_c,
+    )
+    over = lambda k: remote(xsum.at[span(k)], xbuf.at[span(k)], xs.at[k], xr.at[k], to_x)
+    for k in range(cuts):
+        core(k, 1).start()
+    for k in range(cuts):
+        core(k, 0).start()
+
+    def add(k, target, one, two):
+        @pl.loop(0, cut // 16)
+        def _(i):
+            at = pl.ds(pl.multiple_of(k * cut + i * 16, 16), 16)
+            target[at] = (one[at].astype(F32) + two[at].astype(F32)).astype(target.dtype)
+
+    for k in range(cuts):
+        core(k, 1).wait_recv()
+        add(k, xsum, part.at[1 - x, c], cbuf.at[1])
+        over(k).start()
+    for k in range(cuts):
+        core(k, 0).wait_recv()
+        add(k, out, part.at[x, c], cbuf.at[0])
+    for k in range(cuts):
+        over(k).wait_recv()
+        add(k, out, out, xbuf)
+    for k in range(cuts):
+        core(k, 1).wait_send()
+        core(k, 0).wait_send()
+        over(k).wait_send()
+
+
+def sum_group(part, ident, cuts=4):
+    rows, width = part.shape[0] // 4, part.shape[1]
+    dma = pltpu.SemaphoreType.DMA
+    buf = lambda *lead: pltpu.VMEM(lead + (rows, width), part.dtype)
+    return pl.pallas_call(
+        functools.partial(sum_group_kernel, cuts),
+        out_shape=jax.ShapeDtypeStruct((rows, width), F32),
+        in_specs=[VMEM],
+        out_specs=VMEM,
+        scratch_shapes=[
+            buf(2), buf(), buf(),
+            dma((cuts, 2)), dma((cuts, 2)), dma((cuts,)), dma((cuts,)),
+        ],
+        compiler_params=pltpu.CompilerParams(
+            collective_id=ident, has_side_effects=True, vmem_limit_bytes=32 << 20
+        ),
+    )(part.reshape(2, 2, rows, width))
+
+
+def add_blocks(target, one, two):
+    if len(target.shape) > 2:
+        for i in range(target.shape[0]):
+            add_blocks(target.at[i], one.at[i], two.at[i])
+        return
+    rows = target.shape[0]
+    step = 16 if rows % 16 == 0 else rows
+
+    @pl.loop(0, rows // step)
+    def _(i):
+        at = pl.ds(pl.multiple_of(i * step, step), step)
+        target[at] = (one[at].astype(F32) + two[at].astype(F32)).astype(target.dtype)
+
+
+class Copies:
+    def __init__(self):
+        self.started = []
+
+    def go(self, copy):
+        copy.start()
+        self.started.append(copy)
+
+    def finish(self):
+        for copy in self.started:
+            copy.wait_send()
+
+
+def start_kernel(lines, with_o, *refs):
+    jobs = 3
+    tok, kva, *sources = refs[: 2 + jobs]
+    refs = refs[2 + jobs :]
+    if with_o:
+        o_src, refs = refs[0], refs[1:]
+    tok_dst, kva_dst, *dests = refs[: 2 + jobs]
+    refs = refs[2 + jobs :]
+    if with_o:
+        o_dst, refs = refs[0], refs[1:]
+    own_sem, gs, gr, zs, zr, ys, yr, ts, tr, ks, kr, kzs, kzr, kys, kyr = refs[:15]
+    if with_o:
+        o_own, ocs, ocr, ozs, ozr, oys, oyr = refs[15:]
+    me = Place()
+    z, y, x, c = me.z, me.y, me.x, me.c
+    others = [lax.rem(z + 1 + j, lines) for j in range(lines - 1)]
+    near = [(x, 1 - c), (1 - x, c), (1 - x, 1 - c)]
+    to_near = [me.at(x=xx, c=cc) for xx, cc in near]
+    to_y, to_x, to_c = me.at(y=1 - y), to_near[1], to_near[0]
+    greet([me.at(z=o) for o in others] + [to_y] + to_near)
+    copies = Copies()
+    go = copies.go
+
+    locals_ = [
+        pltpu.make_async_copy(src.at[x, c], dst.at[z, y, x, c], own_sem.at[i])
+        for i, (src, dst) in enumerate(zip(sources, dests))
+    ]
+    locals_.append(pltpu.make_async_copy(tok, tok_dst.at[x, c], own_sem.at[jobs]))
+    locals_.append(pltpu.make_async_copy(kva, kva_dst.at[z, y, x, c], own_sem.at[jobs + 1]))
+    for copy in locals_:
+        copy.start()
+    near_copy = lambda i, p: remote(
+        sources[i].at[near[p][0], near[p][1]],
+        dests[i].at[z, y, x, c],
+        gs.at[i, p],
+        gr.at[i, p],
+        to_near[p],
+    )
+    for i in range(jobs):
+        for p in range(3):
+            go(near_copy(i, p))
+    if with_o:
+        o_core = remote(o_src, o_dst.at[z, c], ocs, ocr, to_c)
+        o_local = pltpu.make_async_copy(o_src, o_dst.at[z, c], o_own)
+        holder = c == y
+
+        @pl.when(jnp.logical_not(holder))
+        def _():
+            o_core.start()
+
+        @pl.when(holder)
+        def _():
+            o_local.start()
+
+    kva_z = lambda j, o: remote(
+        kva, kva_dst.at[z, y, x, c], kzs.at[j], kzr.at[z], me.at(z=o)
+    )
+    for j, o in enumerate(others):
+        go(kva_z(j, o))
+    kva_y = lambda j, o, src: remote(src, kva_dst.at[o, y, x, c], kys.at[j], kyr.at[o], to_y)
+    go(kva_y(lines - 1, z, kva))
+    tok_copies = [
+        remote(tok, tok_dst.at[x, c], ts.at[p], tr.at[p], to_near[p]) for p in range(3)
+    ]
+    for copy in tok_copies:
+        go(copy)
+    line_y = lambda i, j, o: remote(
+        dests[i].at[o, y], dests[i].at[o, y], ys.at[i, j], yr.at[i, o], to_y
+    )
+    line_z = lambda i, j, o: remote(
+        dests[i].at[z, y], dests[i].at[z, y], zs.at[i, j], zr.at[i, z], me.at(z=o)
+    )
+    for i in range(jobs):
+        locals_[i].wait()
+        for p in range(3):
+            xx, cc = near[p]
+            block = dests[i].at[z, y, xx, cc]
+            remote(block, block, gs.at[i, p], gr.at[i, p], to_near[p]).wait_recv()
+        for j, o in enumerate(others):
+            go(line_z(i, j, o))
+        go(line_y(i, lines - 1, z))
+    if with_o:
+        o_z = lambda j, o: remote(o_dst.at[z], o_dst.at[z], ozs.at[j], ozr.at[z], me.at(z=o))
+        o_y = lambda j, o: remote(o_dst.at[o], o_dst.at[o], oys.at[j], oyr.at[o], to_y)
+
+        @pl.when(holder)
+        def _():
+            o_local.wait()
+            block = o_dst.at[z, 1 - c]
+            remote(block, block, ocs, ocr, to_c).wait_recv()
+            for j, o in enumerate(others):
+                o_z(j, o).start()
+            o_y(lines - 1, z).start()
+
+    for j, o in reversed(list(enumerate(others))):
+        block = kva_dst.at[o, y, x, c]
+        remote(block, block, kzs.at[j], kzr.at[o], me.at(z=o)).wait_recv()
+        go(kva_y(j, o, block))
+        for i in range(jobs):
+            block = dests[i].at[o, y]
+            remote(block, block, zs.at[i, j], zr.at[i, o], me.at(z=o)).wait_recv()
+            go(line_y(i, j, o))
+        if with_o:
+
+            @pl.when(holder)
+            def _(j=j, o=o):
+                block = o_dst.at[o]
+                remote(block, block, ozs.at[j], ozr.at[o], me.at(z=o)).wait_recv()
+                o_y(j, o).start()
+
+    for o in others + [z]:
+        block = kva_dst.at[o, 1 - y, x, c]
+        remote(block, block, kys.at[0], kyr.at[o], to_y).wait_recv()
+    locals_[jobs + 1].wait()
+    plane = kva_dst.at[:, :, x, c]
+    go(remote(plane, plane, ks.at[0], kr.at[0], to_x))
+    go(remote(plane, plane, ks.at[1], kr.at[1], to_c))
+    plane = kva_dst.at[:, :, 1 - x, c]
+    remote(plane, plane, ks.at[0], kr.at[0], to_x).wait_recv()
+    go(remote(plane, plane, ks.at[2], kr.at[2], to_c))
+    for p in range(3):
+        xx, cc = near[p]
+        block = tok_dst.at[xx, cc]
+        remote(block, block, ts.at[p], tr.at[p], to_near[p]).wait_recv()
+    locals_[jobs].wait()
+    for o in others + [z]:
+        for i in range(jobs):
+            block = dests[i].at[o, 1 - y]
+            remote(block, block, ys.at[i, 0], yr.at[i, o], to_y).wait_recv()
+    if with_o:
+
+        @pl.when(jnp.logical_not(holder))
+        def _():
+            for o in others + [z]:
+                remote(o_dst.at[o], o_dst.at[o], oys.at[0], oyr.at[o], to_y).wait_recv()
+            o_core.wait_send()
+
+        @pl.when(holder)
+        def _():
+            for j, o in list(enumerate(others)):
+                o_z(j, o).wait_send()
+                o_y(j, o).wait_send()
+            o_y(lines - 1, z).wait_send()
+
+    for slot, xx in ((1, x), (2, 1 - x)):
+        plane = kva_dst.at[:, :, xx, 1 - c]
+        remote(plane, plane, ks.at[slot], kr.at[slot], to_c).wait_recv()
+    copies.finish()
+
+
+def start_gather(tokens, kva, column_parts, o_rows, lines, ident):
+    jobs = len(column_parts)
+    with_o = o_rows is not None
+    inputs = [tokens, kva] + column_parts + ([o_rows] if with_o else [])
+    shape = lambda lead, v: jax.ShapeDtypeStruct(lead + v.shape, v.dtype)
+    outs = [shape((2, 2), tokens), shape((lines, 2, 2, 2), kva)]
+    outs += [jax.ShapeDtypeStruct((lines, 2) + v.shape, v.dtype) for v in column_parts]
+    if with_o:
+        outs.append(shape((lines, 2), o_rows))
+    dma = pltpu.SemaphoreType.DMA
+    scratch = [
+        dma((jobs + 2,)), dma((jobs, 3)), dma((jobs, 3)),
+        dma((jobs, lines)), dma((jobs, lines)), dma((jobs, lines)), dma((jobs, lines)),
+        dma((3,)), dma((3,)), dma((3,)), dma((3,)),
+        dma((lines,)), dma((lines,)), dma((lines,)), dma((lines,)),
+    ]
+    if with_o:
+        scratch += [dma, dma, dma, dma((lines,)), dma((lines,)), dma((lines,)), dma((lines,))]
+    return pl.pallas_call(
+        functools.partial(start_kernel, lines, with_o),
+        out_shape=outs,
+        in_specs=[HBM] * len(inputs),
+        out_specs=[HBM] * len(outs),
+        scratch_shapes=scratch,
+        compiler_params=pltpu.CompilerParams(collective_id=ident, has_side_effects=True),
+    )(*inputs)
+
+
+def grads_kernel(lines, kinds, with_o, *refs):
+    jobs = len(kinds)
+    take = lambda n: [refs.pop(0) for _ in range(n)]
+    refs = list(refs)
+    parts = take(jobs)
+    o_part = take(1)[0] if with_o else None
+    outs = take(jobs)
+    o_out = take(1)[0] if with_o else None
+    accs, ybufs, zbufs, tots = take(jobs), take(jobs), take(jobs), take(jobs)
+    if with_o:
+        o_acc, o_ybuf, o_zbuf, o_tot = take(4)
+    ys, yr, zs, zr, gs, gr = take(6)
+    if with_o:
+        oys, oyr, ozs, ozr, ocs, ocr = take(6)
+    me = Place()
+    z, y, x, c = me.z, me.y, me.x, me.c
+    others = [lax.rem(z + 1 + j, lines) for j in range(lines - 1)]
+    near = [(x, 1 - c), (1 - x, c), (1 - x, 1 - c)]
+    to_near = [me.at(x=xx, c=cc) for xx, cc in near]
+    to_y, to_c = me.at(y=1 - y), to_near[0]
+    greet([me.at(z=o) for o in others] + [to_y] + to_near)
+    copies = Copies()
+    go = copies.go
+    over_y = lambda i, j, o: remote(
+        parts[i].at[o, 1 - y], ybufs[i].at[o], ys.at[i, j], yr.at[i, o], to_y
+    )
+    over_z = lambda i, j, o: remote(
+        accs[i].at[o], zbufs[i].at[z], zs.at[i, j], zr.at[i, z], me.at(z=o)
+    )
+    places = list(enumerate(others)) + [(lines - 1, z)]
+    if with_o:
+        holder = c == y
+        o_over_y = lambda j, o: remote(o_part.at[o], o_ybuf.at[o], oys.at[j], oyr.at[o], to_y)
+        o_over_z = lambda j, o: remote(
+            o_acc.at[o], o_zbuf.at[z], ozs.at[j], ozr.at[z], me.at(z=o)
+        )
+    for j, o in places:
+        for i in range(jobs):
+            go(over_y(i, j, o))
+        if with_o:
+
+            @pl.when(jnp.logical_not(holder))
+            def _(j=j, o=o):
+                o_over_y(j, o).start()
+
+    for j, o in places:
+        for i in range(jobs):
+            remote(ybufs[i].at[o], ybufs[i].at[o], ys.at[i, j], yr.at[i, o], to_y).wait_recv()
+            add_blocks(accs[i].at[o], parts[i].at[o, y], ybufs[i].at[o])
+            if j < lines - 1:
+                go(over_z(i, j, o))
+        if with_o:
+
+            @pl.when(holder)
+            def _(j=j, o=o):
+                remote(o_ybuf.at[o], o_ybuf.at[o], oys.at[j], oyr.at[o], to_y).wait_recv()
+                add_blocks(o_acc.at[o], o_part.at[o], o_ybuf.at[o])
+                if j < lines - 1:
+                    o_over_z(j, o).start()
+
+    def line_sum(target, acc, zbuf):
+        if len(target.shape) > 2:
+            for k in range(target.shape[0]):
+                line_sum(target.at[k], acc.at[:, k], zbuf.at[:, k])
+            return
+        rows = target.shape[0]
+        step = 16 if rows % 16 == 0 else rows
+
+        @pl.loop(0, rows // step)
+        def _(i):
+            at = pl.ds(pl.multiple_of(i * step, step), step)
+            value = acc[z, at].astype(F32)
+            for o in others:
+                value = value + zbuf[o, at].astype(F32)
+            target[at] = value.astype(target.dtype)
+
+    near_copy = lambda i, p: remote(
+        tots[i].at[near[p][0], near[p][1]], outs[i].at[x, c], gs.at[i, p], gr.at[i, p], to_near[p]
+    )
+    for i in range(jobs):
+        for j, o in places[:-1]:
+            block = zbufs[i].at[o]
+            remote(block, block, zs.at[i, j], zr.at[i, o], me.at(z=o)).wait_recv()
+        if kinds[i]:
+            for xx in range(2):
+                for cc in range(2):
+                    line_sum(tots[i].at[xx, cc], accs[i].at[:, xx, cc], zbufs[i].at[:, xx, cc])
+            for p in range(3):
+                go(near_copy(i, p))
+            rows = tots[i].shape[2]
+            outs[i][x, c] = tots[i][x, c]
+        else:
+            line_sum(outs[i], accs[i], zbufs[i])
+    if with_o:
+        o_core = remote(o_tot.at[1 - c], o_out, ocs, ocr, to_c)
+
+        @pl.when(holder)
+        def _():
+            for j, o in places[:-1]:
+                block = o_zbuf.at[o]
+                remote(block, block, ozs.at[j], ozr.at[o], me.at(z=o)).wait_recv()
+            line_sum(o_tot.at[1 - c], o_acc.at[:, 1 - c], o_zbuf.at[:, 1 - c])
+            o_core.start()
+            line_sum(o_out, o_acc.at[:, c], o_zbuf.at[:, c])
+            for j, o in places[:-1]:
+                o_over_z(j, o).wait_send()
+            o_core.wait_send()
+
+        @pl.when(jnp.logical_not(holder))
+        def _():
+            for j, o in places:
+                o_over_y(j, o).wait_send()
+            o_core.wait_recv()
+
+    for i in range(jobs):
+        if kinds[i]:
+            for p in range(3):
+                block = outs[i].at[near[p][0], near[p][1]]
+                remote(block, block, gs.at[i, p], gr.at[i, p], to_near[p]).wait_recv()
+    copies.finish()
+
+
+def sum_grads(parts, kinds, o_part, lines, ident):
+    jobs = len(parts)
+    with_o = o_part is not None
+    inputs = list(parts) + ([o_part] if with_o else [])
+    outs = [jax.ShapeDtypeStruct(p.shape[2:], p.dtype) for p in parts]
+    if with_o:
+        outs.append(jax.ShapeDtypeStruct(o_part.shape[2:], o_part.dtype))
+    dma = pltpu.SemaphoreType.DMA
+    line = lambda p: pltpu.VMEM((lines,) + p.shape[2:], p.dtype)
+    scratch = [line(p) for p in parts] * 3
+    scratch += [pltpu.VMEM(p.shape[2:] if k else (8, 128), p.dtype) for p, k in zip(parts, kinds)]
+    if with_o:
+        scratch += [pltpu.VMEM(o_part.shape, o_part.dtype)] * 3
+        scratch += [pltpu.VMEM(o_part.shape[1:], o_part.dtype)]
+    scratch += [dma((jobs, lines))] * 4 + [dma((jobs, 3))] * 2
+    if with_o:
+        scratch += [dma((lines,))] * 4 + [dma, dma]
+    return pl.pallas_call(
+        functools.partial(grads_kernel, lines, tuple(kinds), with_o),
+        out_shape=outs,
+        in_specs=[VMEM] * len(inputs),
+        out_specs=[VMEM] * len(outs),
+        scratch_shapes=scratch,
+        compiler_params=pltpu.CompilerParams(
+            collective_id=ident, has_side_effects=True, vmem_limit_bytes=56 << 20
+        ),
+    )(*inputs)
 
 
 def ffn_chunk(rows, cots, gates, w_gate, w_up, w_down, widths):
@@ -188,15 +948,55 @@
     own_heads = HEADS // shard_count
     latent_width = kva_weight.shape[1]
 
-    q_mine = gather(columns_out(q_weight), "expert")
-    kvb_mine = gather(columns_out(kvb_weight), "expert")
-    kva_all = gather(kva_weight, BOTH)
-    o_all = gather(o_weight, BOTH)
-    o_mine = lax.dynamic_slice_in_dim(o_all, shard_at * own_heads * VDIM, own_heads * VDIM)
-    norm1_scale = gather(norm1_gain, BOTH).astype(F32)
-    latent_scale = gather(kv_gain, BOTH).astype(F32)
-    norm2_scale = gather(norm2_gain, BOTH).astype(F32)
-    router = gather(router_weight, BOTH)
+    lines = expert_count // 2
+    o_rows = o_weight.shape[0]
+    o_pairs = VDIM == 2 * o_rows
+
+    def by_head(weight):
+        rows = weight.shape[0]
+        heads = weight.reshape(rows, own_heads, 2, 2, weight.shape[1] // HEADS)
+        return heads.transpose(3, 2, 0, 1, 4).reshape(2, 2, rows, weight.shape[1] // 4)
+
+    small = [norm1_gain, norm2_gain, kv_gain, router_weight]
+    small_sizes = [v.size for v in small]
+
+    def pack(values):
+        flat = jnp.concatenate(values, axis=-1)
+        pad = -flat.shape[-1] % 2048
+        flat = jnp.pad(flat, [(0, 0)] * (flat.ndim - 1) + [(0, pad)])
+        return flat.reshape(flat.shape[:-1] + (-1, 128))
+
+    def unpack(packed):
+        flat = packed.reshape(packed.shape[:-2] + (-1,))
+        starts = [sum(small_sizes[:i]) for i in range(len(small_sizes))]
+        return [flat[..., b : b + n] for b, n in zip(starts, small_sizes)]
+
+    small_own = pack([v.reshape(-1) for v in small])
+    started = start_gather(
+        tokens,
+        kva_weight,
+        [
+            jnp.broadcast_to(small_own, (2, 2) + small_own.shape),
+            by_head(kvb_weight),
+            by_head(q_weight),
+        ],
+        o_weight if o_pairs else None,
+        lines,
+        1,
+    )
+    group_tokens = started[0].reshape(group_len, width)
+    kva_all = started[1].reshape(width, latent_width)
+    small_all = unpack(started[2].reshape((device_count,) + small_own.shape))
+    kvb_mine = started[3].reshape(KV_RANK, -1)
+    q_mine = started[4].reshape(width, -1)
+    core_at, x_at = shard_at % 2, shard_at // 2
+    if o_pairs:
+        o_mine = started[5].reshape(own_heads * VDIM, width)
+    else:
+        o_mine = gather(o_weight, BOTH).reshape(own_heads, 2, 2, VDIM, width)
+        o_mine = o_mine[:, core_at, x_at].reshape(own_heads * VDIM, width)
+    norm1_scale, norm2_scale, latent_scale = [v.reshape(-1).astype(F32) for v in small_all[:3]]
+    router = small_all[3].reshape(width, all_experts)
 
     positions = positions_of(seq_ids)
     cosine_table, sine_table = rope_tables(positions, ROPE)
@@ -205,7 +1005,7 @@
         (seq_ids[None, :] == 0) | (seq_ids[None, :] == seq_ids[:, None])
     )
     input_rows = tokens.astype(F32)
-    group_rows = gather(tokens, "shard").astype(F32)
+    group_rows = group_tokens.astype(F32)
     normed_group, _ = rms_forward(group_rows, norm1_scale)
     hidden_one = normed_group.astype(BF)
     query_raw = mm(hidden_one, q_mine).reshape(group_len, own_heads, NOPE + ROPE)
@@ -232,7 +1032,7 @@
         .astype(BF)
         .reshape(group_len, own_heads * VDIM)
     )
-    projected = scatter_sum(mm(attended, o_mine).astype(BF), "shard").astype(F32)
+    projected = sum_group(mm(attended, o_mine).astype(BF), 2)
     mixed = input_rows + projected
 
     normed_two, inverse_two = rms_forward(mixed, norm2_scale)
@@ -260,11 +1060,17 @@
     w_up = jnp.concatenate([expert_up[i] for i in range(local_experts)] + [both_shared[1]], 1)
     w_down = jnp.concatenate([expert_down[i] for i in range(local_experts)] + [shared_down], 0)
     def ffn(rows, cots, table):
-        rows_all = gather(rows, BOTH)
+        high = table.astype(BF)
+        low = (table - high.astype(F32)).astype(BF)
+        spare = jnp.zeros((table.shape[0], 128 - 2 * all_experts), BF)
         cots_all = gather(cots, BOTH)
-        gates_all = gather(table, BOTH)
+        all_values = gather_all(jnp.concatenate([rows, high, low, spare], axis=1), lines, 3)
+        rows_all = all_values[:, :width]
+        gates_all = all_values[:, width:].astype(F32)
         gates_mine = lax.dynamic_slice_in_dim(
             gates_all, expert_at * local_experts, local_experts, 1
+        ) + lax.dynamic_slice_in_dim(
+            gates_all, all_experts + expert_at * local_experts, local_experts, 1
         )
         out_part, back_part, gate_grads, *weight_grads = ffn_chunk(
             rows_all, cots_all, gates_mine, w_gate, w_up, w_down, widths
@@ -274,7 +1080,9 @@
             jnp.tile(gate_grads, (1, 128 // local_experts)),
             0.0,
         ).astype(BF)
-        back_sum = scatter_sum(jnp.concatenate([back_part, gate_grad_table], axis=1), BOTH)
+        back_sum = sum_all(
+            jnp.concatenate([back_part, gate_grad_table], axis=1), lines, rows.shape[0], 4
+        )
         return scatter_sum(out_part, BOTH), back_sum, weight_grads
 
     rounds = max(1, tok_rows * device_count // 4096)
@@ -313,8 +1121,8 @@
         .reshape(2, device_count, width // device_count, shared_width)
         .transpose(1, 0, 2, 3)
     )
-    shared_grads = lax.all_to_all(shared_grads, BOTH, split_axis=0, concat_axis=0)
-    shared_grads = shared_grads.transpose(1, 2, 0, 3).reshape(
+    shared_grads = lax.all_to_all(shared_grads.astype(BF), BOTH, split_axis=0, concat_axis=0)
+    shared_grads = shared_grads.astype(F32).transpose(1, 2, 0, 3).reshape(
         2, width // device_count, device_count * shared_width
     )
 
@@ -329,7 +1137,7 @@
     mixed_norm_grad, norm2_part = rms_backward(mixed, inverse_two, norm2_scale, hidden_two_grad)
     mixed_grad = upstream + mixed_norm_grad
 
-    mixed_grad_group = gather(mixed_grad.astype(BF), "shard")
+    mixed_grad_group = gather_group(mixed_grad.astype(BF), 5)
     o_part = mm_tn(attended, mixed_grad_group)
     attended_grad = (
         mm_nt(mixed_grad_group, o_mine).astype(BF).reshape(group_len, own_heads, VDIM)
@@ -358,7 +1166,9 @@
     )
     kvb_part = mm_tn(latent, keyval_grad)
     latent_part = jnp.concatenate([mm_nt(keyval_grad, kvb_mine), rope_grad], axis=1).astype(BF)
-    latent_sum = scatter_sum(latent_part, "shard").astype(F32)
+    latent_sum = sum_group(
+        jnp.pad(latent_part, ((0, 0), (0, -latent_part.shape[1] % 128))), 6
+    )[:, :latent_width]
     own_start = shard_at * tok_rows
     own_rows = lambda value: lax.dynamic_slice_in_dim(value, own_start, tok_rows)
     latent_raw_grad, kv_gain_part = rms_backward(
@@ -374,38 +1184,61 @@
         ],
         axis=1,
     ).astype(BF)
-    compressed_grad_group = gather(compressed_grad, "shard")
-    kva_columns = latent_width // shard_count
-    compressed_mine = lax.dynamic_slice_in_dim(
-        compressed_grad_group, shard_at * kva_columns, kva_columns, 1
-    )
-    kva_mine = lax.dynamic_slice_in_dim(kva_all, shard_at * kva_columns, kva_columns, 1)
+    compressed_grad_group = gather_group(
+        jnp.pad(compressed_grad, ((0, 0), (0, -latent_width % 128))), 7
+    )[:, :latent_width]
     query_grad = jnp.concatenate(
         [q_nope_grad, rotate(q_rope_grad, cosine_table[:, None, :], -sine_table[:, None, :])],
         axis=-1,
     )
     query_grad = query_grad.reshape(group_len, own_heads * (NOPE + ROPE)).astype(BF)
     q_part = mm_tn(hidden_one, query_grad)
-    kva_part = mm_tn(hidden_one, compressed_mine)
-    hidden_one_part = mm_nt(query_grad, q_mine) + mm_nt(compressed_mine, kva_mine)
-    hidden_one_grad = scatter_sum(hidden_one_part.astype(BF), "shard").astype(F32)
+    own_columns = lax.dynamic_index_in_dim(
+        hidden_one.reshape(group_len, expert_count, shard_count, width // device_count),
+        shard_at,
+        2,
+        keepdims=False,
+    ).reshape(group_len, width // shard_count)
+    kva_part = mm_tn(own_columns, compressed_grad_group)
+    hidden_one_grad = sum_group(mm_nt(query_grad, q_mine).astype(BF), 8) + mm_nt(
+        compressed_grad, kva_all
+    )
     _, inverse_one = rms_forward(input_rows, norm1_scale)
     input_norm_grad, norm1_part = rms_backward(
         input_rows, inverse_one, norm1_scale, hidden_one_grad
     )
     tokens_grad = mixed_grad + input_norm_grad
 
-    q_grad = columns_back(scatter_sum(q_part.astype(BF), "expert")).astype(F32)
-    kva_grad = columns_back(scatter_sum(kva_part.astype(BF), "expert")).astype(F32)
-    kvb_grad = columns_back(scatter_sum(kvb_part.astype(BF), "expert")).astype(F32)
-    o_wide = lax.dynamic_update_slice_in_dim(
-        jnp.zeros(o_all.shape, BF), o_part.astype(BF), shard_at * own_heads * VDIM, 0
-    )
-    o_grad = scatter_sum(o_wide, BOTH).astype(F32)
-    router_grad = scatter_sum(router_part, BOTH)
-    norm1_grad = scatter_sum(norm1_part, BOTH)
-    norm2_grad = scatter_sum(norm2_part, BOTH)
-    kv_gain_grad = scatter_sum(kv_gain_part, BOTH)
+    def from_heads(parts):
+        rows = parts.shape[2]
+        heads = parts.reshape(2, 2, rows, own_heads, -1).transpose(2, 3, 1, 0, 4)
+        return heads.reshape(rows, -1).astype(F32)
+
+    line_shape = (lines, 2)
+    small_parts = pack(
+        [v.reshape(device_count, -1) for v in (norm1_part, norm2_part, kv_gain_part, router_part)]
+    )
+    parts = [
+        kvb_part.astype(BF).reshape(line_shape + (2, 2, kvb_weight.shape[0], -1)),
+        kva_part.astype(BF).reshape(line_shape + (width // device_count, latent_width)),
+        q_part.astype(BF).reshape(line_shape + (2, 2, q_weight.shape[0], q_mine.shape[1])),
+        small_parts.reshape(line_shape + (2, 2) + small_parts.shape[1:]),
+    ]
+    o_part = o_part.astype(BF).reshape(own_heads, VDIM, width)
+    if o_pairs:
+        o_sum = o_part.reshape(own_heads, 2, o_rows, width)
+    else:
+        o_sum = None
+        o_wide = jnp.zeros((own_heads, 2, 2, VDIM, width), BF).at[:, core_at, x_at].set(o_part)
+        o_grad = scatter_sum(o_wide.reshape(HEADS * VDIM, width), BOTH).astype(F32)
+    summed = sum_grads(parts, (True, False, True, True), o_sum, lines, 9)
+    kvb_grad = from_heads(summed[0])
+    kva_grad = summed[1].astype(F32)
+    q_grad = from_heads(summed[2])
+    norm1_grad, norm2_grad, kv_gain_grad, router_grad = unpack(jnp.sum(summed[3], axis=(0, 1)))
+    router_grad = router_grad.reshape(router_weight.shape)
+    if o_pairs:
+        o_grad = summed[4].astype(F32)
     return (
         output,
         tokens_grad,

time: 1680 us -> 1040 us (0.62)
  waiting for transfers between devices: 1020 us -> 0.71 us
  Pallas kernels: 0 us -> 536 us
  blocking collectives: 213 us -> 0 us
  local copies, waits for them, and re-layouts: 76 us -> 133 us
    reduce_scatter x8 -> x1, waiting for transfers between devices: 667 us -> 0.01 us  [scatter_sum(): return lax.psum_scatter(value, axes, scatter_dimension=0, tiled=True)]
    pallas_call x0 -> x9, Pallas kernels: none -> 536 us  [the longest x1 192 us: start_gather(): pl.pallas_call(functools.partial(start_kernel, lines, with_o), out_shape=...]
    all_gather x8 -> x1, waiting for transfers between devices: 289 us -> 0.01 us  [gather(): return lax.all_gather(value, axes, axis=0, tiled=True)]
    all_gather x3 -> x0, blocking collectives: 107 us -> none  [gather(): return lax.all_gather(value, axes, axis=0, tiled=True)]
    unnamed x2 -> x0, blocking collectives: 82 us -> none
    all_to_all x4 -> x1, waiting for transfers between devices: 40 us -> 0.01 us  [on_device(): lax.all_to_all(shared_grads.astype(BF), BOTH, split_axis=0, concat_axis=0)]
    concatenate x0 -> x4, local copies, waits for them, and re-layouts: none -> 25 us  [the longest x1 22.2 us: ffn(): jnp.concatenate([back_part, gate_grad_table], axis=1)]
    all_to_all x2 -> x0, blocking collectives: 23.8 us -> none  [columns_out(): lax.all_to_all(parts, 'shard', split_axis=0, concat_axis=0)]
  transfers between devices with their start and end apart: 23 -> 4, of which waited for: 18 -> 0; matrix products, arithmetic and copies ran while one was open for 15% -> 35% of each run, Pallas kernels for 0% -> 52%
where the time goes in v2:
time: 1040 us; the launch traced here: 1020 us
  Pallas kernels  536 us (52%)
  matrix products  267 us (26%)
  local copies, waits for them, and re-layouts  133 us (13%)
  other arithmetic  56.5 us (5%)
  between operations  16.2 us (2%)
  starting transfers between devices  14.9 us (1%)
    pallas_call x1, Pallas kernels, start_gather(): pl.pallas_call(functools.partial(start_kernel, lines, with_o), out_shape=...  192 us
    pallas_call x1, Pallas kernels, gather_all(): pl.pallas_call(functools.partial(gather_all_kernel, lines, chunks), out_s...  102 us
    dot_general x8, matrix products, mm_nt(): lax.dot_general(a, b, (((1,), (1,)), ((), ())), preferred_element_type=F32)  100 us
    pallas_call x1, Pallas kernels, sum_grads(): pl.pallas_call(functools.partial(grads_kernel, lines, tuple(kinds), with_...  91.3 us
    pallas_call x1, Pallas kernels, sum_all(): pl.pallas_call(functools.partial(sum_all_kernel, lines, cuts), out_shape=...  84.4 us
    dot_general x8, matrix products, mm(): return jnp.dot(a, b, preferred_element_type=F32)  83.2 us
    dot_general x8, matrix products, mm_tn(): lax.dot_general(a, b, (((0,), (0,)), ((), ())), preferred_element_type=F32)  75.3 us
    pallas_call x3, Pallas kernels, sum_group(): pl.pallas_call(functools.partial(sum_group_kernel, cuts), out_shape=jax.S...  38.9 us
  transfers between devices with their start and end apart: 4, of which 0 were waited for; matrix products, arithmetic and copies ran while one was open for 35% of the time, Pallas kernels for 52%

profile of v2, /device:TPU:0, one launch (start us, length us, event | category | flops | bytes accessed | tf_op | source)
XLA Modules:
  0.0 1023.8 jit_solution(5503153421366153035)
XLA Ops:
  7.9 2.2 stack.54
  10.2 2.3 stack.55
  14.1 7.4 all-to-all-start
  25.5 192.1 %shard_map.306 = (bf16[2,2,128,2048]{3,2,1,0:T(8,128)(2,1)}, bf16[4,2,2,2,64,576]{5,4,3,2,1,0:T(8,128)(2,1)}, bf16[4,2,2,2,16,128]{5,4,3,2,1,0:T(8,128)(2,1)}, b...) custom-call(bf16[128,2048]{1,0:T(8,128)(2,1)} %refs_0_.1, ...), custom_call_target="tpu_custom_call" | custom-call | tf_op jit(solution)/shard_map/pallas_call | solution.py:716
  220.6 2.2 multiply_reduce_fusion.1
  223.4 1.8 fusion.81
  225.3 2.0 fusion.42
  228.6 3.0 convolution_convert_fusion.6
  231.6 2.6 reshape.627
  236.1 4.8 copy.286
  241.2 4.3 fusion.82
  252.5 15.7 %shard_map.307 = f32[128,2048]{1,0:T(8,128)S(1)} custom-call(bf16[2,2,128,2048]{3,2,1,0:T(8,128)(2,1)S(1)} %bitcast.194), custom_call_target="tpu_custom_call" | custom-call | tf_op jit(solution)/shard_map/pallas_call | solution.py:506
  271.9 3.7 slice_bitcast_fusion.11
  275.6 3.8 slice_bitcast_fusion.9
  279.5 1.9 slice_bitcast_fusion.7
  282.8 102.5 %shard_map.308 = bf16[4,2,2,2,128,2176]{5,4,3,2,1,0:T(8,128)(2,1)} custom-call(bf16[128,2176]{1,0:T(8,128)(2,1)} %concatenate.53.src), custom_call_target="tpu_custom_call" | custom-call | tf_op jit(solution)/shard_map/pallas_call | solution.py:232
  389.1 20.9 %fusion.7 = f32[4096,792]{0,1:T(8,128)} fusion(bf16[4096,2176]{1,0:T(8,128)(2,1)} %bitcast.197, bf16[2048,88]{0,1:T(8,128)(2,1)S(1)} %copy.301, bf16[2048,352]{0,1:T(8,128)(2,1)} %get-tuple-element.161, bf16[2048,352]{0,1:T(8,128)(2,1)} %get-tuple-element.160), kind=kOutput, calls=%fused_computation.17 | convolution fusion | flops 13297287168 | bytes 32997376 | tf_op jit(solution)/shard_map/dot_general | solution.py:84
  410.1 20.5 %fusion.9 = f32[4096,792]{0,1:T(8,128)} fusion(bf16[4096,2176]{1,0:T(8,128)(2,1)} %bitcast.198, bf16[2048,88]{0,1:T(8,128)(2,1)S(1)} %copy.300, bf16[2048,352]{0,1:T(8,128)(2,1)S(1)} %copy-done.37, bf16[2048,352]{0,1:T(8,128)(2,1)S(1)} %copy-done.35), kind=kOutput, calls=%fused_computation.19 | convolution fusion | flops 13297287168 | bytes 32997376 | tf_op jit(solution)/shard_map/dot_general | solution.py:84
  430.6 3.2 broadcast_in_dim.48
  433.8 3.2 broadcast_in_dim.46
  437.0 39.0 %convert_multiply_fusion = (f32[4096,792]{0,1:T(8,128)}, bf16[4096,792]{0,1:T(8,128)(2,1)}, bf16[4096,792]{0,1:T(8,128)(2,1)}, bf16[4096,792]{0,1:T(8,128)(2,1)}) fusion(f32[4096,792]{0,1:T(8,128)} %fusion.7, f32[4096,792]{0,1:T(8,128)} %fusion.9, f32[792]{0:T(1024)S(1)} %pad.47.clone, f32[4096,352]{0,1:T(8,128)} %broadcast_in_dim.48, ...), kind=kOutput, calls=%fused_computation.2 | convolution fusion | flops 13362167808 | bytes 89951328 | tf_op jit(solution)/shard_map/dot_general | solution.py:88
  476.0 31.1 %convolution_convert_fusion = bf16[4096,2048]{1,0:T(8,128)(2,1)} fusion(bf16[88,2048]{1,0:T(8,128)(2,1)S(1)} %copy-done.100, bf16[352,2048]{1,0:T(8,128)(2,1)S(1)} %copy-done.39, bf16[352,2048]{1,0:T(8,128)(2,1)S(1)} %copy-done.38, bf16[4096,792]{0,1:T(8,128)(2,1)} %get-tuple-element.145, f32[4096,352]{0,1:T(8,128)} %broadcast_in_dim.48, ...), kind=kOutput, calls=%fused_computation.4 | convolution fusion | flops 13321895936 | bytes 38046816 | tf_op jit(solution)/shard_map/dot_general | solution.py:84
  508.7 4.2 copy.316
  514.8 6.6 reshape.654
  522.2 2.2 fusion.34
  524.3 24.9 %fusion.71 = f32[792,2048]{1,0:T(8,128)} fusion(bf16[4096,2048]{1,0:T(8,128)(2,1)} %all-gather.2.cloned.1.call-done, bf16[4096,792]{0,1:T(8,128)(2,1)} %get-tuple-element.145, f32[4096,352]{0,1:T(8,128)} %broadcast_in_dim.48, f32[4096,352]{0,1:T(8,128)} %broadcast_in_dim.46, f32[792]{0:T(1024)S(1)} %pad.47.clone), kind=kOutput, calls=%fused_computation.208 | convolution fusion | flops 13303775232 | bytes 41290848 | tf_op jit(solution)/shard_map/dot_general | solution.py:92
  549.2 2.0 slice.255
  551.3 5.0 slice_reduce_fusion.1
  557.8 18.3 %fusion.3 = f32[2048,792]{0,1:T(8,128)S(1)} fusion(bf16[4096,792]{0,1:T(8,128)(2,1)} %get-tuple-element.151, bf16[4096,2176]{1,0:T(8,128)(2,1)} %bitcast.199), kind=kOutput, calls=%fused_computation.13 | convolution fusion | flops 13287555072 | bytes 29753344 | tf_op jit(solution)/shard_map/dot_general | solution.py:92
  576.1 2.7 copy-done.15
  579.2 18.3 %fusion.5 = f32[2048,792]{0,1:T(8,128)S(1)} fusion(bf16[4096,792]{0,1:T(8,128)(2,1)} %get-tuple-element.150, bf16[4096,2176]{1,0:T(8,128)(2,1)} %bitcast.200), kind=kOutput, calls=%fused_computation.15 | convolution fusion | flops 13287555072 | bytes 29753344 | tf_op jit(solution)/shard_map/dot_general | solution.py:92
  597.5 2.8 copy-done.14
  602.0 7.4 all-to-all-start.1
  609.7 23.6 %fusion.19 = f32[4096,2048]{0,1:T(8,128)} fusion(bf16[4096,792]{0,1:T(8,128)(2,1)} %get-tuple-element.150, bf16[2048,88]{0,1:T(8,128)(2,1)S(1)} %copy-done.61, bf16[2048,352]{0,1:T(8,128)(2,1)} %get-tuple-element.159, bf16[2048,352]{0,1:T(8,128)(2,1)S(1)} %copy-done.36), kind=kOutput, calls=%fused_computation.74 | convolution fusion | flops 13297287168 | bytes 43286528 | tf_op jit(solution)/shard_map/dot_general | solution.py:88
  633.3 26.3 %add_convert_fusion = bf16[4096,2048]{0,1:T(8,128)(2,1)} fusion(f32[4096,2048]{0,1:T(8,128)} %fusion.19, bf16[4096,792]{0,1:T(8,128)(2,1)} %get-tuple-element.151, bf16[2048,88]{0,1:T(8,128)(2,1)S(1)} %copy-done.59, bf16[2048,352]{0,1:T(8,128)(2,1)S(1)} %copy-done.34, bf16[2048,352]{0,1:T(8,128)(2,1)S(1)} %copy-done.33), kind=kOutput, calls=%fused_computation | convolution fusion | flops 13314064384 | bytes 60063744 | tf_op jit(solution)/shard_map/dot_general | solution.py:88
  659.6 14.3 %pad_maximum_fusion = bf16[4096,2176]{0,1:T(8,128)(2,1)} fusion(bf16[4096,128]{0,1:T(8,128)(2,1)S(1)} %select_convert_fusion, bf16[4096,2048]{0,1:T(8,128)(2,1)} %add_convert_fusion), kind=kLoop, calls=%fused_computation.1 | loop fusion | flops 35651584 | bytes 35651584 | tf_op jit(solution)/shard_map/concatenate | solution.py:1084
  673.9 22.2 %copy.303 = bf16[4096,2176]{1,0:T(8,128)(2,1)} copy(bf16[4096,2176]{0,1:T(8,128)(2,1)} %pad_maximum_fusion) | data formatting | bytes 35651584 | tf_op jit(solution)/shard_map/concatenate | solution.py:1084
  696.2 84.4 %shard_map.309 = f32[128,2176]{1,0:T(8,128)} custom-call(bf16[4,2,2,2,128,2176]{5,4,3,2,1,0:T(8,128)(2,1)} %bitcast.195), custom_call_target="tpu_custom_call" | custom-call | tf_op jit(solution)/shard_map/pallas_call | solution.py:394
  781.8 1.8 multiply_reduce_fusion.2
  785.6 1.8 reshape.649
  788.0 2.2 fusion.70.src
  790.1 18.7 %shard_map.310 = bf16[2,2,128,2048]{3,2,1,0:T(8,128)(2,1)} custom-call(bf16[128,2048]{1,0:T(8,128)(2,1)} %fusion.70.src), custom_call_target="tpu_custom_call" | custom-call | tf_op jit(solution)/shard_map/pallas_call | solution.py:448
  808.9 3.7 convolution_convert_fusion.8
  816.7 1.8 convolution_convert_fusion.3
  818.6 15.1 %shard_map.311 = f32[128,2048]{1,0:T(8,128)S(1)} custom-call(bf16[2,2,128,2048]{3,2,1,0:T(8,128)(2,1)S(1)} %bitcast.193), custom_call_target="tpu_custom_call" | custom-call | tf_op jit(solution)/shard_map/pallas_call | solution.py:506
  837.6 8.1 shard_map.312
  850.3 3.7 fusion.31
  860.0 7.9 shard_map.313
  868.0 2.6 convolution_convert_fusion.7
  870.6 2.1 copy.317
  872.7 1.9 convolution_convert_fusion.5
  874.6 4.5 convolution_convert_fusion.2
  879.1 3.5 convolution_convert_fusion.1
  882.6 91.3 %shard_map.314 = (bf16[2,2,16,1024]{3,2,1,0:T(8,128)(2,1)}, bf16[64,576]{1,0:T(8,128)(2,1)}, bf16[2,2,64,768]{3,2,1,0:T(8,128)(2,1)}, f32[2,2,16,128]{3,2,1,0:T(8,128)}, bf16[64,2048]{1,0:T(8,128)(2,1)}) custom-call(bf16[4,2,2,2,16,1024]{5,4,3,2,1,0:T(8,128)(2,1)} %bitcast.205, bf16[4,2,64,576]{3,2,1,0:T(8,128)(2,1)} %bitcast.213, ...), custom_call_target="tpu_custom_call" | custom-call | tf_op jit(solution)/shard_map/pallas_call | solution.py:865
  979.7 1.8 convert_element_type.318
  981.5 1.8 reshape.658
  984.1 1.9 reshape.656
  986.6 3.2 slice_bitcast_fusion.1
  989.8 3.3 pad_maximum_fusion.3
  996.2 4.8 pad_maximum_fusion.1
  1005.3 2.7 squeeze.45
  1008.0 2.8 copy.324
  1010.8 2.7 squeeze.44
  1013.5 3.0 fusion.30
  (361 shorter events, 73.3 us)
Async XLA Ops:
  7.2 14.5 %copy-start.93 = (bf16[64,16]{0,1:T(8,128)(2,1)S(1)}, bf16[64,16]{0,1:T(8,128)(2,1)}, u32[]{:S(2)}) copy-start(bf16[64,16]{0,1:T(8,128)(2,1)} %param.28) | copy-start | bytes 6148
  7.2 14.7 %copy-start.71 = (bf16[16,4096]{1,0:T(8,128)(2,1)S(1)}, bf16[16,4096]{1,0:T(8,128)(2,1)}, u32[]{:S(2)}) copy-start(bf16[16,4096]{1,0:T(8,128)(2,1)} %param.25) | copy-start | bytes 393220
  7.2 423.4 %all-gather.2.cloned.1.call-start = ((), (), s32[]{:S(2)}) async-start(), calls=%async_computation.4 | async-start | bytes 17301504 | tf_op jit(solution)/shard_map/all_gather | solution.py:96
  10.2 12.6 %copy-start.57 = (bf16[64,3072]{1,0:T(8,128)(2,1)S(1)}, bf16[64,3072]{1,0:T(8,128)(2,1)}, u32[]{:S(2)}) copy-start(bf16[64,3072]{1,0:T(8,128)(2,1)} %param.22) | copy-start | bytes 1179652
  12.7 12.2 %copy-start.96 = (bf16[64]{0:T(256)(128)(2,1)S(1)}, bf16[64]{0:T(256)(128)(2,1)}, u32[]{:S(2)}) copy-start(bf16[64]{0:T(256)(128)(2,1)} %param.21) | copy-start | bytes 388
  12.7 12.1 %copy-start.97 = (bf16[64]{0:T(256)(128)(2,1)S(1)}, bf16[64]{0:T(256)(128)(2,1)}, u32[]{:S(2)}) copy-start(bf16[64]{0:T(256)(128)(2,1)} %param.27) | copy-start | bytes 388
  12.7 12.1 %copy-start.98 = (bf16[16]{0:T(256)(128)(2,1)S(1)}, bf16[16]{0:T(256)(128)(2,1)}, u32[]{:S(2)}) copy-start(bf16[16]{0:T(256)(128)(2,1)} %param.24) | copy-start | bytes 100
  14.1 206.0 %copy-start.75 = (s32[512]{0:T(512)S(1)}, s32[512]{0:T(512)}, u32[]{:S(2)}) copy-start(s32[512]{0:T(512)} %param.37) | copy-start | bytes 6148
  14.1 373.3 %all-to-all-start = ((bf16[32,2,64,88]{3,2,1,0:T(8,128)(2,1)}), bf16[32,2,64,88]{3,2,1,0:T(8,128)(2,1)}, u32[]{:S(2)}, u32[]{:S(2)}) async-start(bf16[32,2,64,88]{3,2,1,0:T(8,128)(2,1)} %copy.299), calls=%async_computation | async-start | bytes 2097152 | tf_op jit(solution)/shard_map/all_to_all | solution.py:1053
  21.5 991.9 %reduce-scatter.2.cloned.1.call-start = ((), (), s32[]{:S(2)}) async-start(), calls=%async_computation.3 | async-start | bytes 17301504 | tf_op jit(solution)/shard_map/reduce_scatter | solution.py:100
  217.7 5.2 copy-start.4
  219.0 9.6 copy-start.76
  219.1 50.0 %copy-start.63 = (f32[2048]{0:T(1024)}, f32[2048]{0:T(1024)S(1)}, u32[]{:S(2)}) copy-start(f32[2048]{0:T(1024)S(1)} %reshape.653) | copy-start | bytes 24580
  219.7 5.5 copy-start.69
  220.1 50.1 %copy-start.18 = (bf16[2048,16]{1,0:T(8,128)(2,1)}, bf16[2048,16]{1,0:T(8,128)(2,1)S(1)}, u32[]{:S(2)}) copy-start(bf16[2048,16]{1,0:T(8,128)(2,1)S(1)} %reshape.634) | copy-start | bytes 196612
  225.3 9.0 copy-start.6
  227.3 19.4 %copy-start.42 = (bf16[512,32]{1,0:T(8,128)(2,1)}, bf16[512,32]{1,0:T(8,128)(2,1)S(1)}, u32[]{:S(2)}) copy-start(bf16[512,32]{1,0:T(8,128)(2,1)S(1)} %get-tuple-element.191) | copy-start | bytes 98308
  227.3 19.4 %copy-start.44 = (bf16[512,32]{1,0:T(8,128)(2,1)}, bf16[512,32]{1,0:T(8,128)(2,1)S(1)}, u32[]{:S(2)}) copy-start(bf16[512,32]{1,0:T(8,128)(2,1)S(1)} %get-tuple-element.192) | copy-start | bytes 98308
  227.4 18.1 %copy-start.54 = (f32[512,32]{0,1:T(8,128)}, f32[512,32]{0,1:T(8,128)S(1)}, u32[]{:S(2)}) copy-start(f32[512,32]{0,1:T(8,128)S(1)} %copy.292) | copy-start | bytes 196612
  235.8 9.9 copy-start.21
  236.1 12.5 %copy-start.16 = (bf16[512,4,128]{0,2,1:T(8,128)(2,1)}, bf16[512,4,128]{0,2,1:T(8,128)(2,1)S(1)}, u32[]{:S(2)}) copy-start(bf16[512,4,128]{0,2,1:T(8,128)(2,1)S(1)} %copy.343) | copy-start | bytes 1572868
  251.2 17.1 %copy-start.72 = (s32[128,6]{0,1:T(8,128)S(1)}, s32[128,6]{0,1:T(8,128)}, u32[]{:S(2)}) copy-start(s32[128,6]{0,1:T(8,128)} %param.35) | copy-start | bytes 9220
  251.2 17.2 %copy-start.10 = (bf16[128,2048]{1,0:T(8,128)(2,1)S(1)}, bf16[128,2048]{1,0:T(8,128)(2,1)}, u32[]{:S(2)}) copy-start(bf16[128,2048]{1,0:T(8,128)(2,1)} %refs_0_.1) | copy-start | bytes 1572868
  252.5 18.3 %copy-start.101 = (s32[128]{0:T(128)S(1)}, s32[128]{0:T(128)}, u32[]{:S(2)}) copy-start(s32[128]{0:T(128)} %param.36) | copy-start | bytes 1540
  270.3 11.3 %copy-start.12 = (bf16[128,2048]{1,0:T(8,128)(2,1)}, bf16[128,2048]{1,0:T(8,128)(2,1)S(1)}, u32[]{:S(2)}) copy-start(bf16[128,2048]{1,0:T(8,128)(2,1)S(1)} %multiply_convert_fusion.5) | copy-start | bytes 1572868
  388.9 21.2 %copy-start.60 = (bf16[2048,88]{0,1:T(8,128)(2,1)}, bf16[2048,88]{0,1:T(8,128)(2,1)S(1)}, u32[]{:S(2)}) copy-start(bf16[2048,88]{0,1:T(8,128)(2,1)S(1)} %copy.300) | copy-start | bytes 1081348
  389.1 20.9 %copy-start.58 = (bf16[2048,88]{0,1:T(8,128)(2,1)}, bf16[2048,88]{0,1:T(8,128)(2,1)S(1)}, u32[]{:S(2)}) copy-start(bf16[2048,88]{0,1:T(8,128)(2,1)S(1)} %copy.301) | copy-start | bytes 1081348
  389.1 20.9 %copy-start.35 = (bf16[2048,352]{0,1:T(8,128)(2,1)S(1)}, bf16[2048,352]{0,1:T(8,128)(2,1)}, u32[]{:S(2)}) copy-start(bf16[2048,352]{0,1:T(8,128)(2,1)} %get-tuple-element.158) | copy-start | bytes 4325380
  389.1 20.9 %copy-start.37 = (bf16[2048,352]{0,1:T(8,128)(2,1)S(1)}, bf16[2048,352]{0,1:T(8,128)(2,1)}, u32[]{:S(2)}) copy-start(bf16[2048,352]{0,1:T(8,128)(2,1)} %get-tuple-element.159) | copy-start | bytes 4325380
  507.1 5.7 copy-start.51
  514.8 7.4 copy-start.81
  600.7 9.0 copy-start.36
  600.9 8.8 copy-start.61
  602.0 399.0 %all-to-all-start.1 = ((bf16[32,2,64,88]{3,2,1,0:T(8,128)(2,1)}), bf16[32,2,64,88]{3,2,1,0:T(8,128)(2,1)}, u32[]{:S(2)}, u32[]{:S(2)}) async-start(bf16[32,2,64,88]{3,2,1,0:T(8,128)(2,1)} %copy.323), calls=%async_computation.2 | async-start | bytes 2097152 | tf_op jit(solution)/shard_map/all_to_all | solution.py:1124
  609.7 23.6 %copy-start.33 = (bf16[2048,352]{0,1:T(8,128)(2,1)S(1)}, bf16[2048,352]{0,1:T(8,128)(2,1)}, u32[]{:S(2)}) copy-start(bf16[2048,352]{0,1:T(8,128)(2,1)} %get-tuple-element.160) | copy-start | bytes 4325380
  609.7 23.6 %copy-start.34 = (bf16[2048,352]{0,1:T(8,128)(2,1)S(1)}, bf16[2048,352]{0,1:T(8,128)(2,1)}, u32[]{:S(2)}) copy-start(bf16[2048,352]{0,1:T(8,128)(2,1)} %get-tuple-element.161) | copy-start | bytes 4325380
  609.7 23.6 %copy-start.59 = (bf16[2048,88]{0,1:T(8,128)(2,1)S(1)}, bf16[2048,88]{0,1:T(8,128)(2,1)}, u32[]{:S(2)}) copy-start(bf16[2048,88]{0,1:T(8,128)(2,1)} %copy-done.58) | copy-start | bytes 1081348
  696.1 85.5 %copy-start.73 = (s32[128,6]{0,1:T(8,128)S(1)}, s32[128,6]{0,1:T(8,128)}, u32[]{:S(2)}) copy-start(s32[128,6]{0,1:T(8,128)} %param.35) | copy-start | bytes 9220
  696.1 85.5 %copy-start.68 = (f32[128,6]{0,1:T(8,128)S(1)}, f32[128,6]{0,1:T(8,128)}, u32[]{:S(2)}) copy-start(f32[128,6]{0,1:T(8,128)} %copy-done.67) | copy-start | bytes 9220
  696.1 85.5 %copy-start.83 = (f32[128]{0:T(128)S(1)}, f32[128]{0:T(128)}, u32[]{:S(2)}) copy-start(f32[128]{0:T(128)} %copy-done.82) | copy-start | bytes 1540
  696.1 85.5 %copy-start.84 = (pred[128,6]{0,1:T(8,128)(4,1)S(1)}, pred[128,6]{0,1:T(8,128)(4,1)}, u32[]{:S(2)}) copy-start(pred[128,6]{0,1:T(8,128)(4,1)} %get-tuple-element.147) | copy-start | bytes 2308
  696.1 85.5 %copy-start.89 = (f32[128]{0:T(128)S(1)}, f32[128]{0:T(128)}, u32[]{:S(2)}) copy-start(f32[128]{0:T(128)} %copy-done.88) | copy-start | bytes 1540
  696.1 85.6 %copy-start.3 = (f32[128,2048]{1,0:T(8,128)S(1)}, f32[128,2048]{1,0:T(8,128)}, u32[]{:S(2)}) copy-start(f32[128,2048]{1,0:T(8,128)} %copy-done.2) | copy-start | bytes 3145732
  696.1 85.6 %copy-start.19 = (bf16[2048,16]{1,0:T(8,128)(2,1)S(1)}, bf16[2048,16]{1,0:T(8,128)(2,1)}, u32[]{:S(2)}) copy-start(bf16[2048,16]{1,0:T(8,128)(2,1)} %copy-done.18) | copy-start | bytes 196612
  696.1 85.6 %copy-start.64 = (f32[2048]{0:T(1024)S(1)}, f32[2048]{0:T(1024)}, u32[]{:S(2)}) copy-start(f32[2048]{0:T(1024)} %copy-done.63) | copy-start | bytes 24580
  696.2 85.6 %copy-start.86 = (f32[128]{0:T(128)S(1)}, f32[128]{0:T(128)}, u32[]{:S(2)}) copy-start(f32[128]{0:T(128)} %copy-done.85) | copy-start | bytes 1540
  780.6 6.8 copy-start.94
  783.5 25.3 %copy-start.8 = (f32[128,2048]{1,0:T(8,128)}, f32[128,2048]{1,0:T(8,128)S(1)}, u32[]{:S(2)}) copy-start(f32[128,2048]{1,0:T(8,128)S(1)} %get-tuple-element.196) | copy-start | bytes 3145732
  788.0 24.6 %copy-start.91 = (f32[128]{0:T(128)}, f32[128]{0:T(128)S(1)}, u32[]{:S(2)}) copy-start(f32[128]{0:T(128)S(1)} %get-tuple-element.201) | copy-start | bytes 1540
  816.7 16.9 %copy-start.24 = (f32[512,4,192]{0,2,1:T(8,128)S(1)}, f32[512,4,192]{0,2,1:T(8,128)}, u32[]{:S(2)}) copy-start(f32[512,4,192]{0,2,1:T(8,128)} %copy-done.23) | copy-start | bytes 4718596
  837.1 13.1 %copy-start.70 = (f32[2048]{0:T(1024)S(1)}, f32[2048]{0:T(1024)}, u32[]{:S(2)}) copy-start(f32[2048]{0:T(1024)} %copy-done.69) | copy-start | bytes 24580
  837.5 12.8 %copy-start.30 = (bf16[4,2,2,2,64,576]{5,4,3,2,1,0:T(8,128)(2,1)S(1)}, bf16[4,2,2,2,64,576]{5,4,3,2,1,0:T(8,128)(2,1)}, u32[]{:S(2)}) copy-start(bf16[4,2,2,2,64,576]{5,4,3,2,1,0:T(8,128)(2,1)} %get-tuple-element.29) | copy-start | bytes 7077892
  850.3 22.4 %copy-start.7 = (f32[512,576]{1,0:T(8,128)S(1)}, f32[512,576]{1,0:T(8,128)}, u32[]{:S(2)}) copy-start(f32[512,576]{1,0:T(8,128)} %copy-done.6) | copy-start | bytes 3538948
  854.0 18.7 %copy-start.26 = (bf16[512,4,256]{0,2,1:T(8,128)(2,1)S(1)}, bf16[512,4,256]{0,2,1:T(8,128)(2,1)}, u32[]{:S(2)}) copy-start(bf16[512,4,256]{0,2,1:T(8,128)(2,1)} %copy-done.25) | copy-start | bytes 3145732
  858.4 14.4 %copy-start.77 = (f32[512]{0:T(512)S(1)}, f32[512]{0:T(512)}, u32[]{:S(2)}) copy-start(f32[512]{0:T(512)} %copy-done.76) | copy-start | bytes 6148
  858.4 14.4 %copy-start.79 = (f32[512]{0:T(512)S(1)}, f32[512]{0:T(512)}, u32[]{:S(2)}) copy-start(f32[512]{0:T(512)} %copy-done.78) | copy-start | bytes 6148
  986.6 6.6 slice-start.2
  989.8 5.1 slice-start
  1003.7 9.8 copy-start.9
  1003.7 9.8 copy-start.11
  1003.7 9.8 copy-start.20
  1003.7 9.8 copy-start.87
  1003.7 9.8 copy-start.90
  1003.7 9.8 copy-start.92
  (46 other events, 110.1 us)
Sparse Core Ops, SparseCore 0:
  10.9 192.4 all-gather.1
  507.2 196.4 reduce-scatter.1

commit v3 on v2

v3 whole, which is shorter than its diff:
```python
import functools

import jax
import jax.numpy as jnp
from jax import lax
from jax.experimental import pallas as pl
from jax.experimental.pallas import tpu as pltpu
from jax.sharding import PartitionSpec as P

HEADS = 16
NOPE = 128
ROPE = 64
VDIM = 128
KV_RANK = 512
CONTS = 2


EPSILON = 1e-06
THETA = 10000.0
NEGATIVE = -1e30
BOTH = ("expert", "shard")
BF = jnp.bfloat16
F32 = jnp.float32


def rms_forward(values, gain_row):
    inverse = lax.rsqrt(jnp.mean(values * values, axis=-1, keepdims=True) + EPSILON)
    return (values * inverse * gain_row, inverse)


def rms_backward(values, inverse, gain_row, upstream):
    normed = values * inverse
    scaled = upstream * gain_row
    value_grad = inverse * (scaled - normed * jnp.mean(scaled * normed, axis=-1, keepdims=True))
    return (value_grad, jnp.sum(upstream * normed, axis=0))


def rope_tables(positions, width):
    half_width = width // 2
    frequency = THETA ** (-2.0 * jnp.arange(half_width, dtype=jnp.float32) / width)
    angles = positions.astype(jnp.float32)[:, None] * frequency[None, :]
    return (jnp.cos(angles), jnp.sin(angles))


def rotate(values, cosine_table, sine_table):
    half_width = values.shape[-1] // 2
    first_half = values[..., :half_width]
    second = values[..., half_width:]
    return jnp.concatenate(
        [
            first_half * cosine_table - second * sine_table,
            second * cosine_table + first_half * sine_table,
        ],
        axis=-1,
    )


def positions_of(group_ids):
    length = group_ids.shape[0]
    token_index = jnp.arange(length, dtype=jnp.int32)
    labels = jnp.arange(CONTS + 1, dtype=jnp.int32)
    member = (group_ids[:, None] == labels[None, :]).astype(jnp.int32)
    counts = jnp.sum(member, axis=0)
    starts = jnp.cumsum(counts) - counts
    start_of = jnp.sum(member * starts[None, :], axis=1)
    return token_index - start_of + jnp.where(group_ids > 0, counts[0], 0)


def kept_pairs(choice_ids, rank_row, choice_hot, capacity):
    row_count, top_count, expert_total = choice_hot.shape
    per_k = jnp.sum(choice_hot, axis=0)
    before_k = jnp.cumsum(per_k, axis=0) - per_k
    lower = (rank_row[None, :] < rank_row[:, None]).astype(F32)
    same_k = jnp.dot(
        lower.astype(BF),
        choice_hot.reshape(row_count, top_count * expert_total).astype(BF),
        preferred_element_type=F32,
    ).reshape(row_count, top_count, expert_total)
    place = jnp.sum((same_k + before_k[None]) * choice_hot, axis=-1)
    return (place < capacity).astype(F32)


def mm(a, b):
    return jnp.dot(a, b, preferred_element_type=F32)


def mm_nt(a, b):
    return lax.dot_general(a, b, (((1,), (1,)), ((), ())), preferred_element_type=F32)


def mm_tn(a, b):
    return lax.dot_general(a, b, (((0,), (0,)), ((), ())), preferred_element_type=F32)


def gather(value, axes):
    return lax.all_gather(value, axes, axis=0, tiled=True)


def scatter_sum(value, axes):
    return lax.psum_scatter(value, axes, scatter_dimension=0, tiled=True)


HBM = pl.BlockSpec(memory_space=pl.ANY)
VMEM = pl.BlockSpec(memory_space=pltpu.VMEM)


class Place:
    def __init__(self):
        e, s = lax.axis_index("expert"), lax.axis_index("shard")
        self.z, self.y, self.x, self.c = e // 2, e % 2, s // 2, s % 2

    def at(self, z=None, y=None, x=None, c=None):
        z = self.z if z is None else z
        y = self.y if y is None else y
        x = self.x if x is None else x
        c = self.c if c is None else c
        return {"expert": 2 * z + y, "shard": 2 * x + c}


def greet(partners):
    barrier = pltpu.get_barrier_semaphore()
    for partner in partners:
        pl.semaphore_signal(
            barrier, inc=1, device_id=partner, device_id_type=pl.DeviceIdType.MESH
        )
    pl.semaphore_wait(barrier, len(partners))


def remote(src, dst, send, recv, where):
    return pltpu.make_async_remote_copy(
        src_ref=src,
        dst_ref=dst,
        send_sem=send,
        recv_sem=recv,
        device_id=where,
        device_id_type=pl.DeviceIdType.MESH,
    )


def gather_group_kernel(cuts, spans, *refs):
    refs = list(refs)
    take = lambda n: [refs.pop(0) for _ in range(n)]
    (src,) = take(1)
    work = take(4) if spans else None
    (dst,) = take(1)
    made = take(3) if spans else None
    own_sem, send, recv = take(3)
    me = Place()
    x, c = me.x, me.c
    to_x, to_c = me.at(x=1 - x), me.at(c=1 - c)
    greet([to_x, to_c])
    cut = src.shape[0] // cuts
    span = lambda k: pl.ds(k * cut, cut)
    own = pltpu.make_async_copy(src, dst.at[x, c], own_sem)
    own.start()
    over_x = [
        remote(src.at[span(k)], dst.at[x, c, span(k)], send.at[0, k], recv.at[0, k], to_x)
        for k in range(cuts)
    ]
    for copy in over_x:
        copy.start()
    over_c = remote(src, dst.at[x, c], send.at[1, 0], recv.at[1, 0], to_c)
    over_c.start()
    if spans:
        turns, begin_work, work_turn = grad_worker(work, made, refs[:3], refs[3], spans)
        begin_work()

        @pl.loop(0, turns)
        def _(n):
            work_turn(n)

    relays = []
    for k in range(cuts):
        far = dst.at[1 - x, c, span(k)]
        remote(far, far, send.at[0, k], recv.at[0, k], to_x).wait_recv()
        relays.append(remote(far, far, send.at[2, k], recv.at[2, k], to_c))
        relays[-1].start()
    far = dst.at[x, 1 - c]
    remote(far, far, send.at[1, 0], recv.at[1, 0], to_c).wait_recv()
    for k in range(cuts):
        far = dst.at[1 - x, 1 - c, span(k)]
        remote(far, far, send.at[2, k], recv.at[2, k], to_c).wait_recv()
    own.wait()
    for copy in over_x + [over_c] + relays:
        copy.wait_send()


def gather_group(value, ident, work=None, spans=None, lines=None, cuts=4):
    rows, width = value.shape
    dma = pltpu.SemaphoreType.DMA
    inputs, in_specs = [value], [HBM]
    outs = [jax.ShapeDtypeStruct((2, 2, rows, width), value.dtype)]
    scratch = [dma, dma((3, cuts)), dma((3, cuts))]
    if work:
        inputs += work
        in_specs += [HBM] * 4
        shapes, buffers = work_shapes(work, spans, lines)
        outs += shapes
        scratch += buffers
    out, *made = pl.pallas_call(
        functools.partial(gather_group_kernel, cuts, spans if work else None),
        out_shape=outs,
        in_specs=in_specs,
        out_specs=[HBM] + [VMEM] * (len(outs) - 1),
        scratch_shapes=scratch,
        compiler_params=pltpu.CompilerParams(
            collective_id=ident, has_side_effects=True, vmem_limit_bytes=40 << 20
        ),
    )(*inputs)
    return [out.reshape(4 * rows, width)] + made


def sum_group_kernel(cuts, part, out, cbuf, xbuf, xsum, cs, cr, xs, xr):
    me = Place()
    x, c = me.x, me.c
    rows, width = out.shape
    cut = rows // cuts
    to_x, to_c = me.at(x=1 - x), me.at(c=1 - c)
    greet([to_x, to_c])
    span = lambda k: pl.ds(k * cut, cut)
    core = lambda k, far: remote(
        part.at[1 - x if far else x, 1 - c, span(k)],
        cbuf.at[far, span(k)],
        cs.at[k, far],
        cr.at[k, far],
        to_c,
    )
    over = lambda k: remote(xsum.at[span(k)], xbuf.at[span(k)], xs.at[k], xr.at[k], to_x)
    for k in range(cuts):
        core(k, 1).start()
    for k in range(cuts):
        core(k, 0).start()

    def add(k, target, one, two):
        @pl.loop(0, cut // 16)
        def _(i):
            at = pl.ds(pl.multiple_of(k * cut + i * 16, 16), 16)
            target[at] = (one[at].astype(F32) + two[at].astype(F32)).astype(target.dtype)

    for k in range(cuts):
        core(k, 1).wait_recv()
        add(k, xsum, part.at[1 - x, c], cbuf.at[1])
        over(k).start()
    for k in range(cuts):
        core(k, 0).wait_recv()
        add(k, out, part.at[x, c], cbuf.at[0])
    for k in range(cuts):
        over(k).wait_recv()
        add(k, out, out, xbuf)
    for k in range(cuts):
        core(k, 1).wait_send()
        core(k, 0).wait_send()
        over(k).wait_send()


def sum_group(part, ident, cuts=4):
    rows, width = part.shape[0] // 4, part.shape[1]
    dma = pltpu.SemaphoreType.DMA
    buf = lambda *lead: pltpu.VMEM(lead + (rows, width), part.dtype)
    return pl.pallas_call(
        functools.partial(sum_group_kernel, cuts),
        out_shape=jax.ShapeDtypeStruct((rows, width), F32),
        in_specs=[VMEM],
        out_specs=VMEM,
        scratch_shapes=[
            buf(2), buf(), buf(),
            dma((cuts, 2)), dma((cuts, 2)), dma((cuts,)), dma((cuts,)),
        ],
        compiler_params=pltpu.CompilerParams(
            collective_id=ident, has_side_effects=True, vmem_limit_bytes=32 << 20
        ),
    )(part.reshape(2, 2, rows, width))


def add_blocks(target, one, two):
    if len(target.shape) > 2:
        for i in range(target.shape[0]):
            add_blocks(target.at[i], one.at[i], two.at[i])
        return
    rows = target.shape[0]
    step = 16 if rows % 16 == 0 else rows

    @pl.loop(0, rows // step)
    def _(i):
        at = pl.ds(pl.multiple_of(i * step, step), step)
        target[at] = (one[at].astype(F32) + two[at].astype(F32)).astype(target.dtype)


class Copies:
    def __init__(self):
        self.started = []

    def go(self, copy):
        copy.start()
        self.started.append(copy)

    def finish(self):
        for copy in self.started:
            copy.wait_send()


def start_kernel(lines, counts, with_o, *refs):
    jobs, planes = 3, len(counts)
    refs = list(refs)
    take = lambda n: [refs.pop(0) for _ in range(n)]
    (tok,) = take(1)
    plane_src, sources = take(planes), take(jobs)
    o_src = take(1)[0] if with_o else None
    (tok_dst,) = take(1)
    plane_dst, dests = take(planes), take(jobs)
    o_dst = take(1)[0] if with_o else None
    own_sem, gs, gr, zs, zr, ys, yr, ts, tr = take(9)
    plane_sems = [take(6) for _ in range(planes)]
    if with_o:
        o_own, ocs, ocr, ozs, ozr, oys, oyr = take(7)
    me = Place()
    z, y, x, c = me.z, me.y, me.x, me.c
    others = [lax.rem(z + 1 + j, lines) for j in range(lines - 1)]
    places = list(enumerate(others)) + [(lines - 1, z)]
    near = [(x, 1 - c), (1 - x, c), (1 - x, 1 - c)]
    to_near = [me.at(x=xx, c=cc) for xx, cc in near]
    to_y, to_x, to_c = me.at(y=1 - y), to_near[1], to_near[0]
    greet([me.at(z=o) for o in others] + [to_y] + to_near)
    copies = Copies()
    go = copies.go

    def span(i, k):
        rows = plane_src[i].shape[0] // counts[i]
        return pl.ds(k * rows, rows)

    def plane_z_start(i, k):
        zs_, zr_, ys_, yr_ = plane_sems[i][:4]
        src, dst = plane_src[i].at[span(i, k)], plane_dst[i].at[z, y, x, c, span(i, k)]
        for j, o in enumerate(others):
            go(remote(src, dst, zs_.at[k, j], zr_.at[k, z], me.at(z=o)))
        go(remote(src, dst, ys_.at[k, lines - 1], yr_.at[k, z], to_y))

    def plane_z_land(i, k):
        zs_, zr_, ys_, yr_ = plane_sems[i][:4]
        for j, o in reversed(places[:-1]):
            block = plane_dst[i].at[o, y, x, c, span(i, k)]
            remote(block, block, zs_.at[k, j], zr_.at[k, o], me.at(z=o)).wait_recv()
            go(remote(block, block, ys_.at[k, j], yr_.at[k, o], to_y))

    def plane_y_land(i, k):
        ys_, yr_, ps, pr = plane_sems[i][2:]
        for j, o in places:
            block = plane_dst[i].at[o, 1 - y, x, c, span(i, k)]
            remote(block, block, ys_.at[k, j], yr_.at[k, o], to_y).wait_recv()
        block = plane_dst[i].at[:, :, x, c, span(i, k)]
        go(remote(block, block, ps.at[k, 0], pr.at[k, 0], to_x))
        go(remote(block, block, ps.at[k, 1], pr.at[k, 1], to_c))

    def plane_x_land(i, k):
        ps, pr = plane_sems[i][4:]
        block = plane_dst[i].at[:, :, 1 - x, c, span(i, k)]
        remote(block, block, ps.at[k, 0], pr.at[k, 0], to_x).wait_recv()
        go(remote(block, block, ps.at[k, 2], pr.at[k, 2], to_c))

    def plane_c_land(i, k):
        ps, pr = plane_sems[i][4:]
        for slot, xx in ((1, x), (2, 1 - x)):
            block = plane_dst[i].at[:, :, xx, 1 - c, span(i, k)]
            remote(block, block, ps.at[k, slot], pr.at[k, slot], to_c).wait_recv()

    locals_ = [
        pltpu.make_async_copy(src, dst.at[z, y, x, c], own_sem.at[i])
        for i, (src, dst) in enumerate(
            zip([v.at[x, c] for v in sources] + plane_src, dests + plane_dst)
        )
    ]
    locals_.append(pltpu.make_async_copy(tok, tok_dst.at[x, c], own_sem.at[jobs + planes]))
    for copy in locals_:
        copy.start()

    for i in range(jobs):
        for p in range(3):
            go(
                remote(
                    sources[i].at[near[p][0], near[p][1]],
                    dests[i].at[z, y, x, c],
                    gs.at[i, p],
                    gr.at[i, p],
                    to_near[p],
                )
            )
    last = planes - 1
    plane_z_start(last, 0)
    if counts[last] > 1:
        plane_z_start(last, 1)
    if with_o:
        o_core = remote(o_src, o_dst.at[z, c], ocs, ocr, to_c)
        o_local = pltpu.make_async_copy(o_src, o_dst.at[z, c], o_own)
        holder = c == y

        @pl.when(jnp.logical_not(holder))
        def _():
            o_core.start()

        @pl.when(holder)
        def _():
            o_local.start()

    go(remote(tok, tok_dst.at[x, c], ts.at[1], tr.at[1], to_x))
    go(remote(tok, tok_dst.at[x, c], ts.at[0], tr.at[0], to_c))
    line_y = lambda i, j, o: remote(
        dests[i].at[o, y], dests[i].at[o, y], ys.at[i, j], yr.at[i, o], to_y
    )
    line_z = lambda i, j, o: remote(
        dests[i].at[z, y], dests[i].at[z, y], zs.at[i, j], zr.at[i, z], me.at(z=o)
    )

    def job_start(i):
        locals_[i].wait()
        for p in range(3):
            xx, cc = near[p]
            block = dests[i].at[z, y, xx, cc]
            remote(block, block, gs.at[i, p], gr.at[i, p], to_near[p]).wait_recv()
        for j, o in enumerate(others):
            go(line_z(i, j, o))
        go(line_y(i, lines - 1, z))

    job_start(0)
    job_start(1)
    plane_z_land(last, 0)
    for k in range(1, counts[last]):
        if k + 1 < counts[last]:
            plane_z_start(last, k + 1)
        plane_z_land(last, k)
        if k == 1:
            job_start(2)
        locals_[jobs + last].wait() if k == 1 else None
        plane_y_land(last, k - 1)
    if counts[last] == 1:
        job_start(2)
        locals_[jobs + last].wait()
    if with_o:
        o_z = lambda j, o: remote(o_dst.at[z], o_dst.at[z], ozs.at[j], ozr.at[z], me.at(z=o))
        o_y = lambda j, o: remote(o_dst.at[o], o_dst.at[o], oys.at[j], oyr.at[o], to_y)

        @pl.when(holder)
        def _():
            o_local.wait()
            block = o_dst.at[z, 1 - c]
            remote(block, block, ocs, ocr, to_c).wait_recv()
            for j, o in enumerate(others):
                o_z(j, o).start()
            o_y(lines - 1, z).start()

    for i in range(last):
        for k in range(counts[i]):
            plane_z_start(i, k)
    plane_y_land(last, counts[last] - 1)
    block = tok_dst.at[1 - x, c]
    remote(block, block, ts.at[1], tr.at[1], to_x).wait_recv()
    go(remote(block, block, ts.at[2], tr.at[2], to_c))
    for j, o in reversed(places[:-1]):
        for i in range(jobs):
            block = dests[i].at[o, y]
            remote(block, block, zs.at[i, j], zr.at[i, o], me.at(z=o)).wait_recv()
            go(line_y(i, j, o))
        if with_o:

            @pl.when(holder)
            def _(j=j, o=o):
                block = o_dst.at[o]
                remote(block, block, ozs.at[j], ozr.at[o], me.at(z=o)).wait_recv()
                o_y(j, o).start()

    for i in range(last):
        for k in range(counts[i]):
            plane_z_land(i, k)
    for k in range(counts[last]):
        plane_x_land(last, k)
    for i in range(last):
        locals_[jobs + i].wait()
        for k in range(counts[i]):
            plane_y_land(i, k)
            plane_x_land(i, k)
    for slot, xx in ((0, x), (2, 1 - x)):
        block = tok_dst.at[xx, 1 - c]
        remote(block, block, ts.at[slot], tr.at[slot], to_c).wait_recv()
    locals_[jobs + planes].wait()
    for j, o in places:
        for i in range(jobs):
            block = dests[i].at[o, 1 - y]
            remote(block, block, ys.at[i, j], yr.at[i, o], to_y).wait_recv()
    if with_o:

        @pl.when(jnp.logical_not(holder))
        def _():
            for j, o in places:
                remote(o_dst.at[o], o_dst.at[o], oys.at[j], oyr.at[o], to_y).wait_recv()
            o_core.wait_send()

        @pl.when(holder)
        def _():
            for j, o in enumerate(others):
                o_z(j, o).wait_send()
            for j, o in places:
                o_y(j, o).wait_send()

    for i in range(planes):
        for k in range(counts[i]):
            plane_c_land(i, k)
    copies.finish()


def start_gather(tokens, planes, counts, column_parts, o_rows, lines, ident):
    jobs = len(column_parts)
    with_o = o_rows is not None
    inputs = [tokens] + planes + column_parts + ([o_rows] if with_o else [])
    shape = lambda lead, v: jax.ShapeDtypeStruct(lead + v.shape, v.dtype)
    outs = [shape((2, 2), tokens)] + [shape((lines, 2, 2, 2), v) for v in planes]
    outs += [jax.ShapeDtypeStruct((lines, 2) + v.shape, v.dtype) for v in column_parts]
    if with_o:
        outs.append(shape((lines, 2), o_rows))
    dma = pltpu.SemaphoreType.DMA
    scratch = [
        dma((jobs + len(planes) + 1,)), dma((jobs, 3)), dma((jobs, 3)),
        dma((jobs, lines)), dma((jobs, lines)), dma((jobs, lines)), dma((jobs, lines)),
        dma((3,)), dma((3,)),
    ]
    for n in counts:
        scratch += [dma((n, lines))] * 4 + [dma((n, 3))] * 2
    if with_o:
        scratch += [dma, dma, dma, dma((lines,)), dma((lines,)), dma((lines,)), dma((lines,))]
    return pl.pallas_call(
        functools.partial(start_kernel, lines, tuple(counts), with_o),
        out_shape=outs,
        in_specs=[HBM] * len(inputs),
        out_specs=[HBM] * len(outs),
        scratch_shapes=scratch,
        compiler_params=pltpu.CompilerParams(collective_id=ident, has_side_effects=True),
    )(*inputs)


def grad_worker(work, made, slots, ins, spans):
    values, cots, in_d, hid = work
    rows_in, cots_in, left_in = slots
    depth, width = rows_in.shape[1:]
    early = cots.shape[1]
    inner = hid.shape[1]
    turns = cots.shape[0] // depth
    first, units = spans[0][0], left_in.shape[3]

    def loads(n):
        at = pl.ds(pl.multiple_of(n * depth, depth), depth)
        slot = lax.rem(n, 2)
        pairs = (
            (values.at[at, pl.ds(0, width)], rows_in.at[slot]),
            (cots.at[at], cots_in.at[slot, :, pl.ds(0, early)]),
            (
                values.at[at, pl.ds(width + 128, width - early)],
                cots_in.at[slot, :, pl.ds(early, width - early)],
            ),
            (in_d.at[at, pl.ds(first, units)], left_in.at[slot, 0]),
            (in_d.at[at, pl.ds(inner + first, units)], left_in.at[slot, 1]),
            (hid.at[at, pl.ds(first, units)], left_in.at[slot, 2]),
        )
        return [
            pltpu.make_async_copy(src, dst, ins.at[slot, i]) for i, (src, dst) in enumerate(pairs)
        ]

    def begin():
        for copy in loads(0):
            copy.start()
        for ref in made:
            for i in range(ref.shape[0]):
                ref[i] = jnp.zeros(ref.shape[1:], F32)

    def turn(n):
        slot = lax.rem(n, 2)

        @pl.when(n + 1 < turns)
        def _():
            for copy in loads(n + 1):
                copy.start()

        for copy in loads(n):
            copy.wait()

        @pl.loop(0, width // 512)
        def _(m):
            at = pl.ds(pl.multiple_of(m * 512, 512), 512)
            for which, right in enumerate((rows_in, rows_in, cots_in)):
                ref = made[which]
                part = lax.dot_general(
                    left_in[slot, which],
                    right[slot, :, at],
                    (((0,), (0,)), ((), ())),
                    preferred_element_type=F32,
                )
                for i, (begin, _, kept) in enumerate(spans):
                    begin = begin - first
                    ref[i, :, at] = ref[i, :, at] + part[begin : begin + kept]

    return turns, begin, turn


def work_shapes(work, spans, lines):
    count, width = work[1].shape[0], work[0].shape[1] - 128
    width = (width + work[1].shape[1]) // 2
    units = sum(size for _, size, _ in spans)
    depth = min(512, count // lines)
    shapes = [jax.ShapeDtypeStruct((len(spans), spans[0][2], width), F32)] * 3
    rows = pltpu.VMEM((2, depth, width), BF)
    buffers = [rows, rows, pltpu.VMEM((2, 3, depth, units), BF), pltpu.SemaphoreType.DMA((2, 6))]
    return shapes, buffers


def grads_kernel(lines, kinds, with_o, spans, *refs):
    jobs = len(kinds)
    take = lambda n: [refs.pop(0) for _ in range(n)]
    refs = list(refs)
    parts = take(jobs)
    o_part = take(1)[0] if with_o else None
    work = take(4) if spans else None
    outs = take(jobs)
    o_out = take(1)[0] if with_o else None
    made = take(3) if spans else None
    ybufs, zbufs, tots = take(jobs), take(jobs), take(jobs)
    if with_o:
        o_ybuf, o_zbuf, o_tot = take(3)
    ys, yr, zs, zr, gs, gr = take(6)
    if with_o:
        oys, oyr, ozs, ozr, ocs, ocr = take(6)
    if spans:
        rows_in, cots_in, left_in, ins = take(4)
    accs, o_acc = ybufs, (o_ybuf if with_o else None)
    me = Place()
    z, y, x, c = me.z, me.y, me.x, me.c
    others = [lax.rem(z + 1 + j, lines) for j in range(lines - 1)]
    near = [(x, 1 - c), (1 - x, c), (1 - x, 1 - c)]
    to_near = [me.at(x=xx, c=cc) for xx, cc in near]
    to_y, to_c = me.at(y=1 - y), to_near[0]
    greet([me.at(z=o) for o in others] + [to_y] + to_near)
    copies = Copies()
    go = copies.go
    over_y = lambda i, j, o: remote(
        parts[i].at[o, 1 - y], ybufs[i].at[o], ys.at[i, j], yr.at[i, o], to_y
    )
    over_z = lambda i, j, o: remote(
        accs[i].at[o], zbufs[i].at[z], zs.at[i, j], zr.at[i, z], me.at(z=o)
    )
    places = list(enumerate(others)) + [(lines - 1, z)]
    if with_o:
        holder = c == y
        o_over_y = lambda j, o: remote(o_part.at[o], o_ybuf.at[o], oys.at[j], oyr.at[o], to_y)
        o_over_z = lambda j, o: remote(
            o_acc.at[o], o_zbuf.at[z], ozs.at[j], ozr.at[z], me.at(z=o)
        )
    for j, o in places:
        for i in range(jobs):
            go(over_y(i, j, o))
        if with_o:

            @pl.when(jnp.logical_not(holder))
            def _(j=j, o=o):
                o_over_y(j, o).start()

    if spans:
        turns, begin_work, work_turn = grad_worker(work, made, (rows_in, cots_in, left_in), ins, spans)
        begin_work()

    @pl.loop(0, lines)
    def _(j):
        if spans:
            per_line = turns // lines

            @pl.loop(0, per_line)
            def _(n):
                work_turn(j * per_line + n)

        o = lax.rem(z + 1 + j, lines)
        for i in range(jobs):
            remote(ybufs[i].at[o], ybufs[i].at[o], ys.at[i, j], yr.at[i, o], to_y).wait_recv()
            add_blocks(accs[i].at[o], parts[i].at[o, y], ybufs[i].at[o])

            @pl.when(j < lines - 1)
            def _(i=i):
                over_z(i, j, o).start()

        if with_o:

            @pl.when(holder)
            def _():
                remote(o_ybuf.at[o], o_ybuf.at[o], oys.at[j], oyr.at[o], to_y).wait_recv()
                add_blocks(o_acc.at[o], o_part.at[o], o_ybuf.at[o])

                @pl.when(j < lines - 1)
                def _():
                    o_over_z(j, o).start()

    def line_sum(target, acc, zbuf):
        if len(target.shape) > 2:
            for k in range(target.shape[0]):
                line_sum(target.at[k], acc.at[:, k], zbuf.at[:, k])
            return
        rows = target.shape[0]
        step = 16 if rows % 16 == 0 else rows

        @pl.loop(0, rows // step)
        def _(i):
            at = pl.ds(pl.multiple_of(i * step, step), step)
            value = acc[z, at].astype(F32)
            for o in others:
                value = value + zbuf[o, at].astype(F32)
            target[at] = value.astype(target.dtype)

    near_copy = lambda i, p: remote(
        tots[i].at[near[p][0], near[p][1]], outs[i].at[x, c], gs.at[i, p], gr.at[i, p], to_near[p]
    )
    for i in range(jobs):
        for j, o in places[:-1]:
            block = zbufs[i].at[o]
            remote(block, block, zs.at[i, j], zr.at[i, o], me.at(z=o)).wait_recv()
        if kinds[i]:
            for xx in range(2):
                for cc in range(2):
                    line_sum(tots[i].at[xx, cc], accs[i].at[:, xx, cc], zbufs[i].at[:, xx, cc])
            for p in range(3):
                go(near_copy(i, p))
            rows = tots[i].shape[2]
            outs[i][x, c] = tots[i][x, c]
        else:
            line_sum(outs[i], accs[i], zbufs[i])
    if with_o:
        o_core = remote(o_tot.at[1 - c], o_out, ocs, ocr, to_c)

        @pl.when(holder)
        def _():
            for j, o in places[:-1]:
                block = o_zbuf.at[o]
                remote(block, block, ozs.at[j], ozr.at[o], me.at(z=o)).wait_recv()
            line_sum(o_tot.at[1 - c], o_acc.at[:, 1 - c], o_zbuf.at[:, 1 - c])
            o_core.start()
            line_sum(o_out, o_acc.at[:, c], o_zbuf.at[:, c])
            for j, o in places[:-1]:
                o_over_z(j, o).wait_send()
            o_core.wait_send()

        @pl.when(jnp.logical_not(holder))
        def _():
            for j, o in places:
                o_over_y(j, o).wait_send()
            o_core.wait_recv()

    for i in range(jobs):
        if kinds[i]:
            for p in range(3):
                block = outs[i].at[near[p][0], near[p][1]]
                remote(block, block, gs.at[i, p], gr.at[i, p], to_near[p]).wait_recv()
        for j, o in places[:-1]:
            over_z(i, j, o).wait_send()
    copies.finish()


def sum_grads(parts, kinds, o_part, lines, ident, work=None, spans=None):
    jobs = len(parts)
    with_o = o_part is not None
    inputs = list(parts) + ([o_part] if with_o else [])
    outs = [jax.ShapeDtypeStruct(p.shape[2:], p.dtype) for p in parts]
    if with_o:
        outs.append(jax.ShapeDtypeStruct(o_part.shape[2:], o_part.dtype))
    dma = pltpu.SemaphoreType.DMA
    line = lambda p: pltpu.VMEM((lines,) + p.shape[2:], p.dtype)
    scratch = [line(p) for p in parts] * 2
    scratch += [pltpu.VMEM(p.shape[2:] if k else (8, 128), p.dtype) for p, k in zip(parts, kinds)]
    if with_o:
        scratch += [pltpu.VMEM(o_part.shape, o_part.dtype)] * 2
        scratch += [pltpu.VMEM(o_part.shape[1:], o_part.dtype)]
    scratch += [dma((jobs, lines))] * 4 + [dma((jobs, 3))] * 2
    if with_o:
        scratch += [dma((lines,))] * 4 + [dma, dma]
    in_specs = [VMEM] * len(inputs)
    if work:
        inputs += work
        in_specs += [HBM] * 4
        shapes, buffers = work_shapes(work, spans, lines)
        outs += shapes
        scratch += buffers
    return pl.pallas_call(
        functools.partial(grads_kernel, lines, tuple(kinds), with_o, spans if work else None),
        out_shape=outs,
        in_specs=in_specs,
        out_specs=[VMEM] * len(outs),
        scratch_shapes=scratch,
        compiler_params=pltpu.CompilerParams(
            collective_id=ident, has_side_effects=True, vmem_limit_bytes=62 << 20
        ),
    )(*inputs)


def nt(a, b):
    return lax.dot_general(a, b, (((1,), (1,)), ((), ())), preferred_element_type=F32)


def hidden_kernel(
    lines, chunks, spans, local_experts,
    src, cots, spread, e_gate, e_up, e_down, s_in, s_down,
    dst, hid, in_d, gate_g, w_in_out, w_down_out,
    h_in, c_in, hid_out, in_out, g_out, w_in, w_down,
    w_sem, own_sem, hs, cins, sts, zs, zr, xs, xr, ys, yr, ds_, dr, cs, cr,
):
    me = Place()
    z, y, x, c = me.z, me.y, me.x, me.c
    expert_at = 2 * z + y
    rows, wide = src.shape
    width, early = w_down.shape[1], cots.shape[-1]
    inner = w_down.shape[0]
    step_rows = rows // chunks
    units = lines * 2 * step_rows
    others = [lax.rem(z + 1 + j, lines) for j in range(lines - 1)]
    places = [(lines - 1, z)] + list(reversed(list(enumerate(others))))
    to_x, to_y, to_c = me.at(x=1 - x), me.at(y=1 - y), me.at(c=1 - c)
    greet([me.at(z=o) for o in others] + [to_x, to_y, to_c])
    half = wide // 256 * 128
    cuts = (pl.ds(0, half), pl.ds(half, wide - half))
    side_of = lambda side: (lax.rem(y + side // 2, 2), lax.rem(x + lax.rem(side, 2), 2))

    def span(k):
        return pl.ds(pl.multiple_of(k * step_rows, step_rows), step_rows)

    def block(zz, yy, xx, k, cols=None):
        if cols is None:
            return dst.at[zz, yy, xx, c, span(k)]
        return dst.at[zz, yy, xx, c, span(k), cuts[cols]]

    own = pltpu.make_async_copy(src, dst.at[z, y, x, c], own_sem)
    own.start()
    piece = lambda k: src.at[span(k)]
    z_copy = lambda k, j, o: remote(
        piece(k), block(z, y, x, k), zs.at[k, j], zr.at[k, z], me.at(z=o)
    )
    x_copy = lambda k, j, o, b: remote(b, block(o, y, x, k), xs.at[k, j], xr.at[k, o], to_x)
    y_copy = lambda k, j, o, b: remote(b, block(o, y, x, k), ys.at[k, j], yr.at[k, o], to_y)

    def diag_copy(k, j, o, h):
        b = block(o, y, 1 - x, k, 0) if h == 0 else block(o, 1 - y, x, k, 1)
        return remote(b, b, ds_.at[k, j, h], dr.at[k, o, h], to_y if h == 0 else to_x)

    def core_copy(k, side, cc):
        yy, xx = side_of(side)
        b = dst.at[:, yy, xx, cc, span(k)]
        return remote(b, b, cs.at[k, side], cr.at[k, side], to_c)

    def z_land(k):
        for j, o in places[1:]:
            b = block(o, y, x, k)
            remote(b, b, zs.at[k, j], zr.at[k, o], me.at(z=o)).wait_recv()
            x_copy(k, j, o, b).start()
            y_copy(k, j, o, b).start()
        core_copy(k, 0, c).start()

    def xy_land(k):
        for j, o in places:
            b = block(o, y, 1 - x, k)
            remote(b, b, xs.at[k, j], xr.at[k, o], to_x).wait_recv()
            diag_copy(k, j, o, 0).start()
            b = block(o, 1 - y, x, k)
            remote(b, b, ys.at[k, j], yr.at[k, o], to_y).wait_recv()
            diag_copy(k, j, o, 1).start()
        core_copy(k, 1, c).start()
        core_copy(k, 2, c).start()

    def diag_land(k):
        for j, o in places:
            for h, w in ((0, to_y), (1, to_x)):
                b = block(o, 1 - y, 1 - x, k, h)
                remote(b, b, ds_.at[k, j, h], dr.at[k, o, h], w).wait_recv()
        core_copy(k, 3, c).start()

    def loads(k, side):
        yy, xx = side_of(side)
        return (
            pltpu.make_async_copy(dst.at[:, yy, xx, :, span(k)], h_in.at[side], hs.at[side]),
            pltpu.make_async_copy(cots.at[:, yy, xx, :, span(k)], c_in.at[side], cins.at[side]),
        )

    def fetch(k, side):
        core_copy(k, side, 1 - c).wait_recv()
        for copy in loads(k, side):
            copy.start()

    def stores(k, side):
        yy, xx = side_of(side)
        pairs = ((hid_out, hid), (in_out, in_d), (g_out, gate_g))
        return [
            pltpu.make_async_copy(v.at[side], ref.at[:, yy, xx, :, span(k)], sts.at[side, i])
            for i, (v, ref) in enumerate(pairs)
        ]

    def unit(k, side):
        for copy in loads(k, side):
            copy.wait()
        h = h_in[side, :, :, :, :width].reshape(units, width)
        gates = h_in[side, :, :, :, width : width + 128].reshape(units, 128)
        late = h_in[side, :, :, :, width + 128 :].reshape(units, width - early)
        scale = jnp.dot(gates, spread[...], preferred_element_type=F32)
        both = nt(h, w_in[...])
        down = nt(c_in[side].reshape(units, early), w_down[:, :early])
        down = down + nt(late, w_down[:, early:])
        columns = lax.broadcasted_iota(jnp.int32, (units, 128), 1)
        sums = jnp.zeros((units, 128), F32)
        for i, (begin, size) in enumerate(spans):
            at = slice(begin, begin + size)
            up_at = slice(inner + begin, inner + begin + size)
            g, u, d = both[:, at], both[:, up_at], down[:, at]
            sig = 1.0 / (1.0 + jnp.exp(-g))
            act = g * sig
            value = (act * u).astype(BF).astype(F32)
            shape = (lines, 2, step_rows, size)
            if i < local_experts:
                total = jnp.sum(value * d, axis=1, keepdims=True)
                sums = jnp.where(columns == expert_at * local_experts + i, total, sums)
                value = value * scale[:, at]
                d = d * scale[:, at]
            hid_out[side, :, :, :, at] = value.astype(BF).reshape(shape)
            in_out[side, :, :, :, at] = (
                (d * u * (sig + act * (1.0 - sig))).astype(BF).reshape(shape)
            )
            in_out[side, :, :, :, up_at] = (d * act).astype(BF).reshape(shape)
        g_out[side] = sums.astype(BF).reshape(lines, 2, step_rows, 128)
        for copy in stores(k, side):
            copy.start()

    def z_start(k):
        for j, o in enumerate(others):
            z_copy(k, j, o).start()

    z_start(0)
    for k in range(chunks):
        x_copy(k, lines - 1, z, piece(k)).start()
        y_copy(k, lines - 1, z, piece(k)).start()

    fills = []
    for i, (begin, size) in enumerate(spans):
        for target, start, source in (
            (w_in, 0, e_gate.at[i] if i < local_experts else s_in.at[0]),
            (w_in, inner, e_up.at[i] if i < local_experts else s_in.at[1]),
            (w_down, 0, e_down.at[i] if i < local_experts else s_down),
        ):
            held = source.shape[0]
            fills.append(
                pltpu.make_async_copy(
                    source, target.at[pl.ds(start + begin, held)], w_sem.at[2 + len(fills)]
                )
            )
            fills[-1].start()
            if size > held:
                target[start + begin + held : start + begin + size] = jnp.zeros(
                    (size - held, width), BF
                )
    for copy in fills:
        copy.wait()
    keep = [
        pltpu.make_async_copy(w_in, w_in_out, w_sem.at[0]),
        pltpu.make_async_copy(w_down, w_down_out, w_sem.at[1]),
    ]
    for copy in keep:
        copy.start()

    own.wait()
    z_land(0)
    if chunks > 1:
        z_start(1)
    fetch(0, 0)
    valid = lambda k: (k >= 0) & (k < chunks)

    @pl.loop(0, chunks + 2)
    def _(t):
        @pl.loop(0, 4)
        def _(side):
            k = t - (side + 1) // 2

            @pl.when(valid(k))
            def _():
                @pl.when(k >= 1)
                def _():
                    for copy in stores(k - 1, side):
                        copy.wait()

                unit(k, side)

            @pl.when((side == 0) & valid(t - 1))
            def _():
                fetch(t - 1, 2)

            @pl.when((side == 1) & valid(t - 2))
            def _():
                fetch(t - 2, 3)

        @pl.when(valid(t + 1))
        def _():
            z_land(t + 1)

        @pl.when(valid(t + 2))
        def _():
            z_start(t + 2)

        @pl.when(valid(t))
        def _():
            xy_land(t)

        @pl.when(valid(t + 1))
        def _():
            fetch(t + 1, 0)

        @pl.when(valid(t - 1))
        def _():
            diag_land(t - 1)

        @pl.when(valid(t))
        def _():
            fetch(t, 1)

    for copy in keep:
        copy.wait()
    for side in range(4):
        for copy in stores(chunks - 1, side):
            copy.wait()

    @pl.loop(0, chunks)
    def _(k):
        for j, o in enumerate(others):
            z_copy(k, j, o).wait_send()
        for j, o in places:
            b = piece(k) if j == lines - 1 else block(o, y, x, k)
            x_copy(k, j, o, b).wait_send()
            y_copy(k, j, o, b).wait_send()
            diag_copy(k, j, o, 0).wait_send()
            diag_copy(k, j, o, 1).wait_send()
        for side in range(4):
            core_copy(k, side, c).wait_send()


def gather_hidden(
    value, cots, spread, e_gate, e_up, e_down, s_in, s_down, spans, local_experts, lines, ident
):
    rows, wide = value.shape
    width, early = e_down.shape[2], cots.shape[1]
    inner = spans[-1][0] + spans[-1][1]
    step_rows = min(rows, max(16, 128 // lines))
    chunks = rows // step_rows
    lead = (lines, 2, 2, 2, rows)
    dma = pltpu.SemaphoreType.DMA
    slot = lambda n: pltpu.VMEM((4, lines, 2, step_rows, n), BF)
    line = dma((chunks, lines))
    return pl.pallas_call(
        functools.partial(hidden_kernel, lines, chunks, spans, local_experts),
        out_shape=[
            jax.ShapeDtypeStruct(lead + (n,), BF) for n in (wide, inner, 2 * inner, 128)
        ]
        + [
            jax.ShapeDtypeStruct((2 * inner, width), BF),
            jax.ShapeDtypeStruct((inner, width), BF),
        ],
        in_specs=[HBM, HBM, VMEM] + [HBM] * 5,
        out_specs=[HBM] * 6,
        scratch_shapes=[
            slot(wide), slot(early), slot(inner), slot(2 * inner), slot(128),
            pltpu.VMEM((2 * inner, width), BF), pltpu.VMEM((inner, width), BF),
            dma((2 + 3 * len(spans),)), dma, dma((4,)), dma((4,)), dma((4, 3)),
            line, line, line, line, line, line,
            dma((chunks, lines, 2)), dma((chunks, lines, 2)), dma((chunks, 4)), dma((chunks, 4)),
        ],
        compiler_params=pltpu.CompilerParams(
            collective_id=ident, has_side_effects=True, vmem_limit_bytes=60 << 20
        ),
    )(value, cots.reshape(lead + (early,)), spread, e_gate, e_up, e_down, s_in, s_down)


def back_kernel(
    lines,
    hid, in_d, gate_g, w_in, w_down,
    out, parts,
    hid_in, d_in, g_in, part_out, sbuf, acc, cbuf, xbuf, ybuf, zbuf, xdiag, ydiag,
    ins, sts, cs, cr, xs, xr, ys, yr, zs, zr, xds, xdr, yds, ydr,
):
    me = Place()
    z, y, x, c = me.z, me.y, me.x, me.c
    rows, wide = out.shape
    width = wide - 128
    half = wide // 256 * 128
    others = [lax.rem(z + 1 + j, lines) for j in range(lines - 1)]
    to_x, to_y, to_c = me.at(x=1 - x), me.at(y=1 - y), me.at(c=1 - c)
    greet([me.at(z=o) for o in others] + [to_x, to_y, to_c])
    cols = (pl.ds(0, half), pl.ds(half, wide - half))
    lag = (0, 1, 1, 2)
    place = lambda n: lax.rem(z + 1 + n, lines)

    def side_of(side):
        return (
            lax.rem(y + 1 - side // 2, 2),
            lax.rem(x + 1 - lax.rem(side, 2), 2),
        )

    def loads(n, side):
        yy, xx = side_of(side)
        pairs = ((hid, hid_in), (in_d, d_in), (gate_g, g_in))
        return [
            pltpu.make_async_copy(ref.at[place(n), yy, xx], v.at[side], ins.at[side, i])
            for i, (ref, v) in enumerate(pairs)
        ]

    def store(n, side):
        yy, xx = side_of(side)
        return pltpu.make_async_copy(
            part_out.at[side], parts.at[place(n), yy, xx], sts.at[side]
        )

    def to_core(n, side):
        yy, xx = side_of(side)
        return remote(
            sbuf.at[side], cbuf.at[place(n), yy, xx], cs.at[side], cr.at[n, side], to_c
        )

    def unit(n, side):
        yy, xx = side_of(side)
        for copy in loads(n, side):
            copy.wait()
        inner = w_down.shape[0]
        grads = d_in[side].reshape(2 * rows, 2 * inner)
        value = hid_in[side].reshape(2 * rows, inner)
        piece = 512
        for begin in range(0, width, piece):
            at = slice(begin, begin + piece)
            back = jnp.dot(grads, w_in[:, at], preferred_element_type=F32).astype(BF).reshape(2, rows, piece)

            @pl.when(c == 0)
            def _():
                acc[place(n), yy, xx, :, at] = back[0]
                sbuf[side, :, at] = back[1]

            @pl.when(c == 1)
            def _():
                acc[place(n), yy, xx, :, at] = back[1]
                sbuf[side, :, at] = back[0]

            part_out[side, :, :, at] = (
                jnp.dot(value, w_down[:, at], preferred_element_type=F32)
                .astype(BF)
                .reshape(2, rows, piece)
            )
        acc[place(n), yy, xx, :, width:] = g_in[side, c]
        sbuf[side, :, width:] = g_in[side, 1 - c]

    def sums(target, *terms):
        @pl.loop(0, rows // 16)
        def _(i):
            at = pl.ds(pl.multiple_of(i * 16, 16), 16)
            total = terms[0][at].astype(F32)
            for term in terms[1:]:
                total = total + term[at].astype(F32)
            target[at] = total.astype(BF)

    def diag_sends(n):
        o = place(n)
        far = acc.at[o, 1 - y, 1 - x]
        return (
            remote(far.at[:, cols[0]], xdiag.at[o], xds.at[n], xdr.at[n], to_x),
            remote(far.at[:, cols[1]], ydiag.at[o], yds.at[n], ydr.at[n], to_y),
        )

    def side_sends(n):
        o = place(n)
        return (
            remote(acc.at[o, y, 1 - x], xbuf.at[o], xs.at[n], xr.at[n], to_x),
            remote(acc.at[o, 1 - y, x], ybuf.at[o], ys.at[n], yr.at[n], to_y),
        )

    def z_copy(n):
        return remote(
            acc.at[place(n), y, x], zbuf.at[z], zs.at[n], zr.at[z], me.at(z=place(n))
        )

    def first(n):
        to_core(n, 0).wait_recv()
        mine, other = acc.at[place(n), 1 - y, 1 - x], cbuf.at[place(n), 1 - y, 1 - x]
        sums(mine, mine, other)
        for copy in diag_sends(n):
            copy.start()

    def second(n):
        o = place(n)
        mine, other = acc.at[o, 1 - y, x], cbuf.at[o, 1 - y, x]
        to_core(n, 1).wait_recv()
        diag_sends(n)[0].wait_recv()
        sums(mine.at[:, cols[0]], mine.at[:, cols[0]], other.at[:, cols[0]], xdiag.at[o])
        sums(mine.at[:, cols[1]], mine.at[:, cols[1]], other.at[:, cols[1]])
        side_sends(n)[1].start()

    def third(n):
        o = place(n)
        mine, other = acc.at[o, y, 1 - x], cbuf.at[o, y, 1 - x]
        to_core(n, 2).wait_recv()
        diag_sends(n)[1].wait_recv()
        sums(mine.at[:, cols[0]], mine.at[:, cols[0]], other.at[:, cols[0]])
        sums(mine.at[:, cols[1]], mine.at[:, cols[1]], other.at[:, cols[1]], ydiag.at[o])
        side_sends(n)[0].start()

    def fourth(n):
        o = place(n)
        mine, other = acc.at[o, y, x], cbuf.at[o, y, x]
        to_core(n, 3).wait_recv()
        for copy in side_sends(n):
            copy.wait_recv()
        sums(mine, mine, other, xbuf.at[o], ybuf.at[o])

        @pl.when(n < lines - 1)
        def _():
            z_copy(n).start()

    valid = lambda n: (n >= 0) & (n < lines)
    for side in range(4):
        for copy in loads(0, side):
            copy.start()

    @pl.loop(0, lines + 3)
    def _(t):
        @pl.loop(0, 4)
        def _(side):
            n = t - (side + 1) // 2

            @pl.when(valid(n))
            def _():
                @pl.when(n >= 1)
                def _():
                    store(n - 1, side).wait()
                    to_core(n - 1, side).wait_send()

                unit(n, side)
                to_core(n, side).start()
                store(n, side).start()

                @pl.when(n + 1 < lines)
                def _():
                    for copy in loads(n + 1, side):
                        copy.start()

            for turn, (behind, act) in enumerate(((3, fourth), (0, first), (1, second), (1, third))):

                @pl.when((side == turn) & valid(t - behind))
                def _(behind=behind, act=act):
                    act(t - behind)

    for side in range(4):
        store(lines - 1, side).wait()
        to_core(lines - 1, side).wait_send()
    for o in others:
        remote(zbuf.at[o], zbuf.at[o], zs.at[0], zr.at[o], me.at(z=o)).wait_recv()

    @pl.loop(0, rows // 16)
    def _(i):
        at = pl.ds(pl.multiple_of(i * 16, 16), 16)
        total = acc[z, y, x, at].astype(F32)
        for o in others:
            total = total + zbuf[o, at].astype(F32)
        out[at] = total

    @pl.loop(0, lines)
    def _(n):
        for copy in diag_sends(n) + side_sends(n):
            copy.wait_send()

        @pl.when(n < lines - 1)
        def _():
            z_copy(n).wait_send()


def sum_back(hid, in_d, gate_g, w_in, w_down, ident):
    lines, rows, inner = hid.shape[0], hid.shape[4], hid.shape[5]
    width = w_in.shape[1]
    wide = width + 128
    half = wide // 256 * 128
    dma = pltpu.SemaphoreType.DMA
    buf = lambda *shape: pltpu.VMEM(shape, BF)
    line = dma((lines,))
    return pl.pallas_call(
        functools.partial(back_kernel, lines),
        out_shape=[
            jax.ShapeDtypeStruct((rows, wide), F32),
            jax.ShapeDtypeStruct((lines, 2, 2, 2, rows, width), BF),
        ],
        in_specs=[HBM] * 3 + [VMEM] * 2,
        out_specs=[VMEM, HBM],
        scratch_shapes=[
            buf(4, 2, rows, inner), buf(4, 2, rows, 2 * inner),
            buf(4, 2, rows, 128), buf(4, 2, rows, width), buf(4, rows, wide),
            buf(lines, 2, 2, rows, wide), buf(lines, 2, 2, rows, wide),
            buf(lines, rows, wide), buf(lines, rows, wide), buf(lines, rows, wide),
            buf(lines, rows, half), buf(lines, rows, wide - half),
            dma((4, 3)), dma((4,)), dma((4,)), dma((lines, 4)),
            line, line, line, line, line, line, line, line, line, line,
        ],
        compiler_params=pltpu.CompilerParams(
            collective_id=ident, has_side_effects=True, vmem_limit_bytes=62 << 20
        ),
    )(hid, in_d, gate_g, w_in, w_down)


def on_device(
    tokens,
    cotangent,
    norm1_gain,
    q_weight,
    kva_weight,
    kv_gain,
    kvb_weight,
    o_weight,
    norm2_gain,
    router_weight,
    shared_gate,
    shared_up,
    shared_down,
    expert_gate,
    expert_up,
    expert_down,
    expert_ids,
    token_rank,
    seq_ids,
):
    expert_count = lax.axis_size("expert")
    shard_count = lax.axis_size("shard")
    device_count = expert_count * shard_count
    expert_at = lax.axis_index("expert")
    shard_at = lax.axis_index("shard")
    tok_rows, width = tokens.shape
    group_len = seq_ids.shape[0]
    local_experts = expert_gate.shape[0]
    all_experts = local_experts * expert_count
    top_count = expert_ids.shape[1]
    capacity = max(2, tok_rows * top_count // all_experts)
    score_scale = (NOPE + ROPE) ** (-0.5)
    own_heads = HEADS // shard_count
    latent_width = kva_weight.shape[1]

    lines = expert_count // 2
    o_rows = o_weight.shape[0]
    o_pairs = VDIM == 2 * o_rows

    def by_head(weight):
        rows = weight.shape[0]
        heads = weight.reshape(rows, own_heads, 2, 2, weight.shape[1] // HEADS)
        return heads.transpose(3, 2, 0, 1, 4).reshape(2, 2, rows, weight.shape[1] // 4)

    small = [norm1_gain, norm2_gain, kv_gain, router_weight]
    small_sizes = [v.size for v in small]

    def pack(values):
        flat = jnp.concatenate(values, axis=-1)
        pad = -flat.shape[-1] % 2048
        flat = jnp.pad(flat, [(0, 0)] * (flat.ndim - 1) + [(0, pad)])
        return flat.reshape(flat.shape[:-1] + (-1, 128))

    def unpack(packed):
        flat = packed.reshape(packed.shape[:-2] + (-1,))
        starts = [sum(small_sizes[:i]) for i in range(len(small_sizes))]
        return [flat[..., b : b + n] for b, n in zip(starts, small_sizes)]

    small_own = pack([v.reshape(-1) for v in small])
    rounds = max(1, tok_rows * device_count // 4096)
    planes = [kva_weight]
    started = start_gather(
        tokens,
        planes,
        [1],
        [
            jnp.broadcast_to(small_own, (2, 2) + small_own.shape),
            by_head(kvb_weight),
            by_head(q_weight),
        ],
        o_weight if o_pairs else None,
        lines,
        1,
    )
    group_tokens = started[0].reshape(group_len, width)
    kva_all = started[1].reshape(width, latent_width)
    small_set, kvb_set, q_set, *o_set = started[1 + len(planes) :]
    small_all = unpack(small_set.reshape((device_count,) + small_own.shape))
    kvb_mine = kvb_set.reshape(KV_RANK, -1)
    q_mine = q_set.reshape(width, -1)
    core_at, x_at = shard_at % 2, shard_at // 2
    if o_pairs:
        o_mine = o_set[0].reshape(own_heads * VDIM, width)
    else:
        o_mine = gather(o_weight, BOTH).reshape(own_heads, 2, 2, VDIM, width)
        o_mine = o_mine[:, core_at, x_at].reshape(own_heads * VDIM, width)
    norm1_scale, norm2_scale, latent_scale = [v.reshape(-1).astype(F32) for v in small_all[:3]]
    router = small_all[3].reshape(width, all_experts)

    positions = positions_of(seq_ids)
    cosine_table, sine_table = rope_tables(positions, ROPE)
    token_index = jnp.arange(group_len, dtype=jnp.int32)
    allowed = (token_index[None, :] <= token_index[:, None]) & (
        (seq_ids[None, :] == 0) | (seq_ids[None, :] == seq_ids[:, None])
    )
    input_rows = tokens.astype(F32)
    group_rows = group_tokens.astype(F32)
    normed_group, _ = rms_forward(group_rows, norm1_scale)
    hidden_one = normed_group.astype(BF)
    query_raw = mm(hidden_one, q_mine).reshape(group_len, own_heads, NOPE + ROPE)
    q_nope = query_raw[:, :, :NOPE].astype(BF)
    q_rope = rotate(
        query_raw[:, :, NOPE:], cosine_table[:, None, :], sine_table[:, None, :]
    ).astype(BF)
    compressed = mm(hidden_one, kva_all)
    latent_norm, inverse_latent = rms_forward(compressed[:, :KV_RANK], latent_scale)
    latent = latent_norm.astype(BF)
    k_rope = rotate(compressed[:, KV_RANK:], cosine_table, sine_table).astype(BF)
    keyval = mm(latent, kvb_mine).astype(BF).reshape(group_len, own_heads, NOPE + VDIM)
    keys = keyval[:, :, :NOPE]
    values = keyval[:, :, NOPE:]
    scores = jnp.einsum("qhd,khd->hqk", q_nope, keys, preferred_element_type=F32)
    scores = scores + jnp.einsum("qhd,kd->hqk", q_rope, k_rope, preferred_element_type=F32)
    scores = jnp.where(allowed[None], scores * score_scale, NEGATIVE)
    top_score = jnp.max(scores, axis=-1, keepdims=True)
    log_total = top_score + jnp.log(jnp.sum(jnp.exp(scores - top_score), axis=-1, keepdims=True))
    soft_probs = jnp.exp(scores - log_total)
    prob_low = soft_probs.astype(BF)
    attended = (
        jnp.einsum("hqk,khd->qhd", prob_low, values, preferred_element_type=F32)
        .astype(BF)
        .reshape(group_len, own_heads * VDIM)
    )
    projected = sum_group(mm(attended, o_mine).astype(BF), 2)
    mixed = input_rows + projected

    normed_two, inverse_two = rms_forward(mixed, norm2_scale)
    hidden_two = normed_two.astype(BF)
    logits = mm(hidden_two, router)
    choice_hot = (
        expert_ids[:, :, None] == jnp.arange(all_experts, dtype=jnp.int32)[None, None, :]
    ).astype(F32)
    chosen = jnp.sum(choice_hot * logits[:, None, :], axis=-1)
    gate_probs = jax.nn.softmax(chosen, axis=-1)
    kept = kept_pairs(expert_ids, token_rank, choice_hot, capacity)
    gate_table = jnp.sum(choice_hot * (gate_probs * kept)[:, :, None], axis=1)

    shared_width = shared_down.shape[0]
    both_shared = jnp.stack([shared_gate, shared_up]).reshape(
        2, shared_gate.shape[0], device_count, shared_width
    )
    both_shared = lax.all_to_all(
        both_shared.transpose(2, 0, 1, 3), BOTH, split_axis=0, concat_axis=0
    )
    both_shared = both_shared.transpose(1, 0, 2, 3).reshape(2, width, shared_width)
    own_width = expert_gate.shape[2]
    sizes = [own_width + -own_width % 128] * local_experts + [shared_width + -shared_width % 128]
    spans = tuple((sum(sizes[:i]), size) for i, size in enumerate(sizes))

    spare = -shared_width % 128
    shared_in = jnp.pad(both_shared.swapaxes(1, 2), ((0, 0), (0, spare), (0, 0)))
    shared_out = jnp.pad(shared_down, ((0, spare), (0, 0)))
    unit_expert = jnp.concatenate(
        [jnp.full((size,), expert_at * local_experts + i) for i, size in enumerate(sizes[:-1])]
        + [jnp.full((sizes[-1],), -1)]
    )
    column = jnp.arange(128)[:, None]
    spread = (
        (column == unit_expert) | ((column == unit_expert + all_experts) & (unit_expert >= 0))
    ).astype(BF)

    early = width // 2

    def ffn(rows, cots, table):
        cots_all = gather(cots[:, :early] + 0 * group_tokens[0, 0], BOTH)
        high = table.astype(BF)
        low = (table - high.astype(F32)).astype(BF)
        spare = jnp.zeros((table.shape[0], 128 - 2 * all_experts), BF)
        values, hid, in_d, gate_g, w_in, w_down = gather_hidden(
            jnp.concatenate([rows, high, low, spare, cots[:, early:]], axis=1),
            cots_all,
            spread,
            expert_gate.swapaxes(1, 2),
            expert_up.swapaxes(1, 2),
            expert_down,
            shared_in,
            shared_out,
            spans,
            local_experts,
            lines,
            3,
        )
        back_sum, out_part = lax.optimization_barrier(
            sum_back(hid, in_d, gate_g, w_in, w_down, 4)
        )
        flat = lambda v: v.reshape(cots_all.shape[0], -1)
        work = [flat(values), cots_all, flat(in_d), flat(hid)]
        return scatter_sum(flat(out_part), BOTH), back_sum, work

    tail = spans[-1][0]
    inner = tail + spans[-1][1]
    expert_spans = tuple(span + (own_width,) for span in spans[:-1])
    shared_spans = (spans[-1] + (shared_width,),)
    if rounds == 1:
        out_sum, back_sum, work = ffn(hidden_two, cotangent, gate_table)
    else:

        def one_round(total, part):
            out_rows, back_rows, (values, cots, in_d, hid) = ffn(*part)
            rows = values[:, :width]
            cots = jnp.concatenate([cots, values[:, width + 128 :]], axis=1)
            grads = [mm_tn(in_d, rows), mm_tn(hid, cots)]
            return [t + g for t, g in zip(total, grads)], (out_rows, back_rows)

        in_rounds = lambda value: value.reshape((rounds, -1) + value.shape[1:])
        zeros = [jnp.zeros((2 * inner, width), F32), jnp.zeros((inner, width), F32)]
        (w_in_grad, w_down_grad), (out_sum, back_sum) = lax.scan(
            one_round, zeros, (in_rounds(hidden_two), in_rounds(cotangent), in_rounds(gate_table))
        )
        out_sum = out_sum.reshape((tok_rows,) + out_sum.shape[2:])
        back_sum = back_sum.reshape((tok_rows,) + back_sum.shape[2:])
        w_in_grad = w_in_grad.reshape(2, inner, width)
        cut = lambda grad: jnp.stack(
            [grad[spans[i][0] : spans[i][0] + own_width] for i in range(local_experts)]
        )
        expert_grads = [cut(w_in_grad[0]), cut(w_in_grad[1]), cut(w_down_grad)]
        shared_made = [v[tail : tail + shared_width] for v in (*w_in_grad, w_down_grad)]
        work = None
    out_sum, back_sum = out_sum.astype(F32), back_sum.astype(F32)
    output = (mixed + out_sum).astype(BF)

    upstream = cotangent.astype(F32)
    gate_grad = jnp.sum(
        choice_hot * back_sum[:, None, width : width + all_experts], axis=-1
    ) * kept
    chosen_grad = gate_probs * (gate_grad - jnp.sum(gate_probs * gate_grad, axis=-1, keepdims=True))
    logit_grad = jnp.sum(choice_hot * chosen_grad[:, :, None], axis=1).astype(BF)
    router_part = mm_tn(hidden_two, logit_grad)
    hidden_two_grad = back_sum[:, :width] + mm_nt(logit_grad, router)
    mixed_norm_grad, norm2_part = rms_backward(mixed, inverse_two, norm2_scale, hidden_two_grad)
    mixed_grad = upstream + mixed_norm_grad

    mixed_grad_group, *made = gather_group(mixed_grad.astype(BF), 5, work, shared_spans, lines)
    if work:
        shared_made = [v[0] for v in made]
    shared_grad = jnp.stack(shared_made[:2]).astype(BF)
    shared_grad = shared_grad.reshape(2, shared_width, device_count, -1).transpose(2, 0, 3, 1)
    shared_grad = lax.all_to_all(shared_grad, BOTH, split_axis=0, concat_axis=0)
    shared_grad = shared_grad.astype(F32).transpose(1, 2, 0, 3).reshape(
        2, width // device_count, device_count * shared_width
    )
    sdown_grad = shared_made[2]
    o_part = mm_tn(attended, mixed_grad_group)
    attended_grad = (
        mm_nt(mixed_grad_group, o_mine).astype(BF).reshape(group_len, own_heads, VDIM)
    )
    prob_grad = jnp.einsum("qhd,khd->hqk", attended_grad, values, preferred_element_type=F32)
    values_grad = jnp.einsum("hqk,qhd->khd", prob_low, attended_grad, preferred_element_type=F32)
    score_grad = (
        soft_probs * (prob_grad - jnp.sum(soft_probs * prob_grad, axis=-1, keepdims=True))
    ).astype(BF)
    q_nope_grad = (
        jnp.einsum("hqk,khd->qhd", score_grad, keys, preferred_element_type=F32) * score_scale
    )
    q_rope_grad = (
        jnp.einsum("hqk,kd->qhd", score_grad, k_rope, preferred_element_type=F32) * score_scale
    )
    keys_grad = (
        jnp.einsum("hqk,qhd->khd", score_grad, q_nope, preferred_element_type=F32) * score_scale
    )
    rope_grad = (
        jnp.einsum("hqk,qhd->kd", score_grad, q_rope, preferred_element_type=F32) * score_scale
    )
    keyval_grad = (
        jnp.concatenate([keys_grad, values_grad], axis=-1)
        .reshape(group_len, own_heads * (NOPE + VDIM))
        .astype(BF)
    )
    kvb_part = mm_tn(latent, keyval_grad)
    latent_part = jnp.concatenate([mm_nt(keyval_grad, kvb_mine), rope_grad], axis=1).astype(BF)
    latent_sum = sum_group(
        jnp.pad(latent_part, ((0, 0), (0, -latent_part.shape[1] % 128))), 6
    )[:, :latent_width]
    own_start = shard_at * tok_rows
    own_rows = lambda value: lax.dynamic_slice_in_dim(value, own_start, tok_rows)
    latent_raw_grad, kv_gain_part = rms_backward(
        own_rows(compressed[:, :KV_RANK]),
        own_rows(inverse_latent),
        latent_scale,
        latent_sum[:, :KV_RANK],
    )
    compressed_grad = jnp.concatenate(
        [
            latent_raw_grad,
            rotate(latent_sum[:, KV_RANK:], own_rows(cosine_table), -own_rows(sine_table)),
        ],
        axis=1,
    ).astype(BF)
    compressed_grad_group = gather_group(
        jnp.pad(compressed_grad, ((0, 0), (0, -latent_width % 128))), 7
    )[0][:, :latent_width]
    query_grad = jnp.concatenate(
        [q_nope_grad, rotate(q_rope_grad, cosine_table[:, None, :], -sine_table[:, None, :])],
        axis=-1,
    )
    query_grad = query_grad.reshape(group_len, own_heads * (NOPE + ROPE)).astype(BF)
    q_part = mm_tn(hidden_one, query_grad)
    kva_part = mm_tn(hidden_one, compressed_grad_group).astype(BF)
    kva_part = lax.dynamic_index_in_dim(
        kva_part.reshape(expert_count, shard_count, width // device_count, latent_width),
        shard_at,
        1,
        keepdims=False,
    )
    hidden_one_grad = sum_group(mm_nt(query_grad, q_mine).astype(BF), 8) + mm_nt(
        compressed_grad, kva_all
    )
    _, inverse_one = rms_forward(input_rows, norm1_scale)
    input_norm_grad, norm1_part = rms_backward(
        input_rows, inverse_one, norm1_scale, hidden_one_grad
    )
    tokens_grad = mixed_grad + input_norm_grad

    def from_heads(parts):
        rows = parts.shape[2]
        heads = parts.reshape(2, 2, rows, own_heads, -1).transpose(2, 3, 1, 0, 4)
        return heads.reshape(rows, -1).astype(F32)

    line_shape = (lines, 2)
    small_parts = pack(
        [v.reshape(device_count, -1) for v in (norm1_part, norm2_part, kv_gain_part, router_part)]
    )
    parts = [
        kvb_part.astype(BF).reshape(line_shape + (2, 2, kvb_weight.shape[0], -1)),
        kva_part.reshape(line_shape + (width // device_count, latent_width)),
        q_part.astype(BF).reshape(line_shape + (2, 2, q_weight.shape[0], q_mine.shape[1])),
        small_parts.reshape(line_shape + (2, 2) + small_parts.shape[1:]),
    ]
    o_part = o_part.astype(BF).reshape(own_heads, VDIM, width)
    if o_pairs:
        o_sum = o_part.reshape(own_heads, 2, o_rows, width)
    else:
        o_sum = None
        o_wide = jnp.zeros((own_heads, 2, 2, VDIM, width), BF).at[:, core_at, x_at].set(o_part)
        o_grad = scatter_sum(o_wide.reshape(HEADS * VDIM, width), BOTH).astype(F32)
    summed = sum_grads(
        parts, (True, False, True, True), o_sum, lines, 9, work, expert_spans
    )
    if work:
        expert_grads = summed[-3:]
    kvb_grad = from_heads(summed[0])
    kva_grad = summed[1].astype(F32)
    q_grad = from_heads(summed[2])
    norm1_grad, norm2_grad, kv_gain_grad, router_grad = unpack(jnp.sum(summed[3], axis=(0, 1)))
    router_grad = router_grad.reshape(router_weight.shape)
    if o_pairs:
        o_grad = summed[4].astype(F32)
    return (
        output,
        tokens_grad,
        norm1_grad,
        q_grad,
        kva_grad,
        kv_gain_grad,
        kvb_grad,
        o_grad,
        norm2_grad,
        router_grad,
        shared_grad[0],
        shared_grad[1],
        sdown_grad,
        expert_grads[0].swapaxes(1, 2),
        expert_grads[1].swapaxes(1, 2),
        expert_grads[2],
    )


def solution(mesh):
    rows = P(BOTH, None)
    flat = P(BOTH)
    columns = P("expert", None, "shard")
    depth = P("expert", "shard", None)
    return jax.shard_map(
        on_device,
        mesh=mesh,
        in_specs=(
            rows,
            rows,
            flat,
            rows,
            rows,
            flat,
            rows,
            rows,
            flat,
            rows,
            rows,
            rows,
            rows,
            columns,
            columns,
            depth,
            rows,
            flat,
            P("expert"),
        ),
        out_specs=(
            rows,
            rows,
            flat,
            rows,
            rows,
            flat,
            rows,
            rows,
            flat,
            rows,
            rows,
            rows,
            rows,
            columns,
            columns,
            depth,
        ),
        check_vma=False,
    )
```

time: 1040 us -> 801 us (0.77)
  matrix products: 267 us -> 42 us
  local copies, waits for them, and re-layouts: 133 us -> 97.4 us
  other arithmetic: 56.5 us -> 27.8 us
  Pallas kernels: 536 us -> 563 us
  waiting for transfers between devices: 0.71 us -> 19 us
    dot_general x8 -> x5, matrix products: 100 us -> 10.2 us  [mm_nt(): lax.dot_general(a, b, (((1,), (1,)), ((), ())), preferred_element_type=F32)]
    dot_general x8 -> x5, matrix products: 83.2 us -> 8.53 us  [mm(): return jnp.dot(a, b, preferred_element_type=F32)]
    dot_general x8 -> x5, matrix products: 75.3 us -> 15.8 us  [mm_tn(): lax.dot_general(a, b, (((0,), (0,)), ((), ())), preferred_element_type=F32)]
    pallas_call x1, Pallas kernels: 91.3 us -> 127 us  [sum_grads(): pl.pallas_call(functools.partial(grads_kernel, lines, tuple(kinds), with_...]
    pallas_call x5, Pallas kernels: 406 us -> 375 us  [the longest x1 133 us: gather_hidden(): pl.pallas_call(functools.partial(hidden_kernel, lines, chunks, spans, loc...]
    concatenate x3 -> x1, local copies, waits for them, and re-layouts: 23.4 us -> 1.06 us  [ffn(): jnp.concatenate([rows, high, low, spare, cots[:, early:]], axis=1)]
    pallas_call x3, Pallas kernels: 38.9 us -> 60.1 us  [sum_group(): pl.pallas_call(functools.partial(sum_group_kernel, cuts), out_shape=jax.S...]
    all_gather x1, waiting for transfers between devices: 0.01 us -> 19 us  [gather(): return lax.all_gather(value, axes, axis=0, tiled=True)]
  transfers between devices with their start and end apart: 4 -> 4, of which waited for: 0 -> 1; matrix products, arithmetic and copies ran while one was open for 35% -> 16% of each run, Pallas kernels for 52% -> 29%
where the time goes in v3:
time: 801 us; the launch traced here: 790 us
  Pallas kernels  563 us (70%)
  local copies, waits for them, and re-layouts  97.4 us (12%)
  matrix products  42 us (5%)
  other arithmetic  27.8 us (3%)
  starting transfers between devices  24.4 us (3%)
  waiting for transfers between devices  19 us (2%)
  between operations  16.3 us (2%)
    pallas_call x1, Pallas kernels, gather_hidden(): pl.pallas_call(functools.partial(hidden_kernel, lines, chunks, spans, loc...  133 us
    pallas_call x1, Pallas kernels, sum_grads(): pl.pallas_call(functools.partial(grads_kernel, lines, tuple(kinds), with_...  127 us
    pallas_call x1, Pallas kernels, sum_back(): pl.pallas_call(functools.partial(back_kernel, lines), out_shape=[jax.Shap...  106 us
    pallas_call x1, Pallas kernels, start_gather(): pl.pallas_call(functools.partial(start_kernel, lines, tuple(counts), with...  96.8 us
    pallas_call x3, Pallas kernels, sum_group(): pl.pallas_call(functools.partial(sum_group_kernel, cuts), out_shape=jax.S...  60.1 us
    pallas_call x2, Pallas kernels, gather_group(): pl.pallas_call(functools.partial(gather_group_kernel, cuts, spans if work...  39.8 us
    unnamed x157, local copies, waits for them, and re-layouts  32.6 us
    all_gather x1, waiting for transfers between devices, gather(): return lax.all_gather(value, axes, axis=0, tiled=True)  19 us
  transfers between devices with their start and end apart: 4, of which 1 were waited for; matrix products, arithmetic and copies ran while one was open for 16% of the time, Pallas kernels for 29%

profile of v3, /device:TPU:0, one launch (start us, length us, event | category | flops | bytes accessed | tf_op | source)
XLA Modules:
  0.0 789.5 jit_solution(4228685225072540056)
XLA Ops:
  8.2 2.1 concatenate.46
  12.0 1.6 reshape.624
  13.9 1.2 reshape.625.refs_4_
  15.7 96.8 %shard_map.306 = (bf16[2,2,128,2048]{3,2,1,0:T(8,128)(2,1)}, bf16[4,2,2,2,64,576]{5,4,3,2,1,0:T(8,128)(2,1)}, bf16[4,2,2,2,16,128]{5,4,3,2,1,0:T(8,128)(2,1)}, b...) custom-call(bf16[128,2048]{1,0:T(8,128)(2,1)} %refs_0_.1, ...), custom_call_target="tpu_custom_call" | custom-call | tf_op jit(solution)/shard_map/pallas_call | solution.py:528
  115.2 1.3 stack.16
  116.5 1.3 stack.17
  118.0 1.4 copy.281
  119.4 15.6 %all-to-all-start = ((bf16[32,2,64,88]{3,2,1,0:T(8,128)(2,1)}), bf16[32,2,64,88]{3,2,1,0:T(8,128)(2,1)}, u32[]{:S(2)}, u32[]{:S(2)}) async-start(bf16[32,2,64,88]{3,2,1,0:T(8,128)(2,1)} %copy.281), calls=%async_computation | async-start | bytes 2097152 | tf_op jit(solution)/shard_map/all_to_all | solution.py:1445
  138.8 1.4 copy-done.21
  140.3 1.8 fusion.62
  142.1 2.1 fusion.35
  147.4 1.4 convolution_convert_fusion.6
  150.4 4.9 copy.268
  156.3 3.7 fusion.63
  161.3 1.3 fusion.61
  164.6 1.3 copy-done.69
  165.8 1.3 convolution_convert_fusion.4
  167.2 15.8 %shard_map.307 = f32[128,2048]{1,0:T(8,128)S(1)} custom-call(bf16[2,2,128,2048]{3,2,1,0:T(8,128)(2,1)S(1)} %bitcast.159), custom_call_target="tpu_custom_call" | custom-call | tf_op jit(solution)/shard_map/pallas_call | solution.py:260
  188.8 1.3 copy.282
  190.1 1.2 copy.283
  191.3 2.2 pad.25.s_in
  193.5 19.0 %all-gather.2.cloned.1.call-done.refs_2_.refs_6_ = bf16[4096,1024]{1,0:T(8,128)(2,1)} async-done(((bf16[128,1024]{1,0:T(8,128)(2,1)}), bf16[4096,1024]{1,0:T(8,128)(2,1)}) %all-gather.2.cloned.1.call-update) | async-done | bytes 8388624 | tf_op jit(solution)/shard_map/all_gather | solution.py:96
  212.5 133.2 %shard_map.308 = (bf16[4,2,2,2,128,3200]{5,4,3,2,1,0:T(8,128)(2,1)}, bf16[4,2,2,2,128,896]{5,4,3,2,1,0:T(8,128)(2,1)}, bf16[4,2,2,2,128,1792]{5,4,3,2,1,0:T(8,12...) custom-call(bf16[128,3200]{1,0:T(8,128)(2,1)} %concatenate.49.src, ...), custom_call_target="tpu_custom_call" | custom-call | tf_op jit(solution)/shard_map/pallas_call | solution.py:1050
  345.8 105.7 %shard_map.309 = (f32[128,2176]{1,0:T(8,128)}, bf16[4,2,2,2,128,2048]{5,4,3,2,1,0:T(8,128)(2,1)}) custom-call(bf16[4,2,2,2,128,896]{5,4,3,2,1,0:T(8,128)(2,1)} %get-tuple-element.48.hid, bf16[4,2,2,2,128,1792]{5,4,3,2,1,0:T(8,128)(2,1)} %get-tuple-element.49.in_d, bf16[4,2,2,2,128,128]{5,4,3,2,1,0:T(8,128)(2,1)} %get-tuple-element.50.gate_g, ...), custom_call_target="tpu_custom_call" | custom-call | tf_op jit(solution)/shard_map/pallas_call | solution.py:1280
  453.7 1.9 multiply_reduce_fusion.1
  455.7 1.3 fusion.65
  457.0 2.5 reshape.655
  459.6 1.4 fusion.56.refs_0_
  461.0 3.1 copy-done
  464.0 27.1 %shard_map.310 = (bf16[2,2,128,2048]{3,2,1,0:T(8,128)(2,1)S(1)}, f32[1,88,2048]{2,1,0:T(8,128)S(1)}, f32[1,88,2048]{2,1,0:T(8,128)S(1)}, f32[1,88,2048]{2,1,0:T(8,128)S(1)}) custom-call(bf16[128,2048]{1,0:T(8,128)(2,1)S(1)} %fusion.56.refs_0_, bf16[4096,3200]{1,0:T(8,128)(2,1)} %bitcast.166, bf16[4096,1024]{1,0:T(8,128)(2,1)} %all-gather.2.cloned.1.call-done.refs_2_.refs_6_, ...), custom_call_target="tpu_custom_call" | custom-call | tf_op jit(solution)/shard_map/pallas_call | solution.py:200
  491.2 1.4 copy-done.1
  493.3 1.3 copy.300
  495.4 1.3 copy.301
  498.0 8.8 %all-to-all-start.1 = ((bf16[32,2,64,88]{3,2,1,0:T(8,128)(2,1)}), bf16[32,2,64,88]{3,2,1,0:T(8,128)(2,1)}, u32[]{:S(2)}, u32[]{:S(2)}) async-start(bf16[32,2,64,88]{3,2,1,0:T(8,128)(2,1)} %copy.302), calls=%async_computation.2 | async-start | bytes 2097152 | tf_op jit(solution)/shard_map/all_to_all | solution.py:1541
  506.7 3.7 convolution_convert_fusion.7
  511.4 1.2 multiply_convert_fusion.1
  515.8 1.8 convolution_convert_fusion.3
  517.6 30.4 %shard_map.311 = f32[128,2048]{1,0:T(8,128)S(1)} custom-call(bf16[2,2,128,2048]{3,2,1,0:T(8,128)(2,1)S(1)} %bitcast.158), custom_call_target="tpu_custom_call" | custom-call | tf_op jit(solution)/shard_map/pallas_call | solution.py:260
  553.0 2.2 copy.324
  555.2 1.3 pad.27.clone
  556.5 13.9 %shard_map.312 = f32[128,640]{1,0:T(8,128)S(1)} custom-call(bf16[2,2,128,640]{3,2,1,0:T(8,128)(2,1)S(1)} %bitcast.157), custom_call_target="tpu_custom_call" | custom-call | tf_op jit(solution)/shard_map/pallas_call | solution.py:260
  573.8 2.0 fusion.23
  575.9 12.6 %shard_map.313 = bf16[2,2,128,640]{3,2,1,0:T(8,128)(2,1)S(1)} custom-call(bf16[128,640]{1,0:T(8,128)(2,1)S(1)} %pad.28.refs_0_), custom_call_target="tpu_custom_call" | custom-call | tf_op jit(solution)/shard_map/pallas_call | solution.py:200
  588.7 3.6 convolution_convert_fusion.5
  592.3 3.0 convolution_convert_fusion.1
  596.1 4.4 copy.296
  600.5 2.0 constant_dynamic-slice_fusion
  602.5 4.3 convolution_convert_fusion.2
  606.8 3.5 convolution_convert_fusion
  610.4 127.0 %shard_map.314 = (bf16[2,2,16,1024]{3,2,1,0:T(8,128)(2,1)}, bf16[64,576]{1,0:T(8,128)(2,1)}, bf16[2,2,64,768]{3,2,1,0:T(8,128)(2,1)}, f32[2,2,16,128]{3,2,1,0:T(...) custom-call(bf16[4,2,2,2,16,1024]{5,4,3,2,1,0:T(8,128)(2,1)} %bitcas, ...), custom_call_target="tpu_custom_call" | custom-call | tf_op jit(solution)/shard_map/pallas_call | solution.py:783
  739.5 1.6 convert_element_type.269
  743.2 1.8 convert_element_type.274
  745.0 1.7 reshape.662
  746.7 2.0 copy.298
  748.7 1.9 reshape.660
  751.3 1.5 convert_bitcast_fusion
  753.9 1.6 copy.304
  755.5 2.7 squeeze.17
  758.2 2.8 copy.303
  761.0 2.7 squeeze.16
  763.7 3.3 fusion.22
  767.9 6.0 copy.342
  773.9 6.0 copy.343
  779.9 2.5 copy.344
  (269 shorter events, 49.2 us)
Async XLA Ops:
  7.2 107.1 %copy-start.14 = (bf16[128,2048]{1,0:T(8,128)(2,1)S(1)}, bf16[128,2048]{1,0:T(8,128)(2,1)}, u32[]{:S(2)}) copy-start(bf16[128,2048]{1,0:T(8,128)(2,1)} %param.20) | copy-start | bytes 1572868
  7.2 205.4 %all-gather.2.cloned.1.call-start = ((), (), s32[]{:S(2)}) async-start(), calls=%async_computation.3 | async-start | bytes 8650752 | tf_op jit(solution)/shard_map/all_gather | solution.py:96
  12.0 103.2 %copy-start.46 = (bf16[64,2816]{1,0:T(8,128)(2,1)S(1)}, bf16[64,2816]{1,0:T(8,128)(2,1)}, u32[]{:S(2)}) copy-start(bf16[64,2816]{1,0:T(8,128)(2,1)} %param.29) | copy-start | bytes 1081348
  13.7 102.8 %copy-start.47 = (bf16[64,2816]{1,0:T(8,128)(2,1)S(1)}, bf16[64,2816]{1,0:T(8,128)(2,1)}, u32[]{:S(2)}) copy-start(bf16[64,2816]{1,0:T(8,128)(2,1)} %param.30) | copy-start | bytes 1081348
  118.0 17.0 %copy-start.50 = (bf16[4,2,2,2,16,128]{5,4,3,2,1,0:T(8,128)(2,1)S(1)}, bf16[4,2,2,2,16,128]{5,4,3,2,1,0:T(8,128)(2,1)}, u32[]{:S(2)}) copy-start(bf16[4,2,2,2,16,128]{5,4,3,2,1,0:T(8,128)(2,1)} %get-tuple-element.43) | copy-start | bytes 393220
  118.0 19.3 %copy-start.52 = (s32[512]{0:T(512)S(1)}, s32[512]{0:T(512)}, u32[]{:S(2)}) copy-start(s32[512]{0:T(512)} %param.37) | copy-start | bytes 6148
  118.0 19.6 %copy-start.9 = (bf16[2,2,128,2048]{3,2,1,0:T(8,128)(2,1)S(1)}, bf16[2,2,128,2048]{3,2,1,0:T(8,128)(2,1)}, u32[]{:S(2)}) copy-start(bf16[2,2,128,2048]{3,2,1,0:T(8,128)(2,1)} %get-tuple-element.42) | copy-start | bytes 6291460
  119.4 69.4 %all-to-all-start = ((bf16[32,2,64,88]{3,2,1,0:T(8,128)(2,1)}), bf16[32,2,64,88]{3,2,1,0:T(8,128)(2,1)}, u32[]{:S(2)}, u32[]{:S(2)}) async-start(bf16[32,2,64,88]{3,2,1,0:T(8,128)(2,1)} %copy.281), calls=%async_computation | async-start | bytes 2097152 | tf_op jit(solution)/shard_map/all_to_all | solution.py:1445
  135.0 628.7 %reduce-scatter.2.cloned.1.call-start = ((), (), s32[]{:S(2)}) async-start(), calls=%async_computation.4 | async-start | bytes 17301504 | tf_op jit(solution)/shard_map/reduce_scatter | solution.py:100
  138.2 2.1 copy-start.21
  138.8 3.2 copy-start.23
  142.1 6.8 copy-start.4
  142.1 5.3 copy-start.34
  144.2 2.7 copy-start.26
  144.2 2.7 copy-start.27
  150.0 10.2 %copy-start.15 = (bf16[512,4,128]{2,1,0:T(4,128)(2,1)}, bf16[512,4,128]{2,1,0:T(4,128)(2,1)S(1)}, u32[]{:S(2)}) copy-start(bf16[512,4,128]{2,1,0:T(4,128)(2,1)S(1)} %get-tuple-element.186) | copy-start | bytes 1572868
  150.3 12.8 %copy-start.11 = (bf16[512,4,128]{0,2,1:T(8,128)(2,1)}, bf16[512,4,128]{0,2,1:T(8,128)(2,1)S(1)}, u32[]{:S(2)}) copy-start(bf16[512,4,128]{0,2,1:T(8,128)(2,1)S(1)} %copy.322) | copy-start | bytes 1572868
  150.4 4.9 copy-start.53
  150.4 5.9 copy-start.24
  156.3 3.8 copy-start.40
  156.3 3.8 copy-start.49
  160.1 1.1 copy-start.17
  160.2 1.1 copy-start.32
  162.6 2.0 copy-start.2
  163.2 2.6 copy-start.69
  164.6 2.6 copy-start.42
  167.1 15.8 %copy-start.7 = (bf16[128,2048]{1,0:T(8,128)(2,1)S(1)}, bf16[128,2048]{1,0:T(8,128)(2,1)}, u32[]{:S(2)}) copy-start(bf16[128,2048]{1,0:T(8,128)(2,1)} %refs_0_.1) | copy-start | bytes 1572868
  182.9 1.1 copy-start.13
  183.0 1.5 copy-start.51
  183.0 1.8 copy-start.70
  183.0 3.0 copy-start.48
  183.8 3.1 copy-start.37
  451.5 2.1 copy-start.58
  451.5 2.1 copy-start.59
  451.5 2.1 copy-start.65
  451.5 2.1 copy-start.61
  453.7 5.9 copy-start.68
  455.6 5.3 copy-start.5
  459.5 31.6 %copy-start.66 = (f32[128]{0:T(128)}, f32[128]{0:T(128)S(1)}, u32[]{:S(2)}) copy-start(f32[128]{0:T(128)S(1)} %get-tuple-element.213) | copy-start | bytes 1540
  460.9 3.1 copy-start
  491.2 1.4 copy-start.1
  498.0 253.3 %all-to-all-start.1 = ((bf16[32,2,64,88]{3,2,1,0:T(8,128)(2,1)}), bf16[32,2,64,88]{3,2,1,0:T(8,128)(2,1)}, u32[]{:S(2)}, u32[]{:S(2)}) async-start(bf16[32,2,64,88]{3,2,1,0:T(8,128)(2,1)} %copy.302), calls=%async_computation.2 | async-start | bytes 2097152 | tf_op jit(solution)/shard_map/all_to_all | solution.py:1541
  506.7 3.7 copy-start.3
  506.7 3.7 copy-start.12
  511.4 1.2 copy-start.29
  512.7 1.1 copy-start.16
  513.5 2.3 copy-start.20
  517.6 30.5 %copy-start.18 = (f32[512,4,192]{0,2,1:T(8,128)S(1)}, f32[512,4,192]{0,2,1:T(8,128)}, u32[]{:S(2)}) copy-start(f32[512,4,192]{0,2,1:T(8,128)} %copy-done.17) | copy-start | bytes 4718596
  549.8 1.6 copy-start.35
  549.9 2.2 copy-start.19
  552.1 18.3 %copy-start.54 = (f32[512]{0:T(512)S(1)}, f32[512]{0:T(512)}, u32[]{:S(2)}) copy-start(f32[512]{0:T(512)} %reshape.658) | copy-start | bytes 6148
  555.2 18.6 %copy-start.8 = (bf16[128,2048]{1,0:T(8,128)(2,1)S(1)}, bf16[128,2048]{1,0:T(8,128)(2,1)}, u32[]{:S(2)}) copy-start(bf16[128,2048]{1,0:T(8,128)(2,1)} %refs_0_.1) | copy-start | bytes 1572868
  555.2 18.6 %copy-start.22 = (bf16[4,2,2,2,64,576]{5,4,3,2,1,0:T(8,128)(2,1)S(1)}, bf16[4,2,2,2,64,576]{5,4,3,2,1,0:T(8,128)(2,1)}, u32[]{:S(2)}) copy-start(bf16[4,2,2,2,64,576]{5,4,3,2,1,0:T(8,128)(2,1)} %get-tuple-element.44) | copy-start | bytes 7077892
  573.8 14.8 %copy-start.44 = (f32[32,1024]{1,0:T(8,128)S(1)}, f32[32,1024]{1,0:T(8,128)}, u32[]{:S(2)}) copy-start(f32[32,1024]{1,0:T(8,128)} %reshape.655) | copy-start | bytes 393220
  575.8 16.6 %copy-start.63 = (f32[2,2,128]{2,1,0:T(2,128)S(1)}, f32[2,2,128]{2,1,0:T(2,128)}, u32[]{:S(2)}) copy-start(f32[2,2,128]{2,1,0:T(2,128)} %copy-done.62) | copy-start | bytes 6148
  588.7 3.6 copy-start.10
  596.1 6.4 copy-start.43
  602.5 4.3 copy-start.25
  602.5 4.3 copy-start.39
  737.4 7.6 copy-start.45
  755.5 8.2 %copy-start.6 = (f32[128,2048]{1,0:T(8,128)S(1)}, f32[128,2048]{1,0:T(8,128)}, u32[]{:S(2)}) copy-start(f32[128,2048]{1,0:T(8,128)} %copy-done.5) | copy-start | bytes 3145732
  755.5 8.2 %copy-start.67 = (f32[128]{0:T(128)S(1)}, f32[128]{0:T(128)}, u32[]{:S(2)}) copy-start(f32[128]{0:T(128)} %copy-done.66) | copy-start | bytes 1540
  767.9 12.0 %slice-start = ((s8[5767168]{0:T(1024)(128)(4,1)}), s8[4194304]{0:T(1024)(128)(4,1)S(1)}, s32[]{:S(2)}) async-start(s8[5767168]{0:T(1024)(128)(4,1)} %bitcast.172), calls=%async_computation.5 | async-start | bytes 8388608
  773.9 6.0 slice-start.1
  (13 other events, 11.3 us)
Sparse Core Ops, SparseCore 0:
  115.3 97.1 all-gather.1
  451.7 232.6 reduce-scatter.1

commit v4 on v3

--- a/solution.py
+++ b/solution.py
@@ -272,18 +272,32 @@
     )(part.reshape(2, 2, rows, width))
 
 
-def add_blocks(target, one, two):
+def rows_loop(target, act):
     if len(target.shape) > 2:
         for i in range(target.shape[0]):
-            add_blocks(target.at[i], one.at[i], two.at[i])
+            rows_loop(target.at[i], lambda at, i=i: act((i,) + at))
         return
     rows = target.shape[0]
     step = 16 if rows % 16 == 0 else rows
 
     @pl.loop(0, rows // step)
     def _(i):
-        at = pl.ds(pl.multiple_of(i * step, step), step)
+        act((pl.ds(pl.multiple_of(i * step, step), step),))
+
+
+def add_blocks(target, one, two):
+    def act(at):
         target[at] = (one[at].astype(F32) + two[at].astype(F32)).astype(target.dtype)
+
+    rows_loop(target, act)
+
+
+def add_three(target, one, two, three):
+    def act(at):
+        total = one[at].astype(F32) + two[at].astype(F32) + three[at].astype(F32)
+        target[at] = total.astype(target.dtype)
+
+    rows_loop(target, act)
 
 
 class Copies:
@@ -609,49 +623,72 @@
     return shapes, buffers
 
 
-def grads_kernel(lines, kinds, with_o, spans, *refs):
-    jobs = len(kinds)
+def grads_kernel(lines, plane, with_o, spans, *refs):
+    jobs = 4
+    refs = list(refs)
     take = lambda n: [refs.pop(0) for _ in range(n)]
-    refs = list(refs)
     parts = take(jobs)
+    (rows_part,) = take(1)
     o_part = take(1)[0] if with_o else None
     work = take(4) if spans else None
     outs = take(jobs)
+    (rows_out,) = take(1)
     o_out = take(1)[0] if with_o else None
     made = take(3) if spans else None
     ybufs, zbufs, tots = take(jobs), take(jobs), take(jobs)
+    p_own, p_core, p_x, r_own, r_core, r_x = take(6)
+    ys, yr, zs, zr, gs, gr, ls, ss, sr = take(9)
     if with_o:
-        o_ybuf, o_zbuf, o_tot = take(3)
-    ys, yr, zs, zr, gs, gr = take(6)
-    if with_o:
-        oys, oyr, ozs, ozr, ocs, ocr = take(6)
+        o_ybuf, o_zbuf, o_tot, oys, oyr, ozs, ozr, ocs, ocr = take(9)
     if spans:
         rows_in, cots_in, left_in, ins = take(4)
-    accs, o_acc = ybufs, (o_ybuf if with_o else None)
     me = Place()
     z, y, x, c = me.z, me.y, me.x, me.c
     others = [lax.rem(z + 1 + j, lines) for j in range(lines - 1)]
+    places = list(enumerate(others)) + [(lines - 1, z)]
     near = [(x, 1 - c), (1 - x, c), (1 - x, 1 - c)]
     to_near = [me.at(x=xx, c=cc) for xx, cc in near]
-    to_y, to_c = me.at(y=1 - y), to_near[0]
+    to_y, to_x, to_c = me.at(y=1 - y), to_near[1], to_near[0]
     greet([me.at(z=o) for o in others] + [to_y] + to_near)
     copies = Copies()
     go = copies.go
-    over_y = lambda i, j, o: remote(
-        parts[i].at[o, 1 - y], ybufs[i].at[o], ys.at[i, j], yr.at[i, o], to_y
-    )
-    over_z = lambda i, j, o: remote(
-        accs[i].at[o], zbufs[i].at[z], zs.at[i, j], zr.at[i, z], me.at(z=o)
-    )
-    places = list(enumerate(others)) + [(lines - 1, z)]
+    plain = [i for i in range(jobs) if i != plane]
+
+    group = (
+        (parts[plane], p_own, p_core, p_x, lambda ref, xx, cc: ref.at[:, :, xx, cc]),
+        (rows_part, r_own, r_core, r_x, lambda ref, xx, cc: ref.at[xx, cc]),
+    )
+    core_copy = lambda i, far: remote(
+        group[i][4](group[i][0], 1 - x if far else x, 1 - c),
+        group[i][2].at[far],
+        ss.at[i, far],
+        sr.at[i, far],
+        to_c,
+    )
+    own_copy = lambda i, far: pltpu.make_async_copy(
+        group[i][4](group[i][0], 1 - x if far else x, c), group[i][1].at[far], ls.at[i, far]
+    )
+    x_copy = lambda i: remote(group[i][1].at[1], group[i][3], ss.at[i, 2], sr.at[i, 2], to_x)
+    for far in (1, 0):
+        for i in range(2):
+            go(core_copy(i, far))
+            own_copy(i, far).start()
+
+    def over_y(i, j, o):
+        source = p_own.at[0, o, 1 - y] if i == plane else parts[i].at[o, 1 - y]
+        return remote(source, ybufs[i].at[o], ys.at[i, j], yr.at[i, o], to_y)
+
+    def over_z(i, j, o):
+        return remote(ybufs[i].at[o], zbufs[i].at[z], zs.at[i, j], zr.at[i, z], me.at(z=o))
+
     if with_o:
         holder = c == y
         o_over_y = lambda j, o: remote(o_part.at[o], o_ybuf.at[o], oys.at[j], oyr.at[o], to_y)
         o_over_z = lambda j, o: remote(
-            o_acc.at[o], o_zbuf.at[z], ozs.at[j], ozr.at[z], me.at(z=o)
+            o_ybuf.at[o], o_zbuf.at[z], ozs.at[j], ozr.at[z], me.at(z=o)
         )
     for j, o in places:
-        for i in range(jobs):
+        for i in plain:
             go(over_y(i, j, o))
         if with_o:
 
@@ -672,10 +709,34 @@
             def _(n):
                 work_turn(j * per_line + n)
 
+        @pl.when(j == 0)
+        def _():
+            for i in range(2):
+                core_copy(i, 1).wait_recv()
+                own_copy(i, 1).wait()
+                add_blocks(group[i][1].at[1], group[i][1].at[1], group[i][2].at[1])
+                x_copy(i).start()
+
+        @pl.when(j == 1)
+        def _():
+            core_copy(0, 0).wait_recv()
+            own_copy(0, 0).wait()
+            x_copy(0).wait_recv()
+            add_three(p_own.at[0], p_own.at[0], p_core.at[0], p_x)
+            for k, o in places:
+                over_y(plane, k, o).start()
+
+        @pl.when(j == 2)
+        def _():
+            core_copy(1, 0).wait_recv()
+            own_copy(1, 0).wait()
+            x_copy(1).wait_recv()
+            add_three(rows_out, r_own.at[0], r_core.at[0], r_x)
+
         o = lax.rem(z + 1 + j, lines)
-        for i in range(jobs):
-            remote(ybufs[i].at[o], ybufs[i].at[o], ys.at[i, j], yr.at[i, o], to_y).wait_recv()
-            add_blocks(accs[i].at[o], parts[i].at[o, y], ybufs[i].at[o])
+        for i in plain:
+            over_y(i, j, o).wait_recv()
+            add_blocks(ybufs[i].at[o], parts[i].at[o, y], ybufs[i].at[o])
 
             @pl.when(j < lines - 1)
             def _(i=i):
@@ -685,12 +746,18 @@
 
             @pl.when(holder)
             def _():
-                remote(o_ybuf.at[o], o_ybuf.at[o], oys.at[j], oyr.at[o], to_y).wait_recv()
-                add_blocks(o_acc.at[o], o_part.at[o], o_ybuf.at[o])
+                o_over_y(j, o).wait_recv()
+                add_blocks(o_ybuf.at[o], o_part.at[o], o_ybuf.at[o])
 
                 @pl.when(j < lines - 1)
                 def _():
                     o_over_z(j, o).start()
+
+    for j, o in places:
+        over_y(plane, j, o).wait_recv()
+        add_blocks(ybufs[plane].at[o], p_own.at[0, o, y], ybufs[plane].at[o])
+        if j < lines - 1:
+            over_z(plane, j, o).start()
 
     def line_sum(target, acc, zbuf):
         if len(target.shape) > 2:
@@ -711,20 +778,17 @@
     near_copy = lambda i, p: remote(
         tots[i].at[near[p][0], near[p][1]], outs[i].at[x, c], gs.at[i, p], gr.at[i, p], to_near[p]
     )
-    for i in range(jobs):
+    for i in plain + [plane]:
         for j, o in places[:-1]:
             block = zbufs[i].at[o]
             remote(block, block, zs.at[i, j], zr.at[i, o], me.at(z=o)).wait_recv()
-        if kinds[i]:
-            for xx in range(2):
-                for cc in range(2):
-                    line_sum(tots[i].at[xx, cc], accs[i].at[:, xx, cc], zbufs[i].at[:, xx, cc])
+        if i == plane:
+            line_sum(outs[i], ybufs[i], zbufs[i])
+        else:
+            line_sum(tots[i], ybufs[i], zbufs[i])
             for p in range(3):
                 go(near_copy(i, p))
-            rows = tots[i].shape[2]
             outs[i][x, c] = tots[i][x, c]
-        else:
-            line_sum(outs[i], accs[i], zbufs[i])
     if with_o:
         o_core = remote(o_tot.at[1 - c], o_out, ocs, ocr, to_c)
 
@@ -733,9 +797,9 @@
             for j, o in places[:-1]:
                 block = o_zbuf.at[o]
                 remote(block, block, ozs.at[j], ozr.at[o], me.at(z=o)).wait_recv()
-            line_sum(o_tot.at[1 - c], o_acc.at[:, 1 - c], o_zbuf.at[:, 1 - c])
+            line_sum(o_tot.at[1 - c], o_ybuf.at[:, 1 - c], o_zbuf.at[:, 1 - c])
             o_core.start()
-            line_sum(o_out, o_acc.at[:, c], o_zbuf.at[:, c])
+            line_sum(o_out, o_ybuf.at[:, c], o_zbuf.at[:, c])
             for j, o in places[:-1]:
                 o_over_z(j, o).wait_send()
             o_core.wait_send()
@@ -746,48 +810,59 @@
                 o_over_y(j, o).wait_send()
             o_core.wait_recv()
 
+    for i in plain:
+        for p in range(3):
+            block = outs[i].at[near[p][0], near[p][1]]
+            remote(block, block, gs.at[i, p], gr.at[i, p], to_near[p]).wait_recv()
     for i in range(jobs):
-        if kinds[i]:
-            for p in range(3):
-                block = outs[i].at[near[p][0], near[p][1]]
-                remote(block, block, gs.at[i, p], gr.at[i, p], to_near[p]).wait_recv()
         for j, o in places[:-1]:
             over_z(i, j, o).wait_send()
+    for j, o in places:
+        over_y(plane, j, o).wait_send()
+    for i in range(2):
+        x_copy(i).wait_send()
     copies.finish()
 
 
-def sum_grads(parts, kinds, o_part, lines, ident, work=None, spans=None):
+def sum_grads(parts, plane, rows_part, o_part, lines, ident, work=None, spans=None):
     jobs = len(parts)
     with_o = o_part is not None
-    inputs = list(parts) + ([o_part] if with_o else [])
-    outs = [jax.ShapeDtypeStruct(p.shape[2:], p.dtype) for p in parts]
+    inputs = list(parts) + [rows_part] + ([o_part] if with_o else [])
+    in_specs = [HBM if i == plane else VMEM for i in range(jobs)] + [HBM] + [VMEM] * with_o
+    block = lambda i: parts[i].shape[4:] if i == plane else parts[i].shape[2:]
+    outs = [jax.ShapeDtypeStruct(block(i), parts[i].dtype) for i in range(jobs)]
+    outs.append(jax.ShapeDtypeStruct(rows_part.shape[2:], F32))
     if with_o:
         outs.append(jax.ShapeDtypeStruct(o_part.shape[2:], o_part.dtype))
     dma = pltpu.SemaphoreType.DMA
-    line = lambda p: pltpu.VMEM((lines,) + p.shape[2:], p.dtype)
-    scratch = [line(p) for p in parts] * 2
-    scratch += [pltpu.VMEM(p.shape[2:] if k else (8, 128), p.dtype) for p, k in zip(parts, kinds)]
+    buf = lambda lead, i: pltpu.VMEM(lead + block(i), parts[i].dtype)
+    scratch = [buf((lines,), i) for i in range(jobs)] * 2
+    scratch += [pltpu.VMEM((8, 128), BF) if i == plane else buf((), i) for i in range(jobs)]
+    scratch += [buf((2, lines, 2), plane), buf((2, lines, 2), plane), buf((lines, 2), plane)]
+    rows = lambda *lead: pltpu.VMEM(lead + rows_part.shape[2:], rows_part.dtype)
+    scratch += [rows(2), rows(2), rows()]
+    scratch += [dma((jobs, lines))] * 4 + [dma((jobs, 3))] * 2
+    scratch += [dma((2, 2)), dma((2, 3)), dma((2, 3))]
     if with_o:
         scratch += [pltpu.VMEM(o_part.shape, o_part.dtype)] * 2
         scratch += [pltpu.VMEM(o_part.shape[1:], o_part.dtype)]
-    scratch += [dma((jobs, lines))] * 4 + [dma((jobs, 3))] * 2
-    if with_o:
         scratch += [dma((lines,))] * 4 + [dma, dma]
-    in_specs = [VMEM] * len(inputs)
+    out_specs = [VMEM] * len(outs)
     if work:
         inputs += work
         in_specs += [HBM] * 4
         shapes, buffers = work_shapes(work, spans, lines)
         outs += shapes
+        out_specs += [VMEM] * 3
         scratch += buffers
     return pl.pallas_call(
-        functools.partial(grads_kernel, lines, tuple(kinds), with_o, spans if work else None),
+        functools.partial(grads_kernel, lines, plane, with_o, spans if work else None),
         out_shape=outs,
         in_specs=in_specs,
-        out_specs=[VMEM] * len(outs),
+        out_specs=out_specs,
         scratch_shapes=scratch,
         compiler_params=pltpu.CompilerParams(
-            collective_id=ident, has_side_effects=True, vmem_limit_bytes=62 << 20
+            collective_id=ident, has_side_effects=True, vmem_limit_bytes=63 << 20
         ),
     )(*inputs)
 
@@ -799,8 +874,8 @@
 def hidden_kernel(
     lines, chunks, spans, local_experts,
     src, cots, spread, e_gate, e_up, e_down, s_in, s_down,
-    dst, hid, in_d, gate_g, w_in_out, w_down_out,
-    h_in, c_in, hid_out, in_out, g_out, w_in, w_down,
+    dst, hid, in_d, gate_g, w_in_out, parts,
+    h_in, c_in, hid_out, in_out, g_out, part_out, w_in, w_down,
     w_sem, own_sem, hs, cins, sts, zs, zr, xs, xr, ys, yr, ds_, dr, cs, cr,
 ):
     me = Place()
@@ -885,7 +960,7 @@
 
     def stores(k, side):
         yy, xx = side_of(side)
-        pairs = ((hid_out, hid), (in_out, in_d), (g_out, gate_g))
+        pairs = ((hid_out, hid), (in_out, in_d), (g_out, gate_g), (part_out, parts))
         return [
             pltpu.make_async_copy(v.at[side], ref.at[:, yy, xx, :, span(k)], sts.at[side, i])
             for i, (v, ref) in enumerate(pairs)
@@ -922,6 +997,11 @@
             )
             in_out[side, :, :, :, up_at] = (d * act).astype(BF).reshape(shape)
         g_out[side] = sums.astype(BF).reshape(lines, 2, step_rows, 128)
+        hidden = hid_out[side].reshape(units, inner)
+        for begin in range(0, width, 512):
+            at = slice(begin, begin + 512)
+            part = jnp.dot(hidden, w_down[:, at], preferred_element_type=F32)
+            part_out[side, :, :, :, at] = part.astype(BF).reshape(lines, 2, step_rows, 512)
         for copy in stores(k, side):
             copy.start()
 
@@ -954,12 +1034,8 @@
                 )
     for copy in fills:
         copy.wait()
-    keep = [
-        pltpu.make_async_copy(w_in, w_in_out, w_sem.at[0]),
-        pltpu.make_async_copy(w_down, w_down_out, w_sem.at[1]),
-    ]
-    for copy in keep:
-        copy.start()
+    keep = pltpu.make_async_copy(w_in, w_in_out, w_sem.at[0])
+    keep.start()
 
     own.wait()
     z_land(0)
@@ -1015,8 +1091,7 @@
         def _():
             fetch(t, 1)
 
-    for copy in keep:
-        copy.wait()
+    keep.wait()
     for side in range(4):
         for copy in stores(chunks - 1, side):
             copy.wait()
@@ -1054,14 +1129,14 @@
         ]
         + [
             jax.ShapeDtypeStruct((2 * inner, width), BF),
-            jax.ShapeDtypeStruct((inner, width), BF),
+            jax.ShapeDtypeStruct(lead + (width,), BF),
         ],
         in_specs=[HBM, HBM, VMEM] + [HBM] * 5,
         out_specs=[HBM] * 6,
         scratch_shapes=[
-            slot(wide), slot(early), slot(inner), slot(2 * inner), slot(128),
+            slot(wide), slot(early), slot(inner), slot(2 * inner), slot(128), slot(width),
             pltpu.VMEM((2 * inner, width), BF), pltpu.VMEM((inner, width), BF),
-            dma((2 + 3 * len(spans),)), dma, dma((4,)), dma((4,)), dma((4, 3)),
+            dma((2 + 3 * len(spans),)), dma, dma((4,)), dma((4,)), dma((4, 4)),
             line, line, line, line, line, line,
             dma((chunks, lines, 2)), dma((chunks, lines, 2)), dma((chunks, 4)), dma((chunks, 4)),
         ],
@@ -1073,10 +1148,10 @@
 
 def back_kernel(
     lines,
-    hid, in_d, gate_g, w_in, w_down,
-    out, parts,
-    hid_in, d_in, g_in, part_out, sbuf, acc, cbuf, xbuf, ybuf, zbuf, xdiag, ydiag,
-    ins, sts, cs, cr, xs, xr, ys, yr, zs, zr, xds, xdr, yds, ydr,
+    in_d, gate_g, w_in, passed,
+    out, passed_on,
+    d_in, g_in, sbuf, acc, cbuf, xbuf, ybuf, zbuf, xdiag, ydiag,
+    ins, cs, cr, xs, xr, ys, yr, zs, zr, xds, xdr, yds, ydr,
 ):
     me = Place()
     z, y, x, c = me.z, me.y, me.x, me.c
@@ -1098,17 +1173,11 @@
 
     def loads(n, side):
         yy, xx = side_of(side)
-        pairs = ((hid, hid_in), (in_d, d_in), (gate_g, g_in))
+        pairs = ((in_d, d_in), (gate_g, g_in))
         return [
             pltpu.make_async_copy(ref.at[place(n), yy, xx], v.at[side], ins.at[side, i])
             for i, (ref, v) in enumerate(pairs)
         ]
-
-    def store(n, side):
-        yy, xx = side_of(side)
-        return pltpu.make_async_copy(
-            part_out.at[side], parts.at[place(n), yy, xx], sts.at[side]
-        )
 
     def to_core(n, side):
         yy, xx = side_of(side)
@@ -1120,9 +1189,7 @@
         yy, xx = side_of(side)
         for copy in loads(n, side):
             copy.wait()
-        inner = w_down.shape[0]
-        grads = d_in[side].reshape(2 * rows, 2 * inner)
-        value = hid_in[side].reshape(2 * rows, inner)
+        grads = d_in[side].reshape(2 * rows, w_in.shape[0])
         piece = 512
         for begin in range(0, width, piece):
             at = slice(begin, begin + piece)
@@ -1138,11 +1205,6 @@
                 acc[place(n), yy, xx, :, at] = back[1]
                 sbuf[side, :, at] = back[0]
 
-            part_out[side, :, :, at] = (
-                jnp.dot(value, w_down[:, at], preferred_element_type=F32)
-                .astype(BF)
-                .reshape(2, rows, piece)
-            )
         acc[place(n), yy, xx, :, width:] = g_in[side, c]
         sbuf[side, :, width:] = g_in[side, 1 - c]
 
@@ -1227,12 +1289,10 @@
             def _():
                 @pl.when(n >= 1)
                 def _():
-                    store(n - 1, side).wait()
                     to_core(n - 1, side).wait_send()
 
                 unit(n, side)
                 to_core(n, side).start()
-                store(n, side).start()
 
                 @pl.when(n + 1 < lines)
                 def _():
@@ -1246,7 +1306,6 @@
                     act(t - behind)
 
     for side in range(4):
-        store(lines - 1, side).wait()
         to_core(lines - 1, side).wait_send()
     for o in others:
         remote(zbuf.at[o], zbuf.at[o], zs.at[0], zr.at[o], me.at(z=o)).wait_recv()
@@ -1269,8 +1328,45 @@
             z_copy(n).wait_send()
 
 
-def sum_back(hid, in_d, gate_g, w_in, w_down, ident):
-    lines, rows, inner = hid.shape[0], hid.shape[4], hid.shape[5]
+def layout_kernel(own_heads, q, kvb, kva, o, shared, q_out, kvb_out, kva_out, o_out, gate_out, up_out):
+    for source, target in ((q, q_out), (kvb, kvb_out)):
+        size = source.shape[3] // own_heads
+        held = [[source[xx, cc].astype(F32) for cc in range(2)] for xx in range(2)]
+        pieces = [
+            held[xx][cc][:, i * size : (i + 1) * size]
+            for i in range(own_heads)
+            for cc in range(2)
+            for xx in range(2)
+        ]
+        target[...] = jnp.concatenate(pieces, axis=1)
+    kva_out[...] = kva[...].astype(F32)
+    o_out[...] = o[...].astype(F32)
+    for which, target in enumerate((gate_out, up_out)):
+        pieces = [shared[i, which].astype(F32) for i in range(shared.shape[0])]
+        target[...] = jnp.concatenate(pieces, axis=1)
+
+
+def lay_out(q, kvb, kva, o, shared, own_heads):
+    flat = lambda rows, columns: jax.ShapeDtypeStruct((rows, columns), F32)
+    hidden = shared.shape[0] * shared.shape[3]
+    return pl.pallas_call(
+        functools.partial(layout_kernel, own_heads),
+        out_shape=[
+            flat(q.shape[2], 4 * q.shape[3]),
+            flat(kvb.shape[2], 4 * kvb.shape[3]),
+            flat(*kva.shape),
+            flat(*o.shape),
+            flat(shared.shape[2], hidden),
+            flat(shared.shape[2], hidden),
+        ],
+        in_specs=[VMEM] * 5,
+        out_specs=[VMEM] * 6,
+        compiler_params=pltpu.CompilerParams(vmem_limit_bytes=32 << 20),
+    )(q, kvb, kva, o, shared)
+
+
+def sum_back(in_d, gate_g, w_in, passed, ident):
+    lines, rows, inner = in_d.shape[0], in_d.shape[4], in_d.shape[5]
     width = w_in.shape[1]
     wide = width + 128
     half = wide // 256 * 128
@@ -1281,23 +1377,23 @@
         functools.partial(back_kernel, lines),
         out_shape=[
             jax.ShapeDtypeStruct((rows, wide), F32),
-            jax.ShapeDtypeStruct((lines, 2, 2, 2, rows, width), BF),
+            jax.ShapeDtypeStruct(passed.shape, passed.dtype),
         ],
-        in_specs=[HBM] * 3 + [VMEM] * 2,
+        in_specs=[HBM] * 2 + [VMEM, HBM],
         out_specs=[VMEM, HBM],
+        input_output_aliases={3: 1},
         scratch_shapes=[
-            buf(4, 2, rows, inner), buf(4, 2, rows, 2 * inner),
-            buf(4, 2, rows, 128), buf(4, 2, rows, width), buf(4, rows, wide),
+            buf(4, 2, rows, inner), buf(4, 2, rows, 128), buf(4, rows, wide),
             buf(lines, 2, 2, rows, wide), buf(lines, 2, 2, rows, wide),
             buf(lines, rows, wide), buf(lines, rows, wide), buf(lines, rows, wide),
             buf(lines, rows, half), buf(lines, rows, wide - half),
-            dma((4, 3)), dma((4,)), dma((4,)), dma((lines, 4)),
+            dma((4, 2)), dma((4,)), dma((lines, 4)),
             line, line, line, line, line, line, line, line, line, line,
         ],
         compiler_params=pltpu.CompilerParams(
-            collective_id=ident, has_side_effects=True, vmem_limit_bytes=62 << 20
+            collective_id=ident, has_side_effects=True, vmem_limit_bytes=60 << 20
         ),
-    )(hid, in_d, gate_g, w_in, w_down)
+    )(in_d, gate_g, w_in, passed)
 
 
 def on_device(
@@ -1359,12 +1455,19 @@
         starts = [sum(small_sizes[:i]) for i in range(len(small_sizes))]
         return [flat[..., b : b + n] for b, n in zip(starts, small_sizes)]
 
+    shared_width = shared_down.shape[0]
+    both_shared = jnp.stack([shared_gate, shared_up]).reshape(
+        2, shared_gate.shape[0], device_count, shared_width
+    )
+    both_shared = lax.all_to_all(
+        both_shared.transpose(2, 0, 1, 3), BOTH, split_axis=0, concat_axis=0
+    )
+    both_shared = both_shared.transpose(1, 0, 2, 3).reshape(2, width, shared_width)
     small_own = pack([v.reshape(-1) for v in small])
     rounds = max(1, tok_rows * device_count // 4096)
-    planes = [kva_weight]
     started = start_gather(
         tokens,
-        planes,
+        [kva_weight],
         [1],
         [
             jnp.broadcast_to(small_own, (2, 2) + small_own.shape),
@@ -1377,7 +1480,7 @@
     )
     group_tokens = started[0].reshape(group_len, width)
     kva_all = started[1].reshape(width, latent_width)
-    small_set, kvb_set, q_set, *o_set = started[1 + len(planes) :]
+    small_set, kvb_set, q_set, *o_set = started[2:]
     small_all = unpack(small_set.reshape((device_count,) + small_own.shape))
     kvb_mine = kvb_set.reshape(KV_RANK, -1)
     q_mine = q_set.reshape(width, -1)
@@ -1398,7 +1501,7 @@
     )
     input_rows = tokens.astype(F32)
     group_rows = group_tokens.astype(F32)
-    normed_group, _ = rms_forward(group_rows, norm1_scale)
+    normed_group, inverse_group = rms_forward(group_rows, norm1_scale)
     hidden_one = normed_group.astype(BF)
     query_raw = mm(hidden_one, q_mine).reshape(group_len, own_heads, NOPE + ROPE)
     q_nope = query_raw[:, :, :NOPE].astype(BF)
@@ -1438,14 +1541,6 @@
     kept = kept_pairs(expert_ids, token_rank, choice_hot, capacity)
     gate_table = jnp.sum(choice_hot * (gate_probs * kept)[:, :, None], axis=1)
 
-    shared_width = shared_down.shape[0]
-    both_shared = jnp.stack([shared_gate, shared_up]).reshape(
-        2, shared_gate.shape[0], device_count, shared_width
-    )
-    both_shared = lax.all_to_all(
-        both_shared.transpose(2, 0, 1, 3), BOTH, split_axis=0, concat_axis=0
-    )
-    both_shared = both_shared.transpose(1, 0, 2, 3).reshape(2, width, shared_width)
     own_width = expert_gate.shape[2]
     sizes = [own_width + -own_width % 128] * local_experts + [shared_width + -shared_width % 128]
     spans = tuple((sum(sizes[:i]), size) for i, size in enumerate(sizes))
@@ -1469,7 +1564,7 @@
         high = table.astype(BF)
         low = (table - high.astype(F32)).astype(BF)
         spare = jnp.zeros((table.shape[0], 128 - 2 * all_experts), BF)
-        values, hid, in_d, gate_g, w_in, w_down = gather_hidden(
+        values, hid, in_d, gate_g, w_in, out_part = gather_hidden(
             jnp.concatenate([rows, high, low, spare, cots[:, early:]], axis=1),
             cots_all,
             spread,
@@ -1483,9 +1578,7 @@
             lines,
             3,
         )
-        back_sum, out_part = lax.optimization_barrier(
-            sum_back(hid, in_d, gate_g, w_in, w_down, 4)
-        )
+        back_sum, out_part = sum_back(in_d, gate_g, w_in, out_part, 4)
         flat = lambda v: v.reshape(cots_all.shape[0], -1)
         work = [flat(values), cots_all, flat(in_d), flat(hid)]
         return scatter_sum(flat(out_part), BOTH), back_sum, work
@@ -1539,9 +1632,6 @@
     shared_grad = jnp.stack(shared_made[:2]).astype(BF)
     shared_grad = shared_grad.reshape(2, shared_width, device_count, -1).transpose(2, 0, 3, 1)
     shared_grad = lax.all_to_all(shared_grad, BOTH, split_axis=0, concat_axis=0)
-    shared_grad = shared_grad.astype(F32).transpose(1, 2, 0, 3).reshape(
-        2, width // device_count, device_count * shared_width
-    )
     sdown_grad = shared_made[2]
     o_part = mm_tn(attended, mixed_grad_group)
     attended_grad = (
@@ -1570,49 +1660,21 @@
         .astype(BF)
     )
     kvb_part = mm_tn(latent, keyval_grad)
-    latent_part = jnp.concatenate([mm_nt(keyval_grad, kvb_mine), rope_grad], axis=1).astype(BF)
-    latent_sum = sum_group(
-        jnp.pad(latent_part, ((0, 0), (0, -latent_part.shape[1] % 128))), 6
-    )[:, :latent_width]
-    own_start = shard_at * tok_rows
-    own_rows = lambda value: lax.dynamic_slice_in_dim(value, own_start, tok_rows)
-    latent_raw_grad, kv_gain_part = rms_backward(
-        own_rows(compressed[:, :KV_RANK]),
-        own_rows(inverse_latent),
-        latent_scale,
-        latent_sum[:, :KV_RANK],
-    )
-    compressed_grad = jnp.concatenate(
-        [
-            latent_raw_grad,
-            rotate(latent_sum[:, KV_RANK:], own_rows(cosine_table), -own_rows(sine_table)),
-        ],
-        axis=1,
+    latent_raw_part, kv_gain_part = rms_backward(
+        compressed[:, :KV_RANK], inverse_latent, latent_scale, mm_nt(keyval_grad, kvb_mine)
+    )
+    compressed_part = jnp.concatenate(
+        [latent_raw_part, rotate(rope_grad, cosine_table, -sine_table)], axis=1
     ).astype(BF)
-    compressed_grad_group = gather_group(
-        jnp.pad(compressed_grad, ((0, 0), (0, -latent_width % 128))), 7
-    )[0][:, :latent_width]
     query_grad = jnp.concatenate(
         [q_nope_grad, rotate(q_rope_grad, cosine_table[:, None, :], -sine_table[:, None, :])],
         axis=-1,
     )
     query_grad = query_grad.reshape(group_len, own_heads * (NOPE + ROPE)).astype(BF)
     q_part = mm_tn(hidden_one, query_grad)
-    kva_part = mm_tn(hidden_one, compressed_grad_group).astype(BF)
-    kva_part = lax.dynamic_index_in_dim(
-        kva_part.reshape(expert_count, shard_count, width // device_count, latent_width),
-        shard_at,
-        1,
-        keepdims=False,
-    )
-    hidden_one_grad = sum_group(mm_nt(query_grad, q_mine).astype(BF), 8) + mm_nt(
-        compressed_grad, kva_all
-    )
-    _, inverse_one = rms_forward(input_rows, norm1_scale)
-    input_norm_grad, norm1_part = rms_backward(
-        input_rows, inverse_one, norm1_scale, hidden_one_grad
-    )
-    tokens_grad = mixed_grad + input_norm_grad
+    kva_part = mm_tn(hidden_one, compressed_part)
+    hidden_one_part = mm_nt(query_grad, q_mine) + mm_nt(compressed_part, kva_all)
+    norm1_part = jnp.sum(hidden_one_part * (group_rows * inverse_group), axis=0)
 
     def from_heads(parts):
         rows = parts.shape[2]
@@ -1625,7 +1687,7 @@
     )
     parts = [
         kvb_part.astype(BF).reshape(line_shape + (2, 2, kvb_weight.shape[0], -1)),
-        kva_part.reshape(line_shape + (width // device_count, latent_width)),
+        kva_part.astype(BF).reshape(line_shape + (2, 2, width // device_count, latent_width)),
         q_part.astype(BF).reshape(line_shape + (2, 2, q_weight.shape[0], q_mine.shape[1])),
         small_parts.reshape(line_shape + (2, 2) + small_parts.shape[1:]),
     ]
@@ -1637,17 +1699,35 @@
         o_wide = jnp.zeros((own_heads, 2, 2, VDIM, width), BF).at[:, core_at, x_at].set(o_part)
         o_grad = scatter_sum(o_wide.reshape(HEADS * VDIM, width), BOTH).astype(F32)
     summed = sum_grads(
-        parts, (True, False, True, True), o_sum, lines, 9, work, expert_spans
-    )
+        parts,
+        1,
+        hidden_one_part.astype(BF).reshape(2, 2, tok_rows, width),
+        o_sum,
+        lines,
+        9,
+        work,
+        expert_spans,
+    )
+    _, inverse_one = rms_forward(input_rows, norm1_scale)
+    input_norm_grad, _ = rms_backward(input_rows, inverse_one, norm1_scale, summed[4])
+    tokens_grad = mixed_grad + input_norm_grad
     if work:
         expert_grads = summed[-3:]
-    kvb_grad = from_heads(summed[0])
-    kva_grad = summed[1].astype(F32)
-    q_grad = from_heads(summed[2])
     norm1_grad, norm2_grad, kv_gain_grad, router_grad = unpack(jnp.sum(summed[3], axis=(0, 1)))
     router_grad = router_grad.reshape(router_weight.shape)
     if o_pairs:
-        o_grad = summed[4].astype(F32)
+        q_grad, kvb_grad, kva_grad, o_grad, sgate_grad, sup_grad = lay_out(
+            summed[2], summed[0], summed[1], summed[5], shared_grad, own_heads
+        )
+    else:
+        kvb_grad = from_heads(summed[0])
+        kva_grad = summed[1].astype(F32)
+        q_grad = from_heads(summed[2])
+        sgate_grad, sup_grad = (
+            shared_grad.astype(F32)
+            .transpose(1, 2, 0, 3)
+            .reshape(2, width // device_count, device_count * shared_width)
+        )
     return (
         output,
         tokens_grad,
@@ -1659,8 +1739,8 @@
         o_grad,
         norm2_grad,
         router_grad,
-        shared_grad[0],
-        shared_grad[1],
+        sgate_grad,
+        sup_grad,
         sdown_grad,
         expert_grads[0].swapaxes(1, 2),
         expert_grads[1].swapaxes(1, 2),

time: 801 us -> 745 us (0.930)
  Pallas kernels: 563 us -> 533 us
  local copies, waits for them, and re-layouts: 97.4 us -> 75.6 us
    pallas_call x3 -> x1, Pallas kernels: 60.1 us -> 16.3 us  [sum_group(): pl.pallas_call(functools.partial(sum_group_kernel, cuts), out_shape=jax.S...]
    pallas_call x1 -> x2, Pallas kernels: 127 us -> 154 us  [the longest x1 150 us: sum_grads(): pl.pallas_call(functools.partial(grads_kernel, lines, plane, with_o, span...]
    pallas_call x2 -> x1, Pallas kernels: 39.8 us -> 27.2 us  [gather_group(): pl.pallas_call(functools.partial(gather_group_kernel, cuts, spans if work...]
    unnamed x157 -> x184, local copies, waits for them, and re-layouts: 32.6 us -> 31.5 us
  transfers between devices with their start and end apart: 4 -> 4, of which waited for: 1 -> 1; matrix products, arithmetic and copies ran while one was open for 16% -> 13% of each run, Pallas kernels for 29% -> 27%
where the time goes in v4:
time: 745 us; the launch traced here: 733 us
  Pallas kernels  533 us (72%)
  local copies, waits for them, and re-layouts  75.6 us (10%)
  matrix products  44.6 us (6%)
  starting transfers between devices  23.9 us (3%)
  other arithmetic  19.8 us (3%)
  waiting for transfers between devices  19.6 us (3%)
  between operations  16.4 us (2%)
    pallas_call x1, Pallas kernels, sum_grads(): pl.pallas_call(functools.partial(grads_kernel, lines, plane, with_o, span...  150 us
    pallas_call x1, Pallas kernels, gather_hidden(): pl.pallas_call(functools.partial(hidden_kernel, lines, chunks, spans, loc...  139 us
    pallas_call x1, Pallas kernels, sum_back(): pl.pallas_call(functools.partial(back_kernel, lines), out_shape=[jax.Shap...  100 us
    pallas_call x1, Pallas kernels, start_gather(): pl.pallas_call(functools.partial(start_kernel, lines, tuple(counts), with...  96.8 us
    unnamed x184, local copies, waits for them, and re-layouts  31.5 us
    pallas_call x1, Pallas kernels, gather_group(): pl.pallas_call(functools.partial(gather_group_kernel, cuts, spans if work...  27.2 us
    all_gather x1, waiting for transfers between devices, gather(): return lax.all_gather(value, axes, axis=0, tiled=True)  19.6 us
    pallas_call x1, Pallas kernels, sum_group(): pl.pallas_call(functools.partial(sum_group_kernel, cuts), out_shape=jax.S...  16.3 us
  transfers between devices with their start and end apart: 4, of which 1 were waited for; matrix products, arithmetic and copies ran while one was open for 13% of the time, Pallas kernels for 27%

profile of v4, /device:TPU:0, one launch (start us, length us, event | category | flops | bytes accessed | tf_op | source)
XLA Modules:
  0.0 732.7 jit_solution(16014188633511464756)
XLA Ops:
  8.2 2.1 concatenate.42
  10.2 1.0 reshape.580
  12.0 1.6 reshape.582
  13.9 1.2 reshape.583.refs_4_
  15.7 96.8 %shard_map.306 = (bf16[2,2,128,2048]{3,2,1,0:T(8,128)(2,1)}, bf16[4,2,2,2,64,576]{5,4,3,2,1,0:T(8,128)(2,1)}, bf16[4,2,2,2,16,128]{5,4,3,2,1,0:T(8,128)(2,1)}, b...) custom-call(bf16[128,2048]{1,0:T(8,128)(2,1)} %refs_0_.1, ...), custom_call_target="tpu_custom_call" | custom-call | tf_op jit(solution)/shard_map/pallas_call | solution.py:542
  112.5 1.1 slice.128
  115.1 1.3 stack.16
  116.4 1.3 stack.17
  118.0 1.4 copy.173
  119.4 15.6 %all-to-all-start = ((bf16[32,2,64,88]{3,2,1,0:T(8,128)(2,1)}), bf16[32,2,64,88]{3,2,1,0:T(8,128)(2,1)}, u32[]{:S(2)}, u32[]{:S(2)}) async-start(bf16[32,2,64,88]{3,2,1,0:T(8,128)(2,1)} %copy.173), calls=%async_computation | async-start | bytes 2097152 | tf_op jit(solution)/shard_map/all_to_all | solution.py:1462
  135.5 1.2 reshape.593
  137.7 1.6 copy-done.79
  139.3 1.4 fusion.65
  141.0 1.8 convolution_convert_fusion.5
  142.8 2.3 reshape.586
  145.1 1.2 fusion.62
  146.2 1.5 copy.201
  147.7 4.6 copy.166
  153.1 0.9 fusion.35
  154.0 4.4 fusion.66
  159.6 1.2 fusion.64
  164.1 1.3 convolution_convert_fusion.3
  165.4 16.3 %shard_map.307 = f32[128,2048]{1,0:T(8,128)S(1)} custom-call(bf16[2,2,128,2048]{3,2,1,0:T(8,128)(2,1)S(1)} %bitcast.139), custom_call_target="tpu_custom_call" | custom-call | tf_op jit(solution)/shard_map/pallas_call | solution.py:260
  184.4 1.8 pad.18.s_down
  186.3 1.1 concatenate.45.src
  188.2 1.3 copy.174
  189.5 1.2 copy.175
  190.8 2.2 pad.17.s_in
  192.9 19.6 %all-gather.2.cloned.1.call-done.refs_2_.refs_7_ = bf16[4096,1024]{1,0:T(8,128)(2,1)} async-done(((bf16[128,1024]{1,0:T(8,128)(2,1)}), bf16[4096,1024]{1,0:T(8,128)(2,1)}) %all-gather.2.cloned.1.call-update) | async-done | bytes 8388624 | tf_op jit(solution)/shard_map/all_gather | solution.py:96
  212.5 138.9 %shard_map.308 = (bf16[4,2,2,2,128,3200]{5,4,3,2,1,0:T(8,128)(2,1)}, bf16[4,2,2,2,128,896]{5,4,3,2,1,0:T(8,128)(2,1)}, bf16[4,2,2,2,128,1792]{5,4,3,2,1,0:T(8,12...) custom-call(bf16[128,3200]{1,0:T(8,128)(2,1)} %concatenate.45.src, ...), custom_call_target="tpu_custom_call" | custom-call | tf_op jit(solution)/shard_map/pallas_call | solution.py:1125
  351.4 100.1 %shard_map.309 = (f32[128,2176]{1,0:T(8,128)}, bf16[4,2,2,2,128,2048]{5,4,3,2,1,0:T(8,128)(2,1)}) custom-call(bf16[4,2,2,2,128,1792]{5,4,3,2,1,0:T(8,128)(2,1)} %get-tuple-element.55.in_d, bf16[4,2,2,2,128,128]{5,4,3,2,1,0:T(8,128)(2,1)} %get-tuple-element.56.gate_g, bf16[1792,2048]{1,0:T(8,128)(2,1)} %get-tuple-element.57.w_in, ...), custom_call_target="tpu_custom_call", output_to_operand_aliasing={{1}: (3, {})} | custom-call | tf_op jit(solution)/shard_map/pallas_call | solution.py:1376
  453.7 1.9 multiply_reduce_fusion.3
  456.5 1.3 fusion.69
  457.8 2.5 reshape.609
  460.3 1.4 fusion.60.refs_0_
  461.7 3.1 copy-done
  464.8 27.2 %shard_map.310 = (bf16[2,2,128,2048]{3,2,1,0:T(8,128)(2,1)S(1)}, f32[1,88,2048]{2,1,0:T(8,128)S(1)}, f32[1,88,2048]{2,1,0:T(8,128)S(1)}, f32[1,88,2048]{2,1,0:T(8,128)S(1)}) custom-call(bf16[128,2048]{1,0:T(8,128)(2,1)S(1)} %fusion.60.refs_0_, bf16[4096,3200]{1,0:T(8,128)(2,1)} %bitcast.145, bf16[4096,1024]{1,0:T(8,128)(2,1)} %all-gather.2.cloned.1.call-done.refs_2_.refs_7_, ...), custom_call_target="tpu_custom_call" | custom-call | tf_op jit(solution)/shard_map/pallas_call | solution.py:200
  492.0 1.3 copy-done.5
  493.3 1.0 copy.187
  495.1 2.1 copy.188
  497.3 2.4 maximum_bitcast_fusion.1
  499.7 8.3 %all-to-all-start.1 = ((bf16[32,2,64,88]{3,2,1,0:T(8,128)(2,1)}), bf16[32,2,64,88]{3,2,1,0:T(8,128)(2,1)}, u32[]{:S(2)}, u32[]{:S(2)}) async-start(bf16[32,2,64,88]{3,2,1,0:T(8,128)(2,1)} %maximum_bitcast_fusion.1), calls=%async_computation.2 | async-start | bytes 2097152 | tf_op jit(solution)/shard_map/all_to_all | solution.py:1634
  508.0 3.1 convolution_convert_fusion.6
  511.1 1.0 multiply_reduce_fusion.1
  512.0 1.2 multiply_convert_fusion.1
  515.9 1.8 multiply_reduce_fusion.2
  518.3 2.3 fusion.13
  524.2 1.8 fusion.68
  526.6 3.7 fusion.61
  530.5 3.5 convolution_convert_fusion.4
  534.0 3.2 convolution_convert_fusion.1
  538.0 4.3 copy.182
  542.4 2.6 convolution_convert_fusion.2
  544.9 3.5 convolution_convert_fusion
  548.5 150.4 %shard_map.311 = (bf16[2,2,16,1024]{3,2,1,0:T(8,128)(2,1)}, bf16[64,576]{1,0:T(8,128)(2,1)}, bf16[2,2,64,768]{3,2,1,0:T(8,128)(2,1)}, f32[2,2,16,128]{3,2,1,0:T(...) custom-call(bf16[4,2,2,2,16,1024]{5,4,3,2,1,0:T(8,128)(2,1)} %bitcas, ...), custom_call_target="tpu_custom_call" | custom-call | tf_op jit(solution)/shard_map/pallas_call | solution.py:858
  701.1 1.7 fusion.17
  703.4 1.0 copy-done.1
  704.4 0.9 copy-done.2
  707.1 3.3 shard_map.312
  710.5 3.3 fusion.20
  714.6 2.9 copy.221
  717.5 1.8 copy-done.23
  719.3 2.8 copy.222
  722.9 2.5 copy.223
  (271 shorter events, 32.2 us)
Async XLA Ops:
  7.2 107.1 %copy-start.26 = (bf16[128,2048]{1,0:T(8,128)(2,1)S(1)}, bf16[128,2048]{1,0:T(8,128)(2,1)}, u32[]{:S(2)}) copy-start(bf16[128,2048]{1,0:T(8,128)(2,1)} %param.20) | copy-start | bytes 1572868
  7.2 205.3 %all-gather.2.cloned.1.call-start = ((), (), s32[]{:S(2)}) async-start(), calls=%async_computation.3 | async-start | bytes 8650752 | tf_op jit(solution)/shard_map/all_gather | solution.py:96
  12.0 103.1 %copy-start.46 = (bf16[64,2816]{1,0:T(8,128)(2,1)S(1)}, bf16[64,2816]{1,0:T(8,128)(2,1)}, u32[]{:S(2)}) copy-start(bf16[64,2816]{1,0:T(8,128)(2,1)} %param.29) | copy-start | bytes 1081348
  13.7 102.8 %copy-start.47 = (bf16[64,2816]{1,0:T(8,128)(2,1)S(1)}, bf16[64,2816]{1,0:T(8,128)(2,1)}, u32[]{:S(2)}) copy-start(bf16[64,2816]{1,0:T(8,128)(2,1)} %param.30) | copy-start | bytes 1081348
  118.0 17.0 %copy-start.53 = (bf16[4,2,2,2,16,128]{5,4,3,2,1,0:T(8,128)(2,1)S(1)}, bf16[4,2,2,2,16,128]{5,4,3,2,1,0:T(8,128)(2,1)}, u32[]{:S(2)}) copy-start(bf16[4,2,2,2,16,128]{5,4,3,2,1,0:T(8,128)(2,1)} %get-tuple-element.50) | copy-start | bytes 393220
  118.0 18.7 %copy-start.18 = (bf16[2,2,128,2048]{3,2,1,0:T(8,128)(2,1)S(1)}, bf16[2,2,128,2048]{3,2,1,0:T(8,128)(2,1)}, u32[]{:S(2)}) copy-start(bf16[2,2,128,2048]{3,2,1,0:T(8,128)(2,1)} %get-tuple-element.49) | copy-start | bytes 6291460
  119.4 68.8 %all-to-all-start = ((bf16[32,2,64,88]{3,2,1,0:T(8,128)(2,1)}), bf16[32,2,64,88]{3,2,1,0:T(8,128)(2,1)}, u32[]{:S(2)}, u32[]{:S(2)}) async-start(bf16[32,2,64,88]{3,2,1,0:T(8,128)(2,1)} %copy.173), calls=%async_computation | async-start | bytes 2097152 | tf_op jit(solution)/shard_map/all_to_all | solution.py:1462
  134.9 575.5 %reduce-scatter.2.cloned.1.call-start = ((), (), s32[]{:S(2)}) async-start(), calls=%async_computation.4 | async-start | bytes 17301504 | tf_op jit(solution)/shard_map/reduce_scatter | solution.py:100
  135.2 5.7 copy-start.60
  135.5 2.3 copy-start.51
  137.1 2.2 copy-start.79
  137.2 3.6 copy-start.69
  137.7 3.1 copy-start.33
  140.8 12.3 %copy-start.15 = (f32[512,576]{0,1:T(8,128)}, f32[512,576]{0,1:T(8,128)S(1)}, u32[]{:S(2)}) copy-start(f32[512,576]{0,1:T(8,128)S(1)} %fusion.65) | copy-start | bytes 3538948
  146.2 12.3 %copy-start.27 = (bf16[512,4,128]{2,1,0:T(4,128)(2,1)}, bf16[512,4,128]{2,1,0:T(4,128)(2,1)S(1)}, u32[]{:S(2)}) copy-start(bf16[512,4,128]{2,1,0:T(4,128)(2,1)S(1)} %get-tuple-element.180) | copy-start | bytes 1572868
  147.7 4.7 copy-start.55
  152.7 5.7 copy-start.73
  152.8 5.6 copy-start.58
  154.0 5.6 copy-start.48
  154.0 5.6 copy-start.49
  160.9 2.0 copy-start.7
  161.5 2.6 copy-start.81
  165.4 16.3 %copy-start.21 = (bf16[128,2048]{1,0:T(8,128)(2,1)S(1)}, bf16[128,2048]{1,0:T(8,128)(2,1)}, u32[]{:S(2)}) copy-start(bf16[128,2048]{1,0:T(8,128)(2,1)} %refs_0_.1) | copy-start | bytes 1572868
  181.8 2.0 copy-start.84
  182.6 277.7 %copy-start.11 = (f32[128,2048]{1,0:T(8,128)}, f32[128,2048]{1,0:T(8,128)S(1)}, u32[]{:S(2)}) copy-start(f32[128,2048]{1,0:T(8,128)S(1)} %get-tuple-element.171) | copy-start | bytes 3145732
  182.6 3.7 copy-start.38
  183.8 3.6 copy-start.71
  451.5 2.2 copy-start.72
  451.5 2.2 copy-start.67
  455.6 6.0 copy-start.13
  461.7 3.1 copy-start
  495.1 12.8 %copy-start.6 = (bf16[2,2,128,2048]{3,2,1,0:T(8,128)(2,1)S(1)}, bf16[2,2,128,2048]{3,2,1,0:T(8,128)(2,1)}, u32[]{:S(2)}) copy-start(bf16[2,2,128,2048]{3,2,1,0:T(8,128)(2,1)} %copy-done.5) | copy-start | bytes 6291460
  499.7 203.7 %all-to-all-start.1 = ((bf16[32,2,64,88]{3,2,1,0:T(8,128)(2,1)}), bf16[32,2,64,88]{3,2,1,0:T(8,128)(2,1)}, u32[]{:S(2)}, u32[]{:S(2)}) async-start(bf16[32,2,64,88]{3,2,1,0:T(8,128)(2,1)} %maximum_bitcast_fusion.1), calls=%async_computation.2 | async-start | bytes 2097152 | tf_op jit(solution)/shard_map/all_to_all | solution.py:1634
  508.0 3.1 copy-start.8
  515.2 2.4 copy-start.31
  517.6 3.1 copy-start.28
  518.3 2.3 copy-start.50
  518.3 2.4 copy-start.10
  521.3 1.9 copy-start.37
  521.3 2.0 copy-start.39
  521.5 2.6 copy-start.32
  523.4 2.6 copy-start.44
  524.2 1.9 copy-start.19
  524.2 1.9 copy-start.70
  524.2 2.4 copy-start.80
  526.6 3.8 copy-start.43
  526.6 3.8 copy-start.56
  526.6 3.8 copy-start.57
  530.3 3.7 copy-start.52
  530.5 3.5 copy-start.20
  530.5 3.5 copy-start.45
  537.2 5.1 copy-start.42
  542.3 2.6 copy-start.34
  542.3 2.6 copy-start.40
  548.4 152.6 %copy-start.75 = (f32[128]{0:T(128)S(1)}, f32[128]{0:T(128)}, u32[]{:S(2)}) copy-start(f32[128]{0:T(128)} %add_rsqrt_fusion.2) | copy-start | bytes 1540
  698.9 11.5 %copy-start.12 = (f32[128,2048]{1,0:T(8,128)S(1)}, f32[128,2048]{1,0:T(8,128)}, u32[]{:S(2)}) copy-start(f32[128,2048]{1,0:T(8,128)} %copy-done.11) | copy-start | bytes 3145732
  698.9 11.5 %copy-start.22 = (bf16[128,2048]{1,0:T(8,128)(2,1)S(1)}, bf16[128,2048]{1,0:T(8,128)(2,1)}, u32[]{:S(2)}) copy-start(bf16[128,2048]{1,0:T(8,128)(2,1)} %refs_0_.1) | copy-start | bytes 1572868
  698.9 11.5 %copy-start.68 = (f32[128]{0:T(128)S(1)}, f32[128]{0:T(128)}, u32[]{:S(2)}) copy-start(f32[128]{0:T(128)} %copy-done.66) | copy-start | bytes 1540
  698.9 11.5 %copy-start.77 = (f32[128]{0:T(128)S(1)}, f32[128]{0:T(128)}, u32[]{:S(2)}) copy-start(f32[128]{0:T(128)} %copy-done.76) | copy-start | bytes 1540
  707.1 3.3 copy-start.14
  710.4 4.1 copy-start.24
  714.6 4.7 copy-start.23
  714.6 7.5 %slice-start = ((s8[5767168]{0:T(1024)(128)(4,1)}), s8[4194304]{0:T(1024)(128)(4,1)S(1)}, s32[]{:S(2)}) async-start(s8[5767168]{0:T(1024)(128)(4,1)} %bitcast.152), calls=%async_computation.5 | async-start | bytes 8388608
  719.3 3.6 slice-start.1
  (27 other events, 34.3 us)
Sparse Core Ops, SparseCore 0:
  115.3 97.1 all-gather.1
  451.6 233.9 reduce-scatter.1

commit v5 on v4

--- a/solution.py
+++ b/solution.py
@@ -313,81 +313,118 @@
             copy.wait_send()
 
 
-def start_kernel(lines, counts, with_o, *refs):
-    jobs, planes = 3, len(counts)
+class LineGather:
+    def __init__(self, me, lines, block, sems):
+        self.z, self.lines, self.block, self.sems = me.z, lines, block, sems
+        self.to = (me.at(z=lax.rem(me.z + 1, lines)), me.at(z=lax.rem(me.z + lines - 1, lines)))
+
+    def place(self, way, distance):
+        return self.z - distance if way == 0 else self.z + distance
+
+    def comes(self, way, distance):
+        place = self.place(way, distance)
+        return place >= 0 if way == 0 else place < self.lines
+
+    def goes(self, way, distance):
+        on = self.z + 1 < self.lines if way == 0 else self.z >= 1
+        return on & self.comes(way, distance - 1)
+
+    def hop(self, way, distance, place):
+        ref = self.block(place)
+        send, recv = self.sems[2 * way], self.sems[2 * way + 1]
+        return remote(ref, ref, send.at[distance], recv.at[distance], self.to[way])
+
+    def start(self):
+        for way in range(2):
+
+            @pl.when(self.goes(way, 1))
+            def _(way=way):
+                self.hop(way, 1, self.z).start()
+
+    def land(self, distance, then=None):
+        for way in range(2):
+            place = self.place(way, distance)
+
+            @pl.when(self.comes(way, distance))
+            def _(way=way, place=place):
+                self.hop(way, distance, place).wait_recv()
+
+                @pl.when(self.goes(way, distance + 1))
+                def _():
+                    self.hop(way, distance + 1, place).start()
+
+                if then is not None:
+                    then(place)
+
+    def finish(self):
+        for distance in range(1, self.lines):
+            for way in range(2):
+
+                @pl.when(self.goes(way, distance))
+                def _(way=way, distance=distance):
+                    self.hop(way, distance, self.place(way, distance - 1)).wait_send()
+
+
+def start_kernel(lines, with_o, *refs):
+    jobs = 3
     refs = list(refs)
     take = lambda n: [refs.pop(0) for _ in range(n)]
-    (tok,) = take(1)
-    plane_src, sources = take(planes), take(jobs)
+    tok, kva = take(2)
+    sources = take(jobs)
     o_src = take(1)[0] if with_o else None
-    (tok_dst,) = take(1)
-    plane_dst, dests = take(planes), take(jobs)
+    tok_dst, kva_dst = take(2)
+    dests = take(jobs)
     o_dst = take(1)[0] if with_o else None
-    own_sem, gs, gr, zs, zr, ys, yr, ts, tr = take(9)
-    plane_sems = [take(6) for _ in range(planes)]
+    own_sem, gs, gr, ys, yr, ts, tr, ks, kr = take(9)
+    line_sems = [take(4) for _ in range(jobs + 1 + with_o)]
     if with_o:
-        o_own, ocs, ocr, ozs, ozr, oys, oyr = take(7)
+        o_own, ocs, ocr = take(3)
     me = Place()
     z, y, x, c = me.z, me.y, me.x, me.c
-    others = [lax.rem(z + 1 + j, lines) for j in range(lines - 1)]
-    places = list(enumerate(others)) + [(lines - 1, z)]
     near = [(x, 1 - c), (1 - x, c), (1 - x, 1 - c)]
     to_near = [me.at(x=xx, c=cc) for xx, cc in near]
     to_y, to_x, to_c = me.at(y=1 - y), to_near[1], to_near[0]
-    greet([me.at(z=o) for o in others] + [to_y] + to_near)
+    last, kva_at, o_at = jobs - 1, jobs, jobs + 1
+    wide_lines = [
+        LineGather(me, lines, lambda p, i=i: dests[i].at[p], line_sems[i]) for i in range(last)
+    ]
+    q_line = LineGather(me, lines, lambda p: dests[last].at[p, y], line_sems[last])
+    kva_line = LineGather(me, lines, lambda p: kva_dst.at[p, y, x, c], line_sems[kva_at])
+    greet([*q_line.to, to_y] + to_near)
     copies = Copies()
     go = copies.go
 
-    def span(i, k):
-        rows = plane_src[i].shape[0] // counts[i]
-        return pl.ds(k * rows, rows)
-
-    def plane_z_start(i, k):
-        zs_, zr_, ys_, yr_ = plane_sems[i][:4]
-        src, dst = plane_src[i].at[span(i, k)], plane_dst[i].at[z, y, x, c, span(i, k)]
-        for j, o in enumerate(others):
-            go(remote(src, dst, zs_.at[k, j], zr_.at[k, z], me.at(z=o)))
-        go(remote(src, dst, ys_.at[k, lines - 1], yr_.at[k, z], to_y))
-
-    def plane_z_land(i, k):
-        zs_, zr_, ys_, yr_ = plane_sems[i][:4]
-        for j, o in reversed(places[:-1]):
-            block = plane_dst[i].at[o, y, x, c, span(i, k)]
-            remote(block, block, zs_.at[k, j], zr_.at[k, o], me.at(z=o)).wait_recv()
-            go(remote(block, block, ys_.at[k, j], yr_.at[k, o], to_y))
-
-    def plane_y_land(i, k):
-        ys_, yr_, ps, pr = plane_sems[i][2:]
-        for j, o in places:
-            block = plane_dst[i].at[o, 1 - y, x, c, span(i, k)]
-            remote(block, block, ys_.at[k, j], yr_.at[k, o], to_y).wait_recv()
-        block = plane_dst[i].at[:, :, x, c, span(i, k)]
-        go(remote(block, block, ps.at[k, 0], pr.at[k, 0], to_x))
-        go(remote(block, block, ps.at[k, 1], pr.at[k, 1], to_c))
-
-    def plane_x_land(i, k):
-        ps, pr = plane_sems[i][4:]
-        block = plane_dst[i].at[:, :, 1 - x, c, span(i, k)]
-        remote(block, block, ps.at[k, 0], pr.at[k, 0], to_x).wait_recv()
-        go(remote(block, block, ps.at[k, 2], pr.at[k, 2], to_c))
-
-    def plane_c_land(i, k):
-        ps, pr = plane_sems[i][4:]
-        for slot, xx in ((1, x), (2, 1 - x)):
-            block = plane_dst[i].at[:, :, xx, 1 - c, span(i, k)]
-            remote(block, block, ps.at[k, slot], pr.at[k, slot], to_c).wait_recv()
+    def over_y(i, p):
+        if i < last:
+            block = dests[i].at[z, y]
+        elif i == last:
+            block = dests[i].at[p, y]
+        elif i == kva_at:
+            block = kva_dst.at[p, y, x, c]
+        else:
+            block = o_dst.at[p]
+        return remote(block, block, ys.at[i, p], yr.at[i, p], to_y)
+
+    def from_y(i, p):
+        if i < last:
+            block = dests[i].at[z, 1 - y]
+        elif i == last:
+            block = dests[i].at[p, 1 - y]
+        elif i == kva_at:
+            block = kva_dst.at[p, 1 - y, x, c]
+        else:
+            block = o_dst.at[p]
+        return remote(block, block, ys.at[i, p], yr.at[i, p], to_y)
 
     locals_ = [
-        pltpu.make_async_copy(src, dst.at[z, y, x, c], own_sem.at[i])
-        for i, (src, dst) in enumerate(
-            zip([v.at[x, c] for v in sources] + plane_src, dests + plane_dst)
-        )
+        pltpu.make_async_copy(sources[i].at[x, c], dests[i].at[z, y, x, c], own_sem.at[i])
+        for i in range(jobs)
     ]
-    locals_.append(pltpu.make_async_copy(tok, tok_dst.at[x, c], own_sem.at[jobs + planes]))
+    locals_.append(pltpu.make_async_copy(kva, kva_dst.at[z, y, x, c], own_sem.at[jobs]))
+    locals_.append(pltpu.make_async_copy(tok, tok_dst.at[x, c], own_sem.at[jobs + 1]))
     for copy in locals_:
         copy.start()
-
-    for i in range(jobs):
+    for i in (last, *range(last)):
         for p in range(3):
             go(
                 remote(
@@ -398,13 +435,10 @@
                     to_near[p],
                 )
             )
-    last = planes - 1
-    plane_z_start(last, 0)
-    if counts[last] > 1:
-        plane_z_start(last, 1)
     if with_o:
         o_core = remote(o_src, o_dst.at[z, c], ocs, ocr, to_c)
         o_local = pltpu.make_async_copy(o_src, o_dst.at[z, c], o_own)
+        o_line = LineGather(me, lines, lambda p: o_dst.at[p], line_sems[o_at])
         holder = c == y
 
         @pl.when(jnp.logical_not(holder))
@@ -417,130 +451,117 @@
 
     go(remote(tok, tok_dst.at[x, c], ts.at[1], tr.at[1], to_x))
     go(remote(tok, tok_dst.at[x, c], ts.at[0], tr.at[0], to_c))
-    line_y = lambda i, j, o: remote(
-        dests[i].at[o, y], dests[i].at[o, y], ys.at[i, j], yr.at[i, o], to_y
-    )
-    line_z = lambda i, j, o: remote(
-        dests[i].at[z, y], dests[i].at[z, y], zs.at[i, j], zr.at[i, z], me.at(z=o)
-    )
-
-    def job_start(i):
+
+    def near_land(i):
         locals_[i].wait()
         for p in range(3):
             xx, cc = near[p]
             block = dests[i].at[z, y, xx, cc]
             remote(block, block, gs.at[i, p], gr.at[i, p], to_near[p]).wait_recv()
-        for j, o in enumerate(others):
-            go(line_z(i, j, o))
-        go(line_y(i, lines - 1, z))
-
-    job_start(0)
-    job_start(1)
-    plane_z_land(last, 0)
-    for k in range(1, counts[last]):
-        if k + 1 < counts[last]:
-            plane_z_start(last, k + 1)
-        plane_z_land(last, k)
-        if k == 1:
-            job_start(2)
-        locals_[jobs + last].wait() if k == 1 else None
-        plane_y_land(last, k - 1)
-    if counts[last] == 1:
-        job_start(2)
-        locals_[jobs + last].wait()
+
+    locals_[jobs].wait()
+    kva_line.start()
+    go(over_y(kva_at, z))
+    near_land(last)
+    q_line.start()
+    go(over_y(last, z))
+    for i in range(last):
+        near_land(i)
+        go(over_y(i, z))
     if with_o:
-        o_z = lambda j, o: remote(o_dst.at[z], o_dst.at[z], ozs.at[j], ozr.at[z], me.at(z=o))
-        o_y = lambda j, o: remote(o_dst.at[o], o_dst.at[o], oys.at[j], oyr.at[o], to_y)
 
         @pl.when(holder)
         def _():
             o_local.wait()
             block = o_dst.at[z, 1 - c]
             remote(block, block, ocs, ocr, to_c).wait_recv()
-            for j, o in enumerate(others):
-                o_z(j, o).start()
-            o_y(lines - 1, z).start()
-
-    for i in range(last):
-        for k in range(counts[i]):
-            plane_z_start(i, k)
-    plane_y_land(last, counts[last] - 1)
+            o_line.start()
+            over_y(o_at, z).start()
+
+    for distance in range(1, lines):
+        kva_line.land(distance, lambda p: over_y(kva_at, p).start())
     block = tok_dst.at[1 - x, c]
     remote(block, block, ts.at[1], tr.at[1], to_x).wait_recv()
     go(remote(block, block, ts.at[2], tr.at[2], to_c))
-    for j, o in reversed(places[:-1]):
-        for i in range(jobs):
-            block = dests[i].at[o, y]
-            remote(block, block, zs.at[i, j], zr.at[i, o], me.at(z=o)).wait_recv()
-            go(line_y(i, j, o))
+    for distance in range(1, lines):
+        q_line.land(distance, lambda p: over_y(last, p).start())
         if with_o:
 
             @pl.when(holder)
-            def _(j=j, o=o):
-                block = o_dst.at[o]
-                remote(block, block, ozs.at[j], ozr.at[o], me.at(z=o)).wait_recv()
-                o_y(j, o).start()
-
-    for i in range(last):
-        for k in range(counts[i]):
-            plane_z_land(i, k)
-    for k in range(counts[last]):
-        plane_x_land(last, k)
-    for i in range(last):
-        locals_[jobs + i].wait()
-        for k in range(counts[i]):
-            plane_y_land(i, k)
-            plane_x_land(i, k)
+            def _(distance=distance):
+                o_line.land(distance, lambda p: over_y(o_at, p).start())
+
+        if distance == 1:
+            for p in range(lines):
+                from_y(kva_at, p).wait_recv()
+            plane = kva_dst.at[:, :, x, c]
+            go(remote(plane, plane, ks.at[0], kr.at[0], to_x))
+            go(remote(plane, plane, ks.at[1], kr.at[1], to_c))
+        if distance == lines - 2:
+            for i in range(last):
+                from_y(i, z).wait_recv()
+                wide_lines[i].start()
+            plane = kva_dst.at[:, :, 1 - x, c]
+            remote(plane, plane, ks.at[0], kr.at[0], to_x).wait_recv()
+            go(remote(plane, plane, ks.at[2], kr.at[2], to_c))
+    for distance in range(1, lines):
+        for one in wide_lines:
+            one.land(distance)
     for slot, xx in ((0, x), (2, 1 - x)):
         block = tok_dst.at[xx, 1 - c]
         remote(block, block, ts.at[slot], tr.at[slot], to_c).wait_recv()
-    locals_[jobs + planes].wait()
-    for j, o in places:
-        for i in range(jobs):
-            block = dests[i].at[o, 1 - y]
-            remote(block, block, ys.at[i, j], yr.at[i, o], to_y).wait_recv()
+    locals_[jobs + 1].wait()
+    for p in range(lines):
+        from_y(last, p).wait_recv()
     if with_o:
 
         @pl.when(jnp.logical_not(holder))
         def _():
-            for j, o in places:
-                remote(o_dst.at[o], o_dst.at[o], oys.at[j], oyr.at[o], to_y).wait_recv()
+            for p in range(lines):
+                from_y(o_at, p).wait_recv()
             o_core.wait_send()
 
         @pl.when(holder)
         def _():
-            for j, o in enumerate(others):
-                o_z(j, o).wait_send()
-            for j, o in places:
-                o_y(j, o).wait_send()
-
-    for i in range(planes):
-        for k in range(counts[i]):
-            plane_c_land(i, k)
+            for p in range(lines):
+                over_y(o_at, p).wait_send()
+            o_line.finish()
+
+    for slot, xx in ((1, x), (2, 1 - x)):
+        plane = kva_dst.at[:, :, xx, 1 - c]
+        remote(plane, plane, ks.at[slot], kr.at[slot], to_c).wait_recv()
+    for one in wide_lines + [q_line, kva_line]:
+        one.finish()
+    for i in (last, kva_at):
+        for p in range(lines):
+
+            @pl.when(z != p)
+            def _(i=i, p=p):
+                over_y(i, p).wait_send()
+
     copies.finish()
 
 
-def start_gather(tokens, planes, counts, column_parts, o_rows, lines, ident):
+def start_gather(tokens, kva, column_parts, o_rows, lines, ident):
     jobs = len(column_parts)
     with_o = o_rows is not None
-    inputs = [tokens] + planes + column_parts + ([o_rows] if with_o else [])
+    inputs = [tokens, kva] + column_parts + ([o_rows] if with_o else [])
     shape = lambda lead, v: jax.ShapeDtypeStruct(lead + v.shape, v.dtype)
-    outs = [shape((2, 2), tokens)] + [shape((lines, 2, 2, 2), v) for v in planes]
+    outs = [shape((2, 2), tokens), shape((lines, 2, 2, 2), kva)]
     outs += [jax.ShapeDtypeStruct((lines, 2) + v.shape, v.dtype) for v in column_parts]
     if with_o:
         outs.append(shape((lines, 2), o_rows))
     dma = pltpu.SemaphoreType.DMA
     scratch = [
-        dma((jobs + len(planes) + 1,)), dma((jobs, 3)), dma((jobs, 3)),
-        dma((jobs, lines)), dma((jobs, lines)), dma((jobs, lines)), dma((jobs, lines)),
-        dma((3,)), dma((3,)),
+        dma((jobs + 2,)), dma((jobs, 3)), dma((jobs, 3)),
+        dma((jobs + 2, lines)), dma((jobs + 2, lines)),
+        dma((3,)), dma((3,)), dma((3,)), dma((3,)),
     ]
-    for n in counts:
-        scratch += [dma((n, lines))] * 4 + [dma((n, 3))] * 2
+    scratch += [dma((lines,))] * (4 * (jobs + 1 + with_o))
     if with_o:
-        scratch += [dma, dma, dma, dma((lines,)), dma((lines,)), dma((lines,)), dma((lines,))]
+        scratch += [dma] * 3
     return pl.pallas_call(
-        functools.partial(start_kernel, lines, tuple(counts), with_o),
+        functools.partial(start_kernel, lines, with_o),
         out_shape=outs,
         in_specs=[HBM] * len(inputs),
         out_specs=[HBM] * len(outs),
@@ -1467,8 +1488,7 @@
     rounds = max(1, tok_rows * device_count // 4096)
     started = start_gather(
         tokens,
-        [kva_weight],
-        [1],
+        kva_weight,
         [
             jnp.broadcast_to(small_own, (2, 2) + small_own.shape),
             by_head(kvb_weight),

time: 745 us -> 728 us (0.977)
  starting transfers between devices: 23.9 us -> 11.7 us
    all_to_all x1, starting transfers between devices: 15.6 us -> 3.38 us  [on_device(): lax.all_to_all(both_shared.transpose(2, 0, 1, 3), BOTH, split_axis=0, con...]
  transfers between devices with their start and end apart: 4 -> 4, of which waited for: 1 -> 1; matrix products, arithmetic and copies ran while one was open for 13% -> 14% of each run, Pallas kernels for 27% -> 27%
where the time goes in v5:
time: 728 us; the launch traced here: 716 us
  Pallas kernels  529 us (73%)
  local copies, waits for them, and re-layouts  75.6 us (10%)
  matrix products  44.6 us (6%)
  other arithmetic  19.8 us (3%)
  waiting for transfers between devices  19 us (3%)
  between operations  16.4 us (2%)
  starting transfers between devices  11.7 us (2%)
    pallas_call x1, Pallas kernels, sum_grads(): pl.pallas_call(functools.partial(grads_kernel, lines, plane, with_o, span...  150 us
    pallas_call x1, Pallas kernels, gather_hidden(): pl.pallas_call(functools.partial(hidden_kernel, lines, chunks, spans, loc...  139 us
    pallas_call x1, Pallas kernels, sum_back(): pl.pallas_call(functools.partial(back_kernel, lines), out_shape=[jax.Shap...  100 us
    pallas_call x1, Pallas kernels, start_gather(): pl.pallas_call(functools.partial(start_kernel, lines, with_o), out_shape=...  93.1 us
    unnamed x184, local copies, waits for them, and re-layouts  31.5 us
    pallas_call x1, Pallas kernels, gather_group(): pl.pallas_call(functools.partial(gather_group_kernel, cuts, spans if work...  27.2 us
    all_gather x1, waiting for transfers between devices, gather(): return lax.all_gather(value, axes, axis=0, tiled=True)  19 us
    pallas_call x1, Pallas kernels, sum_group(): pl.pallas_call(functools.partial(sum_group_kernel, cuts), out_shape=jax.S...  16.2 us
  transfers between devices with their start and end apart: 4, of which 1 were waited for; matrix products, arithmetic and copies ran while one was open for 14% of the time, Pallas kernels for 27%

profile of v5, /device:TPU:0, one launch (start us, length us, event | category | flops | bytes accessed | tf_op | source)
XLA Modules:
  0.0 715.8 jit_solution(16802762904357167728)
XLA Ops:
  8.2 2.1 concatenate.42
  10.2 1.0 reshape.580
  12.0 1.6 reshape.582
  13.9 1.2 reshape.583.refs_4_
  15.7 93.1 %shard_map.306 = (bf16[2,2,128,2048]{3,2,1,0:T(8,128)(2,1)}, bf16[4,2,2,2,64,576]{5,4,3,2,1,0:T(8,128)(2,1)}, bf16[4,2,2,2,16,128]{5,4,3,2,1,0:T(8,128)(2,1)}, b...) custom-call(bf16[128,2048]{1,0:T(8,128)(2,1)} %refs_0_.1, ...), custom_call_target="tpu_custom_call" | custom-call | tf_op jit(solution)/shard_map/pallas_call | solution.py:563
  108.9 1.1 slice.128
  111.5 1.3 stack.16
  112.8 1.3 stack.17
  114.4 1.4 copy.173
  115.8 3.4 all-to-all-start
  119.7 1.2 reshape.593
  121.9 1.6 copy-done.79
  123.5 1.4 fusion.65
  125.2 1.8 convolution_convert_fusion.5
  127.0 2.3 reshape.586
  129.3 1.2 fusion.62
  130.4 1.5 copy.201
  131.9 4.6 copy.166
  137.3 0.9 fusion.35
  138.2 4.4 fusion.66
  143.8 1.2 fusion.64
  148.3 1.3 convolution_convert_fusion.3
  149.6 16.2 %shard_map.307 = f32[128,2048]{1,0:T(8,128)S(1)} custom-call(bf16[2,2,128,2048]{3,2,1,0:T(8,128)(2,1)S(1)} %bitcast.139), custom_call_target="tpu_custom_call" | custom-call | tf_op jit(solution)/shard_map/pallas_call | solution.py:260
  168.6 1.8 pad.18.s_down
  170.4 1.1 concatenate.45.src
  172.4 1.3 copy.174
  173.7 1.2 copy.175
  174.9 2.2 pad.17.s_in
  177.1 19.0 %all-gather.2.cloned.1.call-done.refs_2_.refs_7_ = bf16[4096,1024]{1,0:T(8,128)(2,1)} async-done(((bf16[128,1024]{1,0:T(8,128)(2,1)}), bf16[4096,1024]{1,0:T(8,128)(2,1)}) %all-gather.2.cloned.1.call-update) | async-done | bytes 8388624 | tf_op jit(solution)/shard_map/all_gather | solution.py:96
  196.0 138.9 %shard_map.308 = (bf16[4,2,2,2,128,3200]{5,4,3,2,1,0:T(8,128)(2,1)}, bf16[4,2,2,2,128,896]{5,4,3,2,1,0:T(8,128)(2,1)}, bf16[4,2,2,2,128,1792]{5,4,3,2,1,0:T(8,12...) custom-call(bf16[128,3200]{1,0:T(8,128)(2,1)} %concatenate.45.src, ...), custom_call_target="tpu_custom_call" | custom-call | tf_op jit(solution)/shard_map/pallas_call | solution.py:1146
  334.9 100.1 %shard_map.309 = (f32[128,2176]{1,0:T(8,128)}, bf16[4,2,2,2,128,2048]{5,4,3,2,1,0:T(8,128)(2,1)}) custom-call(bf16[4,2,2,2,128,1792]{5,4,3,2,1,0:T(8,128)(2,1)} %get-tuple-element.55.in_d, bf16[4,2,2,2,128,128]{5,4,3,2,1,0:T(8,128)(2,1)} %get-tuple-element.56.gate_g, bf16[1792,2048]{1,0:T(8,128)(2,1)} %get-tuple-element.57.w_in, ...), custom_call_target="tpu_custom_call", output_to_operand_aliasing={{1}: (3, {})} | custom-call | tf_op jit(solution)/shard_map/pallas_call | solution.py:1397
  437.3 1.9 multiply_reduce_fusion.3
  440.0 1.3 fusion.69
  441.3 2.5 reshape.609
  443.8 1.4 fusion.60.refs_0_
  445.2 3.1 copy-done
  448.3 27.2 %shard_map.310 = (bf16[2,2,128,2048]{3,2,1,0:T(8,128)(2,1)S(1)}, f32[1,88,2048]{2,1,0:T(8,128)S(1)}, f32[1,88,2048]{2,1,0:T(8,128)S(1)}, f32[1,88,2048]{2,1,0:T(8,128)S(1)}) custom-call(bf16[128,2048]{1,0:T(8,128)(2,1)S(1)} %fusion.60.refs_0_, bf16[4096,3200]{1,0:T(8,128)(2,1)} %bitcast.145, bf16[4096,1024]{1,0:T(8,128)(2,1)} %all-gather.2.cloned.1.call-done.refs_2_.refs_7_, ...), custom_call_target="tpu_custom_call" | custom-call | tf_op jit(solution)/shard_map/pallas_call | solution.py:200
  475.6 1.3 copy-done.5
  476.9 1.0 copy.187
  478.7 2.1 copy.188
  480.9 2.4 maximum_bitcast_fusion.1
  483.3 8.2 %all-to-all-start.1 = ((bf16[32,2,64,88]{3,2,1,0:T(8,128)(2,1)}), bf16[32,2,64,88]{3,2,1,0:T(8,128)(2,1)}, u32[]{:S(2)}, u32[]{:S(2)}) async-start(bf16[32,2,64,88]{3,2,1,0:T(8,128)(2,1)} %maximum_bitcast_fusion.1), calls=%async_computation.2 | async-start | bytes 2097152 | tf_op jit(solution)/shard_map/all_to_all | solution.py:1654
  491.6 3.1 convolution_convert_fusion.6
  494.6 0.9 multiply_reduce_fusion.1
  495.6 1.2 multiply_convert_fusion.1
  499.4 1.8 multiply_reduce_fusion.2
  501.9 2.3 fusion.13
  507.8 1.8 fusion.68
  510.2 3.7 fusion.61
  514.1 3.5 convolution_convert_fusion.4
  517.6 3.2 convolution_convert_fusion.1
  521.6 4.3 copy.182
  526.0 2.6 convolution_convert_fusion.2
  528.5 3.5 convolution_convert_fusion
  532.1 149.9 %shard_map.311 = (bf16[2,2,16,1024]{3,2,1,0:T(8,128)(2,1)}, bf16[64,576]{1,0:T(8,128)(2,1)}, bf16[2,2,64,768]{3,2,1,0:T(8,128)(2,1)}, f32[2,2,16,128]{3,2,1,0:T(...) custom-call(bf16[4,2,2,2,16,1024]{5,4,3,2,1,0:T(8,128)(2,1)} %bitcas, ...), custom_call_target="tpu_custom_call" | custom-call | tf_op jit(solution)/shard_map/pallas_call | solution.py:879
  684.2 1.7 fusion.17
  686.5 1.0 copy-done.1
  687.5 0.9 copy-done.2
  690.2 3.3 shard_map.312
  693.6 3.3 fusion.20
  697.7 2.9 copy.221
  700.7 1.8 copy-done.23
  702.4 2.8 copy.222
  706.0 2.5 copy.223
  (271 shorter events, 32.2 us)
Async XLA Ops:
  7.2 103.5 %copy-start.26 = (bf16[128,2048]{1,0:T(8,128)(2,1)S(1)}, bf16[128,2048]{1,0:T(8,128)(2,1)}, u32[]{:S(2)}) copy-start(bf16[128,2048]{1,0:T(8,128)(2,1)} %param.20) | copy-start | bytes 1572868
  7.2 188.9 %all-gather.2.cloned.1.call-start = ((), (), s32[]{:S(2)}) async-start(), calls=%async_computation.3 | async-start | bytes 8650752 | tf_op jit(solution)/shard_map/all_gather | solution.py:96
  12.0 99.5 %copy-start.46 = (bf16[64,2816]{1,0:T(8,128)(2,1)S(1)}, bf16[64,2816]{1,0:T(8,128)(2,1)}, u32[]{:S(2)}) copy-start(bf16[64,2816]{1,0:T(8,128)(2,1)} %param.29) | copy-start | bytes 1081348
  13.7 99.2 %copy-start.47 = (bf16[64,2816]{1,0:T(8,128)(2,1)S(1)}, bf16[64,2816]{1,0:T(8,128)(2,1)}, u32[]{:S(2)}) copy-start(bf16[64,2816]{1,0:T(8,128)(2,1)} %param.30) | copy-start | bytes 1081348
  114.4 4.8 copy-start.53
  114.4 6.5 copy-start.18
  115.8 56.6 %all-to-all-start = ((bf16[32,2,64,88]{3,2,1,0:T(8,128)(2,1)}), bf16[32,2,64,88]{3,2,1,0:T(8,128)(2,1)}, u32[]{:S(2)}, u32[]{:S(2)}) async-start(bf16[32,2,64,88]{3,2,1,0:T(8,128)(2,1)} %copy.173), calls=%async_computation | async-start | bytes 2097152 | tf_op jit(solution)/shard_map/all_to_all | solution.py:1483
  119.1 574.4 %reduce-scatter.2.cloned.1.call-start = ((), (), s32[]{:S(2)}) async-start(), calls=%async_computation.4 | async-start | bytes 17301504 | tf_op jit(solution)/shard_map/reduce_scatter | solution.py:100
  119.4 5.7 copy-start.60
  119.7 2.3 copy-start.51
  121.3 2.2 copy-start.79
  121.4 3.6 copy-start.69
  121.9 3.1 copy-start.33
  125.0 12.3 %copy-start.15 = (f32[512,576]{0,1:T(8,128)}, f32[512,576]{0,1:T(8,128)S(1)}, u32[]{:S(2)}) copy-start(f32[512,576]{0,1:T(8,128)S(1)} %fusion.65) | copy-start | bytes 3538948
  130.4 12.3 %copy-start.27 = (bf16[512,4,128]{2,1,0:T(4,128)(2,1)}, bf16[512,4,128]{2,1,0:T(4,128)(2,1)S(1)}, u32[]{:S(2)}) copy-start(bf16[512,4,128]{2,1,0:T(4,128)(2,1)S(1)} %get-tuple-element.180) | copy-start | bytes 1572868
  131.9 4.7 copy-start.55
  136.9 5.7 copy-start.73
  137.0 5.6 copy-start.58
  138.2 5.6 copy-start.48
  138.2 5.6 copy-start.49
  145.1 2.0 copy-start.7
  145.7 2.6 copy-start.81
  149.6 16.2 %copy-start.21 = (bf16[128,2048]{1,0:T(8,128)(2,1)S(1)}, bf16[128,2048]{1,0:T(8,128)(2,1)}, u32[]{:S(2)}) copy-start(bf16[128,2048]{1,0:T(8,128)(2,1)} %refs_0_.1) | copy-start | bytes 1572868
  165.9 2.1 copy-start.84
  166.7 277.1 %copy-start.11 = (f32[128,2048]{1,0:T(8,128)}, f32[128,2048]{1,0:T(8,128)S(1)}, u32[]{:S(2)}) copy-start(f32[128,2048]{1,0:T(8,128)S(1)} %get-tuple-element.171) | copy-start | bytes 3145732
  166.7 3.7 copy-start.38
  167.9 3.6 copy-start.71
  435.0 2.2 copy-start.72
  435.0 2.2 copy-start.67
  439.2 6.0 copy-start.13
  445.2 3.1 copy-start
  478.7 12.8 %copy-start.6 = (bf16[2,2,128,2048]{3,2,1,0:T(8,128)(2,1)S(1)}, bf16[2,2,128,2048]{3,2,1,0:T(8,128)(2,1)}, u32[]{:S(2)}) copy-start(bf16[2,2,128,2048]{3,2,1,0:T(8,128)(2,1)} %copy-done.5) | copy-start | bytes 6291460
  483.3 203.2 %all-to-all-start.1 = ((bf16[32,2,64,88]{3,2,1,0:T(8,128)(2,1)}), bf16[32,2,64,88]{3,2,1,0:T(8,128)(2,1)}, u32[]{:S(2)}, u32[]{:S(2)}) async-start(bf16[32,2,64,88]{3,2,1,0:T(8,128)(2,1)} %maximum_bitcast_fusion.1), calls=%async_computation.2 | async-start | bytes 2097152 | tf_op jit(solution)/shard_map/all_to_all | solution.py:1654
  491.6 3.1 copy-start.8
  498.8 2.4 copy-start.31
  501.2 3.1 copy-start.28
  501.9 2.3 copy-start.50
  501.9 2.4 copy-start.10
  504.9 1.9 copy-start.37
  505.0 2.0 copy-start.39
  505.1 2.6 copy-start.32
  507.0 2.7 copy-start.44
  507.8 1.9 copy-start.19
  507.8 1.9 copy-start.70
  507.8 2.4 copy-start.80
  510.2 3.8 copy-start.43
  510.2 3.8 copy-start.56
  510.2 3.8 copy-start.57
  513.9 3.7 copy-start.52
  514.1 3.5 copy-start.20
  514.1 3.5 copy-start.45
  520.8 5.1 copy-start.42
  526.0 2.6 copy-start.34
  526.0 2.6 copy-start.40
  532.1 152.1 %copy-start.75 = (f32[128]{0:T(128)S(1)}, f32[128]{0:T(128)}, u32[]{:S(2)}) copy-start(f32[128]{0:T(128)} %add_rsqrt_fusion.2) | copy-start | bytes 1540
  682.0 11.5 %copy-start.12 = (f32[128,2048]{1,0:T(8,128)S(1)}, f32[128,2048]{1,0:T(8,128)}, u32[]{:S(2)}) copy-start(f32[128,2048]{1,0:T(8,128)} %copy-done.11) | copy-start | bytes 3145732
  682.0 11.5 %copy-start.22 = (bf16[128,2048]{1,0:T(8,128)(2,1)S(1)}, bf16[128,2048]{1,0:T(8,128)(2,1)}, u32[]{:S(2)}) copy-start(bf16[128,2048]{1,0:T(8,128)(2,1)} %refs_0_.1) | copy-start | bytes 1572868
  682.0 11.5 %copy-start.68 = (f32[128]{0:T(128)S(1)}, f32[128]{0:T(128)}, u32[]{:S(2)}) copy-start(f32[128]{0:T(128)} %copy-done.66) | copy-start | bytes 1540
  682.0 11.5 %copy-start.77 = (f32[128]{0:T(128)S(1)}, f32[128]{0:T(128)}, u32[]{:S(2)}) copy-start(f32[128]{0:T(128)} %copy-done.76) | copy-start | bytes 1540
  690.2 3.3 copy-start.14
  693.6 4.1 copy-start.24
  697.7 4.7 copy-start.23
  697.7 7.5 %slice-start = ((s8[5767168]{0:T(1024)(128)(4,1)}), s8[4194304]{0:T(1024)(128)(4,1)S(1)}, s32[]{:S(2)}) async-start(s8[5767168]{0:T(1024)(128)(4,1)} %bitcast.152), calls=%async_computation.5 | async-start | bytes 8388608
  702.4 3.6 slice-start.1
  (27 other events, 34.4 us)
Sparse Core Ops, SparseCore 0:
  111.6 84.3 all-gather.1
  435.2 234.0 reduce-scatter.1

commit v6 on v5

--- a/solution.py
+++ b/solution.py
@@ -1031,6 +1031,8 @@
             z_copy(k, j, o).start()
 
     z_start(0)
+    if chunks > 1:
+        z_start(1)
     for k in range(chunks):
         x_copy(k, lines - 1, z, piece(k)).start()
         y_copy(k, lines - 1, z, piece(k)).start()
@@ -1060,8 +1062,6 @@
 
     own.wait()
     z_land(0)
-    if chunks > 1:
-        z_start(1)
     fetch(0, 0)
     valid = lambda k: (k >= 0) & (k < chunks)
 

time: 728 us -> 724 us (level)
  transfers between devices with their start and end apart: 4 -> 4, of which waited for: 1 -> 1; matrix products, arithmetic and copies ran while one was open for 14% -> 14% of each run, Pallas kernels for 27% -> 28%
where the time goes in v6:
time: 724 us; the launch traced here: 711 us
  Pallas kernels  524 us (72%)
  local copies, waits for them, and re-layouts  75.6 us (10%)
  matrix products  44.6 us (6%)
  other arithmetic  19.7 us (3%)
  waiting for transfers between devices  19 us (3%)
  between operations  16.4 us (2%)
  starting transfers between devices  11.4 us (2%)
    pallas_call x1, Pallas kernels, sum_grads(): pl.pallas_call(functools.partial(grads_kernel, lines, plane, with_o, span...  151 us
    pallas_call x1, Pallas kernels, gather_hidden(): pl.pallas_call(functools.partial(hidden_kernel, lines, chunks, spans, loc...  139 us
    pallas_call x1, Pallas kernels, sum_back(): pl.pallas_call(functools.partial(back_kernel, lines), out_shape=[jax.Shap...  94.9 us
    pallas_call x1, Pallas kernels, start_gather(): pl.pallas_call(functools.partial(start_kernel, lines, with_o), out_shape=...  93.1 us
    unnamed x184, local copies, waits for them, and re-layouts  31.5 us
    pallas_call x1, Pallas kernels, gather_group(): pl.pallas_call(functools.partial(gather_group_kernel, cuts, spans if work...  27.2 us
    all_gather x1, waiting for transfers between devices, gather(): return lax.all_gather(value, axes, axis=0, tiled=True)  19 us
    pallas_call x1, Pallas kernels, sum_group(): pl.pallas_call(functools.partial(sum_group_kernel, cuts), out_shape=jax.S...  16.2 us
  transfers between devices with their start and end apart: 4, of which 1 were waited for; matrix products, arithmetic and copies ran while one was open for 14% of the time, Pallas kernels for 28%

profile of v6, /device:TPU:0, one launch (start us, length us, event | category | flops | bytes accessed | tf_op | source)
XLA Modules:
  0.0 711.1 jit_solution(17424834341902931870)
XLA Ops:
  8.2 2.1 concatenate.42
  10.2 1.0 reshape.580
  12.0 1.6 reshape.582
  13.9 1.2 reshape.583.refs_4_
  15.7 93.1 %shard_map.306 = (bf16[2,2,128,2048]{3,2,1,0:T(8,128)(2,1)}, bf16[4,2,2,2,64,576]{5,4,3,2,1,0:T(8,128)(2,1)}, bf16[4,2,2,2,16,128]{5,4,3,2,1,0:T(8,128)(2,1)}, b...) custom-call(bf16[128,2048]{1,0:T(8,128)(2,1)} %refs_0_.1, ...), custom_call_target="tpu_custom_call" | custom-call | tf_op jit(solution)/shard_map/pallas_call | solution.py:563
  108.9 1.1 slice.128
  111.5 1.3 stack.16
  112.8 1.3 stack.17
  114.4 1.4 copy.173
  115.8 3.4 all-to-all-start
  119.7 1.2 reshape.593
  121.9 1.6 copy-done.79
  123.5 1.4 fusion.65
  125.2 1.8 convolution_convert_fusion.5
  127.0 2.3 reshape.586
  129.3 1.2 fusion.62
  130.4 1.5 copy.201
  131.9 4.6 copy.166
  137.3 0.9 fusion.35
  138.2 4.4 fusion.66
  143.8 1.2 fusion.64
  148.3 1.3 convolution_convert_fusion.3
  149.6 16.2 %shard_map.307 = f32[128,2048]{1,0:T(8,128)S(1)} custom-call(bf16[2,2,128,2048]{3,2,1,0:T(8,128)(2,1)S(1)} %bitcast.139), custom_call_target="tpu_custom_call" | custom-call | tf_op jit(solution)/shard_map/pallas_call | solution.py:260
  168.6 1.8 pad.18.s_down
  170.4 1.1 concatenate.45.src
  172.4 1.3 copy.174
  173.7 1.2 copy.175
  174.9 2.2 pad.17.s_in
  177.1 19.0 %all-gather.2.cloned.1.call-done.refs_2_.refs_7_ = bf16[4096,1024]{1,0:T(8,128)(2,1)} async-done(((bf16[128,1024]{1,0:T(8,128)(2,1)}), bf16[4096,1024]{1,0:T(8,128)(2,1)}) %all-gather.2.cloned.1.call-update) | async-done | bytes 8388624 | tf_op jit(solution)/shard_map/all_gather | solution.py:96
  196.0 138.9 %shard_map.308 = (bf16[4,2,2,2,128,3200]{5,4,3,2,1,0:T(8,128)(2,1)}, bf16[4,2,2,2,128,896]{5,4,3,2,1,0:T(8,128)(2,1)}, bf16[4,2,2,2,128,1792]{5,4,3,2,1,0:T(8,12...) custom-call(bf16[128,3200]{1,0:T(8,128)(2,1)} %concatenate.45.src, ...), custom_call_target="tpu_custom_call" | custom-call | tf_op jit(solution)/shard_map/pallas_call | solution.py:1146
  334.9 94.9 %shard_map.309 = (f32[128,2176]{1,0:T(8,128)}, bf16[4,2,2,2,128,2048]{5,4,3,2,1,0:T(8,128)(2,1)}) custom-call(bf16[4,2,2,2,128,1792]{5,4,3,2,1,0:T(8,128)(2,1)} %get-tuple-element.55.in_d, bf16[4,2,2,2,128,128]{5,4,3,2,1,0:T(8,128)(2,1)} %get-tuple-element.56.gate_g, bf16[1792,2048]{1,0:T(8,128)(2,1)} %get-tuple-element.57.w_in, ...), custom_call_target="tpu_custom_call", output_to_operand_aliasing={{1}: (3, {})} | custom-call | tf_op jit(solution)/shard_map/pallas_call | solution.py:1397
  432.1 1.9 multiply_reduce_fusion.3
  434.9 1.3 fusion.69
  436.2 2.5 reshape.609
  438.7 1.4 fusion.60.refs_0_
  440.1 3.1 copy-done
  443.2 27.2 %shard_map.310 = (bf16[2,2,128,2048]{3,2,1,0:T(8,128)(2,1)S(1)}, f32[1,88,2048]{2,1,0:T(8,128)S(1)}, f32[1,88,2048]{2,1,0:T(8,128)S(1)}, f32[1,88,2048]{2,1,0:T(8,128)S(1)}) custom-call(bf16[128,2048]{1,0:T(8,128)(2,1)S(1)} %fusion.60.refs_0_, bf16[4096,3200]{1,0:T(8,128)(2,1)} %bitcast.145, bf16[4096,1024]{1,0:T(8,128)(2,1)} %all-gather.2.cloned.1.call-done.refs_2_.refs_7_, ...), custom_call_target="tpu_custom_call" | custom-call | tf_op jit(solution)/shard_map/pallas_call | solution.py:200
  470.5 1.3 copy-done.5
  471.8 1.0 copy.187
  473.6 2.1 copy.188
  475.8 2.4 maximum_bitcast_fusion.1
  478.2 8.0 %all-to-all-start.1 = ((bf16[32,2,64,88]{3,2,1,0:T(8,128)(2,1)}), bf16[32,2,64,88]{3,2,1,0:T(8,128)(2,1)}, u32[]{:S(2)}, u32[]{:S(2)}) async-start(bf16[32,2,64,88]{3,2,1,0:T(8,128)(2,1)} %maximum_bitcast_fusion.1), calls=%async_computation.2 | async-start | bytes 2097152 | tf_op jit(solution)/shard_map/all_to_all | solution.py:1654
  486.2 3.0 convolution_convert_fusion.6
  489.2 1.0 multiply_reduce_fusion.1
  490.2 1.2 multiply_convert_fusion.1
  494.1 1.8 multiply_reduce_fusion.2
  496.5 2.3 fusion.13
  502.3 1.8 fusion.68
  504.7 3.7 fusion.61
  508.6 3.4 convolution_convert_fusion.4
  512.1 3.2 convolution_convert_fusion.1
  516.1 4.3 copy.182
  520.4 2.6 convolution_convert_fusion.2
  523.0 3.5 convolution_convert_fusion
  526.5 150.7 %shard_map.311 = (bf16[2,2,16,1024]{3,2,1,0:T(8,128)(2,1)}, bf16[64,576]{1,0:T(8,128)(2,1)}, bf16[2,2,64,768]{3,2,1,0:T(8,128)(2,1)}, f32[2,2,16,128]{3,2,1,0:T(...) custom-call(bf16[4,2,2,2,16,1024]{5,4,3,2,1,0:T(8,128)(2,1)} %bitcas, ...), custom_call_target="tpu_custom_call" | custom-call | tf_op jit(solution)/shard_map/pallas_call | solution.py:879
  679.5 1.7 fusion.17
  681.8 1.0 copy-done.1
  682.8 0.9 copy-done.2
  685.5 3.3 shard_map.312
  688.9 3.3 fusion.20
  693.0 2.9 copy.221
  695.9 1.8 copy-done.23
  697.7 2.8 copy.222
  701.3 2.5 copy.223
  (271 shorter events, 32.1 us)
Async XLA Ops:
  7.2 103.5 %copy-start.26 = (bf16[128,2048]{1,0:T(8,128)(2,1)S(1)}, bf16[128,2048]{1,0:T(8,128)(2,1)}, u32[]{:S(2)}) copy-start(bf16[128,2048]{1,0:T(8,128)(2,1)} %param.20) | copy-start | bytes 1572868
  7.2 188.9 %all-gather.2.cloned.1.call-start = ((), (), s32[]{:S(2)}) async-start(), calls=%async_computation.3 | async-start | bytes 8650752 | tf_op jit(solution)/shard_map/all_gather | solution.py:96
  12.0 99.5 %copy-start.46 = (bf16[64,2816]{1,0:T(8,128)(2,1)S(1)}, bf16[64,2816]{1,0:T(8,128)(2,1)}, u32[]{:S(2)}) copy-start(bf16[64,2816]{1,0:T(8,128)(2,1)} %param.29) | copy-start | bytes 1081348
  13.7 99.2 %copy-start.47 = (bf16[64,2816]{1,0:T(8,128)(2,1)S(1)}, bf16[64,2816]{1,0:T(8,128)(2,1)}, u32[]{:S(2)}) copy-start(bf16[64,2816]{1,0:T(8,128)(2,1)} %param.30) | copy-start | bytes 1081348
  114.4 4.8 copy-start.53
  114.4 6.5 copy-start.18
  115.8 56.6 %all-to-all-start = ((bf16[32,2,64,88]{3,2,1,0:T(8,128)(2,1)}), bf16[32,2,64,88]{3,2,1,0:T(8,128)(2,1)}, u32[]{:S(2)}, u32[]{:S(2)}) async-start(bf16[32,2,64,88]{3,2,1,0:T(8,128)(2,1)} %copy.173), calls=%async_computation | async-start | bytes 2097152 | tf_op jit(solution)/shard_map/all_to_all | solution.py:1483
  119.1 569.7 %reduce-scatter.2.cloned.1.call-start = ((), (), s32[]{:S(2)}) async-start(), calls=%async_computation.4 | async-start | bytes 17301504 | tf_op jit(solution)/shard_map/reduce_scatter | solution.py:100
  119.4 5.7 copy-start.60
  119.7 2.3 copy-start.51
  121.3 2.2 copy-start.79
  121.4 3.6 copy-start.69
  121.9 3.1 copy-start.33
  125.0 12.3 %copy-start.15 = (f32[512,576]{0,1:T(8,128)}, f32[512,576]{0,1:T(8,128)S(1)}, u32[]{:S(2)}) copy-start(f32[512,576]{0,1:T(8,128)S(1)} %fusion.65) | copy-start | bytes 3538948
  130.4 12.3 %copy-start.27 = (bf16[512,4,128]{2,1,0:T(4,128)(2,1)}, bf16[512,4,128]{2,1,0:T(4,128)(2,1)S(1)}, u32[]{:S(2)}) copy-start(bf16[512,4,128]{2,1,0:T(4,128)(2,1)S(1)} %get-tuple-element.180) | copy-start | bytes 1572868
  131.9 4.7 copy-start.55
  136.9 5.7 copy-start.73
  137.0 5.6 copy-start.58
  138.2 5.6 copy-start.48
  138.2 5.6 copy-start.49
  145.1 2.0 copy-start.7
  145.7 2.6 copy-start.81
  149.6 16.2 %copy-start.21 = (bf16[128,2048]{1,0:T(8,128)(2,1)S(1)}, bf16[128,2048]{1,0:T(8,128)(2,1)}, u32[]{:S(2)}) copy-start(bf16[128,2048]{1,0:T(8,128)(2,1)} %refs_0_.1) | copy-start | bytes 1572868
  165.9 2.1 copy-start.84
  166.7 272.0 %copy-start.11 = (f32[128,2048]{1,0:T(8,128)}, f32[128,2048]{1,0:T(8,128)S(1)}, u32[]{:S(2)}) copy-start(f32[128,2048]{1,0:T(8,128)S(1)} %get-tuple-element.171) | copy-start | bytes 3145732
  166.7 3.7 copy-start.38
  167.9 3.6 copy-start.71
  429.9 2.2 copy-start.72
  429.9 2.2 copy-start.67
  434.0 6.0 copy-start.13
  440.1 3.2 copy-start
  473.6 12.5 %copy-start.6 = (bf16[2,2,128,2048]{3,2,1,0:T(8,128)(2,1)S(1)}, bf16[2,2,128,2048]{3,2,1,0:T(8,128)(2,1)}, u32[]{:S(2)}) copy-start(bf16[2,2,128,2048]{3,2,1,0:T(8,128)(2,1)} %copy-done.5) | copy-start | bytes 6291460
  478.2 203.6 %all-to-all-start.1 = ((bf16[32,2,64,88]{3,2,1,0:T(8,128)(2,1)}), bf16[32,2,64,88]{3,2,1,0:T(8,128)(2,1)}, u32[]{:S(2)}, u32[]{:S(2)}) async-start(bf16[32,2,64,88]{3,2,1,0:T(8,128)(2,1)} %maximum_bitcast_fusion.1), calls=%async_computation.2 | async-start | bytes 2097152 | tf_op jit(solution)/shard_map/all_to_all | solution.py:1654
  486.2 3.1 copy-start.8
  493.4 2.4 copy-start.31
  495.8 3.1 copy-start.28
  496.5 2.3 copy-start.50
  496.5 2.4 copy-start.10
  499.4 1.9 copy-start.37
  499.5 2.0 copy-start.39
  499.7 2.6 copy-start.32
  501.6 2.6 copy-start.44
  502.3 1.9 copy-start.19
  502.3 1.9 copy-start.70
  502.3 2.4 copy-start.80
  504.7 3.8 copy-start.43
  504.7 3.8 copy-start.56
  504.7 3.8 copy-start.57
  508.4 3.7 copy-start.52
  508.6 3.5 copy-start.20
  508.6 3.5 copy-start.45
  515.3 5.1 copy-start.42
  520.4 2.6 copy-start.34
  520.4 2.6 copy-start.40
  526.5 152.9 %copy-start.75 = (f32[128]{0:T(128)S(1)}, f32[128]{0:T(128)}, u32[]{:S(2)}) copy-start(f32[128]{0:T(128)} %add_rsqrt_fusion.2) | copy-start | bytes 1540
  677.3 11.5 %copy-start.12 = (f32[128,2048]{1,0:T(8,128)S(1)}, f32[128,2048]{1,0:T(8,128)}, u32[]{:S(2)}) copy-start(f32[128,2048]{1,0:T(8,128)} %copy-done.11) | copy-start | bytes 3145732
  677.3 11.5 %copy-start.22 = (bf16[128,2048]{1,0:T(8,128)(2,1)S(1)}, bf16[128,2048]{1,0:T(8,128)(2,1)}, u32[]{:S(2)}) copy-start(bf16[128,2048]{1,0:T(8,128)(2,1)} %refs_0_.1) | copy-start | bytes 1572868
  677.3 11.5 %copy-start.68 = (f32[128]{0:T(128)S(1)}, f32[128]{0:T(128)}, u32[]{:S(2)}) copy-start(f32[128]{0:T(128)} %copy-done.66) | copy-start | bytes 1540
  677.3 11.5 %copy-start.77 = (f32[128]{0:T(128)S(1)}, f32[128]{0:T(128)}, u32[]{:S(2)}) copy-start(f32[128]{0:T(128)} %copy-done.76) | copy-start | bytes 1540
  685.5 3.3 copy-start.14
  688.9 4.1 copy-start.24
  693.0 4.7 copy-start.23
  693.0 7.5 %slice-start = ((s8[5767168]{0:T(1024)(128)(4,1)}), s8[4194304]{0:T(1024)(128)(4,1)S(1)}, s32[]{:S(2)}) async-start(s8[5767168]{0:T(1024)(128)(4,1)} %bitcast.152), calls=%async_computation.5 | async-start | bytes 8388608
  697.7 3.6 slice-start.1
  (27 other events, 34.4 us)
Sparse Core Ops, SparseCore 0:
  111.6 84.3 all-gather.1
  430.1 234.0 reduce-scatter.1
